TPU v7x, 32 devices: a whole 2x2x4 slice. The times are simulated.
32 devices in a mesh: dp: 16 (over z, y, x), outer: 2 (over core).
Axes of the slice: x: 2, y: 2, z: 4, core: 2. Of those that a mesh axis runs over, the one named last changes fastest.
Arguments:
- tokens: bfloat16 [4, 32, 512, 512], P(None, ('dp', 'outer')), may hold values from -6 to 6
- memory: float32 [4, 32, 64, 512], P(None, ('dp', 'outer')), may hold values from -6 to 6
- doc_ids: int32 [4, 32, 512], P(None, ('dp', 'outer')), may hold values from 0 to 3, never falling along the last dimension, each value on 1 to 256 neighbouring positions
- resets: int32 [4, 32], P(None, ('dp', 'outer')), may hold values 0 or 1
- out_grad: bfloat16 [4, 32, 512, 512], P(None, ('dp', 'outer')), may hold values from -6 to 6
- memory_grad: float32 [4, 32, 64, 512], P(None, ('dp', 'outer')), may hold values from -6 to 6
- attn_qkv: bfloat16 [3, 512, 512], P(None, 'dp'), may hold values from -0.25 to 0.25
- attn_out: bfloat16 [512, 512], P('dp'), may hold values from -0.75 to 0.75
- ffn_in: bfloat16 [512, 2048], P('dp'), may hold values from -0.25 to 0.25
- ffn_bias: bfloat16 [2048], P('dp'), may hold values from -3 to 3
- ffn_out: bfloat16 [2048, 512], P('dp'), may hold values from -0.125 to 0.125
- writer_qkv: bfloat16 [3, 512, 512], P(None, 'dp'), may hold values from -0.25 to 0.25
- writer_out: bfloat16 [512, 512], P('dp'), may hold values from -0.75 to 0.75
- gate_weight: bfloat16 [1024, 512], P('dp'), may hold values from -0.1875 to 0.1875
- gate_bias: bfloat16 [512], P('dp'), may hold values from -4 to 4
- gains: bfloat16 [3, 512], P(None, 'dp'), may hold values from 0.099609375 to 1.8984375
Outputs:
- out: bfloat16 [4, 32, 512, 512], P(None, ('dp', 'outer'))
- new_memory: float32 [4, 32, 64, 512], P(None, ('dp', 'outer'))
- grad_tokens: float32 [4, 32, 512, 512], P(None, ('dp', 'outer'))
- grad_memory: float32 [4, 32, 64, 512], P(None, ('dp', 'outer'))
- grad_attn_qkv: float32 [3, 512, 512], P(None, 'dp')
- grad_attn_out: float32 [512, 512], P('dp')
- grad_ffn_in: float32 [512, 2048], P('dp')
- grad_ffn_bias: float32 [2048], P('dp')
- grad_ffn_out: float32 [2048, 512], P('dp')
- grad_writer_qkv: float32 [3, 512, 512], P(None, 'dp')
- grad_writer_out: float32 [512, 512], P('dp')
- grad_gate_weight: float32 [1024, 512], P('dp')
- grad_gate_bias: float32 [512], P('dp')
- grad_gains: float32 [3, 512], P(None, 'dp')
Inputs may be any that keep to these rules, and one draw needn't show every extreme that they name: `doc_ids`: within each segment the document numbers start at 0, never fall and run up to 3, every document holds 1 to 256 tokens, and some document holds exactly 256.
All inputs are finite; a program needn't handle non-finite values. No bound on the sum of `resets` on one device may be relied on, other than what follows from the above.
Results may differ from a plain program's by a relative error of at most 0.017.
Values may be sent and summed in bfloat16 or wider, within the bound.
A program may use at most 256 MiB of HBM per device.

v0:
```python
from functools import partial

import jax
import jax.numpy as jnp
from jax import lax
from jax.sharding import PartitionSpec as P

HEADS = 8


def matmul(left_side, right_side):
    return jnp.dot(left_side, right_side, preferred_element_type=jnp.float32)


def matmul_back(left_side, right_side):
    return lax.dot_general(
        left_side, right_side, (((1,), (1,)), ((), ())), preferred_element_type=jnp.float32
    )


def outer_sum(left_side, right_side):
    return lax.dot_general(
        left_side, right_side, (((0,), (0,)), ((), ())), preferred_element_type=jnp.float32
    )


def layer_norm(rows_in, gain):
    centred = rows_in - jnp.mean(rows_in, axis=-1, keepdims=True)
    spread = jnp.mean(centred * centred, axis=-1, keepdims=True)
    return centred * lax.rsqrt(spread + 1e-05) * gain


def exact_gelu(inputs):
    return jax.nn.gelu(inputs, approximate=False)


def mix_gate(gate_logit, kept_memory, write_value):
    gate_value = jax.nn.sigmoid(gate_logit)
    return gate_value * kept_memory + (1.0 - gate_value) * write_value


def attention_forward(query_rows, key_rows, value_rows, allowed):
    row_count = query_rows.shape[0]
    head_size = query_rows.shape[1] // HEADS
    query_heads = query_rows.reshape(row_count, HEADS, head_size)
    key_heads = key_rows.reshape(key_rows.shape[0], HEADS, head_size)
    value_heads = value_rows.reshape(value_rows.shape[0], HEADS, head_size)
    scores = jnp.einsum(
        "qhd,khd->hqk", query_heads, key_heads, preferred_element_type=jnp.float32
    ) * head_size ** (-0.5)
    scores = jnp.where(allowed[None], scores, -1000000000.0)
    largest = jnp.max(scores, axis=-1, keepdims=True)
    expanded = jnp.exp(scores - largest)
    attn_weights = expanded / jnp.sum(expanded, axis=-1, keepdims=True)
    mixed_rows = jnp.einsum(
        "hqk,khd->qhd",
        attn_weights.astype(jnp.bfloat16),
        value_heads,
        preferred_element_type=jnp.float32,
    )
    return (mixed_rows.reshape(row_count, -1).astype(jnp.bfloat16), attn_weights)


def attention_backward(grad_rows, query_rows, key_rows, value_rows, attn_weights):
    row_count = query_rows.shape[0]
    key_count = key_rows.shape[0]
    head_size = query_rows.shape[1] // HEADS
    scale = head_size ** (-0.5)
    query_heads = query_rows.reshape(row_count, HEADS, head_size)
    key_heads = key_rows.reshape(key_count, HEADS, head_size)
    value_heads = value_rows.reshape(key_count, HEADS, head_size)
    grad_heads = grad_rows.reshape(row_count, HEADS, head_size)
    grad_weights = jnp.einsum(
        "qhd,khd->hqk", grad_heads, value_heads, preferred_element_type=jnp.float32
    )
    grad_scores = attn_weights * (
        grad_weights - jnp.sum(grad_weights * attn_weights, axis=-1, keepdims=True)
    )
    scores_low = grad_scores.astype(jnp.bfloat16)
    grad_query = (
        jnp.einsum("hqk,khd->qhd", scores_low, key_heads, preferred_element_type=jnp.float32)
        * scale
    )
    grad_keys = (
        jnp.einsum("hqk,qhd->khd", scores_low, query_heads, preferred_element_type=jnp.float32)
        * scale
    )
    grad_values = jnp.einsum(
        "hqk,qhd->khd",
        attn_weights.astype(jnp.bfloat16),
        grad_heads,
        preferred_element_type=jnp.float32,
    )
    return (
        grad_query.reshape(row_count, -1).astype(jnp.bfloat16),
        grad_keys.reshape(key_count, -1).astype(jnp.bfloat16),
        grad_values.reshape(key_count, -1).astype(jnp.bfloat16),
    )


def replay(params, token_rows, memory_rows, documents, reset_flag):
    (
        attn_qkv,
        attn_out,
        ffn_in,
        ffn_bias,
        ffn_out,
        writer_qkv,
        writer_out,
        gate_weight,
        gate_bias,
        gains,
    ) = params
    slot_count = memory_rows.shape[0]
    token_count = token_rows.shape[0]
    gain_float = gains.astype(jnp.float32)
    token_float = token_rows.astype(jnp.float32)
    kept_memory = memory_rows * (1 - reset_flag).astype(jnp.float32)
    stacked_one = jnp.concatenate([kept_memory, token_float], 0)
    normed_one = layer_norm(stacked_one, gain_float[0]).astype(jnp.bfloat16)
    query_rows = matmul(normed_one[slot_count:], attn_qkv[0]).astype(jnp.bfloat16)
    key_rows = matmul(normed_one, attn_qkv[1]).astype(jnp.bfloat16)
    value_rows = matmul(normed_one, attn_qkv[2]).astype(jnp.bfloat16)
    position = jnp.arange(token_count)
    same_doc = documents[:, None] == documents[None, :]
    causal = same_doc & (position[None, :] <= position[:, None])
    sees_memory = (documents == documents[0]) & (reset_flag == 0)
    allowed = jnp.concatenate(
        [jnp.broadcast_to(sees_memory[:, None], (token_count, slot_count)), causal], 1
    )
    mixed_rows, attn_weights = attention_forward(query_rows, key_rows, value_rows, allowed)
    hidden_one = token_float + matmul(mixed_rows, attn_out)
    normed_two = layer_norm(hidden_one, gain_float[1]).astype(jnp.bfloat16)
    ffn_before = matmul(normed_two, ffn_in) + ffn_bias.astype(jnp.float32)
    active = exact_gelu(ffn_before).astype(jnp.bfloat16)
    result = hidden_one + matmul(active, ffn_out)
    stacked_two = jnp.concatenate([kept_memory, result], 0)
    normed_three = layer_norm(stacked_two, gain_float[2]).astype(jnp.bfloat16)
    slot_query = matmul(normed_three[:slot_count], writer_qkv[0]).astype(jnp.bfloat16)
    token_keys = matmul(normed_three[slot_count:], writer_qkv[1]).astype(jnp.bfloat16)
    token_values = matmul(normed_three[slot_count:], writer_qkv[2]).astype(jnp.bfloat16)
    reading = jnp.broadcast_to(
        (documents == documents[token_count - 1])[None, :], (slot_count, token_count)
    )
    written, writer_weights = attention_forward(slot_query, token_keys, token_values, reading)
    write_value = matmul(written, writer_out)
    joined = jnp.concatenate([kept_memory, write_value], 1).astype(jnp.bfloat16)
    gate_logit = matmul(joined, gate_weight) + gate_bias.astype(jnp.float32)
    new_memory = mix_gate(gate_logit, kept_memory, write_value)
    return dict(
        stacked_one=stacked_one,
        normed_one=normed_one,
        query_rows=query_rows,
        key_rows=key_rows,
        value_rows=value_rows,
        attn_weights=attn_weights,
        mixed_rows=mixed_rows,
        hidden_one=hidden_one,
        normed_two=normed_two,
        ffn_before=ffn_before,
        active=active,
        result=result,
        stacked_two=stacked_two,
        normed_three=normed_three,
        slot_query=slot_query,
        token_keys=token_keys,
        token_values=token_values,
        writer_weights=writer_weights,
        written=written,
        write_value=write_value,
        joined=joined,
        gate_logit=gate_logit,
        kept_memory=kept_memory,
        new_memory=new_memory,
    )


def forward_segment(params, pieces):
    token_rows, memory_rows, documents, reset_flag = pieces
    saved = replay(params, token_rows, memory_rows, documents, reset_flag)
    return (saved["result"].astype(jnp.bfloat16), saved["new_memory"])


def backward(
    params, token_rows, memory_rows, documents, reset_flag, out_grad_rows, memory_grad_rows
):
    (
        attn_qkv,
        attn_out,
        ffn_in,
        ffn_bias,
        ffn_out,
        writer_qkv,
        writer_out,
        gate_weight,
        gate_bias,
        gains,
    ) = params
    saved = replay(params, token_rows, memory_rows, documents, reset_flag)
    slot_count = memory_rows.shape[0]
    model_width = memory_rows.shape[1]
    gain_float = gains.astype(jnp.float32)
    keep_scale = (1 - reset_flag).astype(jnp.float32)
    discard, gate_pull = jax.vjp(
        mix_gate, saved["gate_logit"], saved["kept_memory"], saved["write_value"]
    )
    grad_logit, grad_kept, grad_write = gate_pull(memory_grad_rows)
    logit_low = grad_logit.astype(jnp.bfloat16)
    grad_gate_bias = jnp.sum(logit_low.astype(jnp.float32), axis=0)
    grad_gate_weight = outer_sum(saved["joined"], logit_low)
    grad_joined = matmul_back(logit_low, gate_weight)
    grad_kept = grad_kept + grad_joined[:, :model_width]
    write_low = (grad_write + grad_joined[:, model_width:]).astype(jnp.bfloat16)
    grad_writer_out = outer_sum(saved["written"], write_low)
    written_low = matmul_back(write_low, writer_out).astype(jnp.bfloat16)
    grad_slot, grad_tkeys, grad_tvalues = attention_backward(
        written_low,
        saved["slot_query"],
        saved["token_keys"],
        saved["token_values"],
        saved["writer_weights"],
    )
    normed_three = saved["normed_three"]
    grad_writer_qkv = jnp.stack(
        [
            outer_sum(normed_three[:slot_count], grad_slot),
            outer_sum(normed_three[slot_count:], grad_tkeys),
            outer_sum(normed_three[slot_count:], grad_tvalues),
        ]
    )
    grad_read = jnp.concatenate(
        [
            matmul_back(grad_slot, writer_qkv[0]),
            matmul_back(grad_tkeys, writer_qkv[1]) + matmul_back(grad_tvalues, writer_qkv[2]),
        ],
        0,
    )
    discard, norm_pull = jax.vjp(layer_norm, saved["stacked_two"], gain_float[2])
    grad_stacked, grad_gain_three = norm_pull(grad_read)
    grad_kept = grad_kept + grad_stacked[:slot_count]
    grad_result = out_grad_rows.astype(jnp.float32) + grad_stacked[slot_count:]
    result_low = grad_result.astype(jnp.bfloat16)
    grad_ffn_out = outer_sum(saved["active"], result_low)
    grad_active = matmul_back(result_low, ffn_out)
    discard, gelu_pull = jax.vjp(exact_gelu, saved["ffn_before"])
    (grad_before,) = gelu_pull(grad_active)
    before_low = grad_before.astype(jnp.bfloat16)
    grad_ffn_bias = jnp.sum(before_low.astype(jnp.float32), axis=0)
    grad_ffn_in = outer_sum(saved["normed_two"], before_low)
    discard, norm_pull = jax.vjp(layer_norm, saved["hidden_one"], gain_float[1])
    grad_hidden_part, grad_gain_two = norm_pull(matmul_back(before_low, ffn_in))
    grad_hidden = grad_result + grad_hidden_part
    hidden_low = grad_hidden.astype(jnp.bfloat16)
    grad_attn_out = outer_sum(saved["mixed_rows"], hidden_low)
    mixed_low = matmul_back(hidden_low, attn_out).astype(jnp.bfloat16)
    grad_query, grad_keys, grad_values = attention_backward(
        mixed_low,
        saved["query_rows"],
        saved["key_rows"],
        saved["value_rows"],
        saved["attn_weights"],
    )
    normed_one = saved["normed_one"]
    grad_attn_qkv = jnp.stack(
        [
            outer_sum(normed_one[slot_count:], grad_query),
            outer_sum(normed_one, grad_keys),
            outer_sum(normed_one, grad_values),
        ]
    )
    grad_normed = matmul_back(grad_keys, attn_qkv[1]) + matmul_back(grad_values, attn_qkv[2])
    grad_normed = grad_normed + jnp.concatenate(
        [jnp.zeros((slot_count, model_width), jnp.float32), matmul_back(grad_query, attn_qkv[0])], 0
    )
    discard, norm_pull = jax.vjp(layer_norm, saved["stacked_one"], gain_float[0])
    grad_stacked, grad_gain_one = norm_pull(grad_normed)
    grad_tokens = grad_hidden + grad_stacked[slot_count:]
    grad_memory = (grad_kept + grad_stacked[:slot_count]) * keep_scale
    grad_gains = jnp.stack([grad_gain_one, grad_gain_two, grad_gain_three])
    grads = (
        grad_attn_qkv,
        grad_attn_out,
        grad_ffn_in,
        grad_ffn_bias,
        grad_ffn_out,
        grad_writer_qkv,
        grad_writer_out,
        grad_gate_weight,
        grad_gate_bias,
        grad_gains,
    )
    return (grads, grad_tokens, grad_memory)


def backward_step(params, carried, pieces):
    grads, grad_tokens, grad_memory = backward(params, *pieces)
    summed = tuple((running + addend for running, addend in zip(carried, grads)))
    return (summed, (grad_tokens, grad_memory))


def body(
    tokens,
    memory,
    doc_ids,
    resets,
    out_grad,
    memory_grad,
    attn_qkv,
    attn_out,
    ffn_in,
    ffn_bias,
    ffn_out,
    writer_qkv,
    writer_out,
    gate_weight,
    gate_bias,
    gains,
):
    micro_count = tokens.shape[0]
    shard_tuple = (
        attn_qkv,
        attn_out,
        ffn_in,
        ffn_bias,
        ffn_out,
        writer_qkv,
        writer_out,
        gate_weight,
        gate_bias,
        gains,
    )
    owned = tuple((jnp.zeros(piece.shape, jnp.float32) for piece in shard_tuple))
    outputs = []
    memories = []
    token_grads = []
    memory_grads = []
    for micro in range(micro_count):
        forward_params = (
            lax.all_gather(attn_qkv, "dp", axis=1, tiled=True),
            lax.all_gather(attn_out, "dp", axis=0, tiled=True),
            lax.all_gather(ffn_in, "dp", axis=0, tiled=True),
            lax.all_gather(ffn_bias, "dp", axis=0, tiled=True),
            lax.all_gather(ffn_out, "dp", axis=0, tiled=True),
            lax.all_gather(writer_qkv, "dp", axis=1, tiled=True),
            lax.all_gather(writer_out, "dp", axis=0, tiled=True),
            lax.all_gather(gate_weight, "dp", axis=0, tiled=True),
            lax.all_gather(gate_bias, "dp", axis=0, tiled=True),
            lax.all_gather(gains, "dp", axis=1, tiled=True),
        )
        result_rows, memory_rows = lax.map(
            partial(forward_segment, forward_params),
            (tokens[micro], memory[micro], doc_ids[micro], resets[micro]),
        )
        outputs.append(result_rows)
        memories.append(memory_rows)
        replay_params = (
            lax.all_gather(attn_qkv, "dp", axis=1, tiled=True),
            lax.all_gather(attn_out, "dp", axis=0, tiled=True),
            lax.all_gather(ffn_in, "dp", axis=0, tiled=True),
            lax.all_gather(ffn_bias, "dp", axis=0, tiled=True),
            lax.all_gather(ffn_out, "dp", axis=0, tiled=True),
            lax.all_gather(writer_qkv, "dp", axis=1, tiled=True),
            lax.all_gather(writer_out, "dp", axis=0, tiled=True),
            lax.all_gather(gate_weight, "dp", axis=0, tiled=True),
            lax.all_gather(gate_bias, "dp", axis=0, tiled=True),
            lax.all_gather(gains, "dp", axis=1, tiled=True),
        )
        zero_full = tuple((jnp.zeros(piece.shape, jnp.float32) for piece in replay_params))
        micro_grads, (grad_token_rows, grad_memory_rows) = lax.scan(
            partial(backward_step, replay_params),
            zero_full,
            (
                tokens[micro],
                memory[micro],
                doc_ids[micro],
                resets[micro],
                out_grad[micro],
                memory_grad[micro],
            ),
        )
        token_grads.append(grad_token_rows)
        memory_grads.append(grad_memory_rows)
        shares = (
            lax.psum_scatter(micro_grads[0], "dp", scatter_dimension=1, tiled=True),
            lax.psum_scatter(micro_grads[1], "dp", scatter_dimension=0, tiled=True),
            lax.psum_scatter(micro_grads[2], "dp", scatter_dimension=0, tiled=True),
            lax.psum_scatter(micro_grads[3], "dp", scatter_dimension=0, tiled=True),
            lax.psum_scatter(micro_grads[4], "dp", scatter_dimension=0, tiled=True),
            lax.psum_scatter(micro_grads[5], "dp", scatter_dimension=1, tiled=True),
            lax.psum_scatter(micro_grads[6], "dp", scatter_dimension=0, tiled=True),
            lax.psum_scatter(micro_grads[7], "dp", scatter_dimension=0, tiled=True),
            lax.psum_scatter(micro_grads[8], "dp", scatter_dimension=0, tiled=True),
            lax.psum_scatter(micro_grads[9], "dp", scatter_dimension=1, tiled=True),
        )
        owned = tuple((running + addend for running, addend in zip(owned, shares)))
    owned = (
        lax.psum(owned[0].astype(jnp.bfloat16), "outer").astype(jnp.float32),
        lax.psum(owned[1].astype(jnp.bfloat16), "outer").astype(jnp.float32),
        lax.psum(owned[2].astype(jnp.bfloat16), "outer").astype(jnp.float32),
        lax.psum(owned[3].astype(jnp.bfloat16), "outer").astype(jnp.float32),
        lax.psum(owned[4].astype(jnp.bfloat16), "outer").astype(jnp.float32),
        lax.psum(owned[5].astype(jnp.bfloat16), "outer").astype(jnp.float32),
        lax.psum(owned[6].astype(jnp.bfloat16), "outer").astype(jnp.float32),
        lax.psum(owned[7].astype(jnp.bfloat16), "outer").astype(jnp.float32),
        lax.psum(owned[8].astype(jnp.bfloat16), "outer").astype(jnp.float32),
        lax.psum(owned[9].astype(jnp.bfloat16), "outer").astype(jnp.float32),
    )
    return (
        jnp.stack(outputs),
        jnp.stack(memories),
        jnp.stack(token_grads),
        jnp.stack(memory_grads),
        owned[0],
        owned[1],
        owned[2],
        owned[3],
        owned[4],
        owned[5],
        owned[6],
        owned[7],
        owned[8],
        owned[9],
    )


def solution(mesh):
    placed = (
        P(None, ("dp", "outer"), None, None),
        P(None, ("dp", "outer"), None, None),
        P(None, ("dp", "outer"), None),
        P(None, ("dp", "outer")),
        P(None, ("dp", "outer"), None, None),
        P(None, ("dp", "outer"), None, None),
        P(None, "dp", None),
        P("dp", None),
        P("dp", None),
        P("dp"),
        P("dp", None),
        P(None, "dp", None),
        P("dp", None),
        P("dp", None),
        P("dp"),
        P(None, "dp"),
    )
    return jax.shard_map(
        body,
        mesh=mesh,
        in_specs=placed,
        out_specs=(
            P(None, ("dp", "outer"), None, None),
            P(None, ("dp", "outer"), None, None),
            P(None, ("dp", "outer"), None, None),
            P(None, ("dp", "outer"), None, None),
            P(None, "dp", None),
            P("dp", None),
            P("dp", None),
            P("dp"),
            P("dp", None),
            P(None, "dp", None),
            P("dp", None),
            P("dp", None),
            P("dp"),
            P(None, "dp"),
        ),
        check_vma=False,
    )
```

profile of v0, /device:TPU:0, one launch (start us, length us, event | category | flops | bytes accessed | tf_op | source)
XLA Modules:
  0.0 1446.1 jit_solution(13910984959907853085)
XLA Ops:
  25.3 42.5 %all-gather = bf16[16,32,3]{1,2,0:T(4,128)(2,1)S(1)} all-gather(bf16[1,32,3]{1,2,0:T(4,128)(2,1)S(1)} %bitcast.893), channel_id=1, replica_groups=mesh['dp'=16,'outer'=2] {'dp'}, dimensions={0}, use_global_device_ids=true | all-gather | bytes 3264 | tf_op jit(solution)/shard_map/all_gather | solution.py:348
  69.3 39.3 %all_gather.22 = bf16[512,512]{1,0:T(8,128)(2,1)S(1)} all-gather(bf16[32,512]{1,0:T(8,128)(2,1)S(1)} %copy-done.348), channel_id=1, replica_groups=mesh['dp'=16,'outer'=2] {'dp'}, dimensions={0}, use_global_device_ids=true | all-gather | bytes 557056 | tf_op jit(solution)/shard_map/all_gather | solution.py:340
  110.8 37.6 %all-gather.1 = bf16[16,1,128]{2,1,0:T(2,128)(2,1)S(1)} all-gather(bf16[1,1,128]{2,1,0:T(2,128)(2,1)S(1)} %bitcast.894), channel_id=1, replica_groups=mesh['dp'=16,'outer'=2] {'dp'}, dimensions={0}, use_global_device_ids=true | all-gather | bytes 4352 | tf_op jit(solution)/shard_map/all_gather | solution.py:342
  149.0 43.3 %all_gather.27 = bf16[512,512]{1,0:T(8,128)(2,1)} all-gather(bf16[32,512]{1,0:T(8,128)(2,1)S(1)} %copy-done.349), channel_id=1, replica_groups=mesh['dp'=16,'outer'=2] {'dp'}, dimensions={0}, use_global_device_ids=true | all-gather | bytes 557056 | tf_op jit(solution)/shard_map/all_gather | solution.py:345
  193.8 37.6 %all-reduce.4 = bf16[512]{0:T(512)(128)(2,1)S(1)} all-reduce(bf16[512]{0:T(512)(128)(2,1)S(1)} %dynamic-update-slice), channel_id=1, replica_groups=mesh['dp'=16,'outer'=2] {'dp'}, use_global_device_ids=true, to_apply=%add.4 | all-reduce | flops 512 | bytes 2048
  256.2 8.3 fusion.386
  264.5 4.7 fusion.108
  279.7 8.3 fusion.391
  288.1 4.7 fusion.111
  306.1 8.1 fusion.389
  314.2 4.7 fusion.114
  333.1 8.3 fusion.385
  341.4 4.7 fusion.117
  358.8 44.5 %multiply_convert_fusion.7 = (bf16[512,2048]{1,0:T(8,128)(2,1)}, f32[512,2048]{1,0:T(8,128)}, bf16[512,2048]{1,0:T(8,128)(2,1)}, f32[512,2048]{1,0:T(8,128)}, bf...) fusion(f32[2048]{0:T(1024)} %bitcast.21, ...), kind=kOutput, calls=%fused_computation.102 | convolution fusion | flops 1351614464 | bytes 45103104 | tf_op jit(solution)/shard_map/while/body/eval_jaxpr/dot_general | solution.py:12
  595.8 11.2 multiply_convert_fusion
  614.1 7.3 multiply_reduce_fusion.3
  621.4 11.2 multiply_convert_fusion.3
  632.6 5.0 fusion.84
  639.4 6.2 fusion.88
  653.2 11.1 multiply_convert_fusion.2
  670.3 6.2 fusion.97
  677.6 4.6 multiply_reduce_fusion.1
  684.6 11.2 multiply_convert_fusion.1
  788.3 73.1 %all-reduce.7 = (bf16[2048]{0:T(1024)(128)(2,1)S(1)}, bf16[512]{0:T(512)(128)(2,1)S(1)}) all-reduce(f32[2048]{0:T(1024)S(1)} %add_add_fusion.19, f32[512]{0:T(512)S(1)} %add_add_fusion.20), channel_id=35, replica_groups=mesh['dp'=16,'outer'=2] {'dp'}, use_global_device_ids=true, to_apply=%region_88.89.clone | all-reduce | flops 2560 | bytes 15360
  878.8 68.2 %reduce-scatter.13.cloned.1.call-done = f32[32,512]{1,0:T(8,128)} async-done(((f32[512,512]{1,0:T(8,128)}), f32[32,512]{1,0:T(8,128)}) %reduce-scatter.13.cloned.1.call-update) | async-done | bytes 65552 | tf_op jit(solution)/shard_map/reduce_scatter | solution.py:385
  950.7 75.5 %reduce-scatter.23.cloned.1.call-done = f32[64,512]{1,0:T(8,128)} async-done(((f32[1024,512]{1,0:T(8,128)}), f32[64,512]{1,0:T(8,128)}) %reduce-scatter.23.cloned.1.call-update) | async-done | bytes 131088 | tf_op jit(solution)/shard_map/reduce_scatter | solution.py:391
  1027.7 82.4 %reduce-scatter.19.cloned.1.call-done = f32[3,32,512]{2,1,0:T(8,128)} async-done(((f32[3,512,512]{2,1,0:T(8,128)}), f32[3,32,512]{2,1,0:T(8,128)}) %reduce-scatter.19.cloned.1.call-update) | async-done | bytes 196624 | tf_op jit(solution)/shard_map/reduce_scatter | solution.py:389
  1111.7 82.2 %reduce-scatter.11.cloned.1.call-done = f32[3,32,512]{2,1,0:T(8,128)} async-done(((f32[3,512,512]{2,1,0:T(8,128)}), f32[3,32,512]{2,1,0:T(8,128)}) %reduce-scatter.11.cloned.1.call-update) | async-done | bytes 196624 | tf_op jit(solution)/shard_map/reduce_scatter | solution.py:384
  1195.5 92.5 %reduce-scatter.17.cloned.1.call-done = f32[128,512]{1,0:T(8,128)} async-done(((f32[2048,512]{1,0:T(8,128)}), f32[128,512]{1,0:T(8,128)}) %reduce-scatter.17.cloned.1.call-update) | async-done | bytes 262160 | tf_op jit(solution)/shard_map/reduce_scatter | solution.py:388
  1289.6 96.1 %reduce-scatter.15.cloned.1.call-done = f32[32,2048]{1,0:T(8,128)} async-done(((f32[512,2048]{1,0:T(8,128)}), f32[32,2048]{1,0:T(8,128)}) %reduce-scatter.15.cloned.1.call-update) | async-done | bytes 262160 | tf_op jit(solution)/shard_map/reduce_scatter | solution.py:386
  1392.0 15.2 %all-reduce.13.cloned.1.call-done = (bf16[32,512]{1,0:T(8,128)(2,1)}, bf16[128]{0:T(256)(128)(2,1)}, bf16[32,512]{1,0:T(8,128)(2,1)}, bf16[32]{0:T(256)(128)(2,1)}, bf16[3,32]{1,0:T(4,128)(2,1)}) async-done(((bf16[32,512]{1,0:T(8,128)(2,1)}, bf16[128]{0:T(256)(128)(2,1)}, bf16[32,512]{1,0:T(8,128)(2,1)}, bf16[32]{0:T(256)(128)(2,1)}, bf16[3,32]{1,0:T(4,128)(2,1)}), (bf16[32,512]{1,0:T(8,128)(2,1)}, ...) | async-done | bytes 66064 | tf_op jit(solution)/shard_map/psum | solution.py:398
  1413.5 17.9 %all-reduce.15.cloned.1.call-done = (bf16[3,32,512]{2,1,0:T(8,128)(2,1)}, bf16[32,2048]{1,0:T(8,128)(2,1)}, bf16[128,512]{1,0:T(8,128)(2,1)}, bf16[3,32,512]{2,1,0:T(8,128)(2,1)}, bf16[64,512]{1,0:T(8,128)(2,1)}) async-done(((bf16[3,32,512]{2,1,0:T(8,128)(2,1)}, bf16[32,2048]{1,0:T(8,128)(2,1)}, bf16[128,512]{1,0:T(8,128)(2,1)}, bf16[3,32,512]{2,1,0:T(8,128)(2,1)}, bf16[64,512]{1,0:T(8,128)(2,1)}), ...) | async-done | bytes 524304 | tf_op jit(solution)/shard_map/psum | solution.py:397
  (1190 shorter events, 445.7 us)
Async XLA Ops:
  7.2 240.2 %all-gather.8.cloned.1.call-start = ((), (), s32[]{:S(2)}) async-start(), calls=%async_computation.8 | async-start | bytes 1671168 | tf_op jit(solution)/shard_map/all_gather | solution.py:339
  7.9 341.3 %all-gather.10.cloned.1.call-start = ((), (), s32[]{:S(2)}) async-start(), calls=%async_computation.9 | async-start | bytes 2228224 | tf_op jit(solution)/shard_map/all_gather | solution.py:341
  8.7 394.7 %all-gather.12.cloned.1.call-start = ((), (), s32[]{:S(2)}) async-start(), calls=%async_computation.10 | async-start | bytes 2228224 | tf_op jit(solution)/shard_map/all_gather | solution.py:343
  9.4 410.4 %all-gather.14.cloned.1.call-start = ((), (), s32[]{:S(2)}) async-start(), calls=%async_computation.11 | async-start | bytes 1671168 | tf_op jit(solution)/shard_map/all_gather | solution.py:344
  10.0 473.9 %all-gather.16.cloned.1.call-start = ((), (), s32[]{:S(2)}) async-start(), calls=%async_computation.12 | async-start | bytes 1114112 | tf_op jit(solution)/shard_map/all_gather | solution.py:346
  10.6 865.4 %reduce-scatter.25.cloned.1.call-start = ((), (), s32[]{:S(2)}) async-start(), calls=%async_computation.20 | async-start | bytes 278528
  21.3 223.7 %copy-start.2 = (f32[512,512]{1,0:T(8,128)}, f32[512,512]{1,0:T(8,128)S(1)}, u32[]{:S(2)}) copy-start(f32[512,512]{1,0:T(8,128)S(1)} %get-tuple-element.554) | copy-start | bytes 3145732
  21.3 223.7 %copy-start.4 = (f32[512,512]{1,0:T(8,128)}, f32[512,512]{1,0:T(8,128)S(1)}, u32[]{:S(2)}) copy-start(f32[512,512]{1,0:T(8,128)S(1)} %get-tuple-element.555) | copy-start | bytes 3145732
  22.3 222.8 %copy-start.49 = (f32[64,512]{1,0:T(8,128)}, f32[64,512]{1,0:T(8,128)S(1)}, u32[]{:S(2)}) copy-start(f32[64,512]{1,0:T(8,128)S(1)} %get-tuple-element.587) | copy-start | bytes 393220
  22.3 222.8 %copy-start.52 = (f32[64,512]{1,0:T(8,128)}, f32[64,512]{1,0:T(8,128)S(1)}, u32[]{:S(2)}) copy-start(f32[64,512]{1,0:T(8,128)S(1)} %get-tuple-element.589) | copy-start | bytes 393220
  22.3 222.8 %copy-start.56 = (f32[64,512]{1,0:T(8,128)}, f32[64,512]{1,0:T(8,128)S(1)}, u32[]{:S(2)}) copy-start(f32[64,512]{1,0:T(8,128)S(1)} %get-tuple-element.504) | copy-start | bytes 393220
  22.3 222.8 %copy-start.59 = (f32[64,512]{1,0:T(8,128)}, f32[64,512]{1,0:T(8,128)S(1)}, u32[]{:S(2)}) copy-start(f32[64,512]{1,0:T(8,128)S(1)} %get-tuple-element.568) | copy-start | bytes 393220
  22.5 222.6 %copy-start.287 = (f32[576]{0:T(1024)}, f32[576]{0:T(1024)S(1)}, u32[]{:S(2)}) copy-start(f32[576]{0:T(1024)S(1)} %broadcast_multiply_fusion.4) | copy-start | bytes 6916
  22.7 222.4 %copy-start.289 = (f32[576]{0:T(1024)}, f32[576]{0:T(1024)S(1)}, u32[]{:S(2)}) copy-start(f32[576]{0:T(1024)S(1)} %broadcast_multiply_fusion.5) | copy-start | bytes 6916
  23.2 221.9 %copy-start.308 = (f32[576]{0:T(1024)}, f32[576]{0:T(1024)S(1)}, u32[]{:S(2)}) copy-start(f32[576]{0:T(1024)S(1)} %fusion.288) | copy-start | bytes 6916
  23.2 221.9 %copy-start.310 = (f32[576]{0:T(1024)}, f32[576]{0:T(1024)S(1)}, u32[]{:S(2)}) copy-start(f32[576]{0:T(1024)S(1)} %fusion.289) | copy-start | bytes 6916
  23.9 221.2 %copy-start.298 = (f32[576]{0:T(1024)}, f32[576]{0:T(1024)S(1)}, u32[]{:S(2)}) copy-start(f32[576]{0:T(1024)S(1)} %broadcast_multiply_fusion.6) | copy-start | bytes 6916
  24.2 220.9 %copy-start.296 = (f32[576]{0:T(1024)}, f32[576]{0:T(1024)S(1)}, u32[]{:S(2)}) copy-start(f32[576]{0:T(1024)S(1)} %broadcast_multiply_fusion.7) | copy-start | bytes 6916
  108.7 237.4 %copy-start.21 = (bf16[512,512]{1,0:T(8,128)(2,1)}, bf16[512,512]{1,0:T(8,128)(2,1)S(1)}, u32[]{:S(2)}) copy-start(bf16[512,512]{1,0:T(8,128)(2,1)S(1)} %all_gather.22) | copy-start | bytes 1572868
  720.8 156.6 %reduce-scatter.21.cloned.1.call-start = ((), (), s32[]{:S(2)}) async-start(), calls=%async_computation.18 | async-start | bytes 1114112 | tf_op jit(solution)/shard_map/reduce_scatter | solution.py:390
  725.1 222.0 %reduce-scatter.13.cloned.1.call-start = ((), (), s32[]{:S(2)}) async-start(), calls=%async_computation.14 | async-start | bytes 1114112 | tf_op jit(solution)/shard_map/reduce_scatter | solution.py:385
  731.3 294.9 %reduce-scatter.23.cloned.1.call-start = ((), (), s32[]{:S(2)}) async-start(), calls=%async_computation.19 | async-start | bytes 2228224 | tf_op jit(solution)/shard_map/reduce_scatter | solution.py:391
  735.6 374.6 %reduce-scatter.19.cloned.1.call-start = ((), (), s32[]{:S(2)}) async-start(), calls=%async_computation.17 | async-start | bytes 3342336 | tf_op jit(solution)/shard_map/reduce_scatter | solution.py:389
  747.8 446.1 %reduce-scatter.11.cloned.1.call-start = ((), (), s32[]{:S(2)}) async-start(), calls=%async_computation.13 | async-start | bytes 3342336 | tf_op jit(solution)/shard_map/reduce_scatter | solution.py:384
  761.5 526.4 %reduce-scatter.17.cloned.1.call-start = ((), (), s32[]{:S(2)}) async-start(), calls=%async_computation.16 | async-start | bytes 4456448 | tf_op jit(solution)/shard_map/reduce_scatter | solution.py:388
  773.0 612.7 %reduce-scatter.15.cloned.1.call-start = ((), (), s32[]{:S(2)}) async-start(), calls=%async_computation.15 | async-start | bytes 4456448 | tf_op jit(solution)/shard_map/reduce_scatter | solution.py:386
  786.6 620.6 %all-reduce.13.cloned.1.call-start = ((), (), s32[]{:S(2)}) async-start(), calls=%async_computation.21 | async-start | bytes 135168 | tf_op jit(solution)/shard_map/psum | solution.py:398
  876.0 511.4 %copy-start.259 = (f32[1,1,64,512]{3,2,1,0:T(8,128)S(1)}, f32[1,1,64,512]{3,2,1,0:T(8,128)}, u32[]{:S(2)}) copy-start(f32[1,1,64,512]{3,2,1,0:T(8,128)} %get-tuple-element.591) | copy-start | bytes 393220
  876.0 511.4 %copy-start.260 = (f32[1,1,64,512]{3,2,1,0:T(8,128)S(1)}, f32[1,1,64,512]{3,2,1,0:T(8,128)}, u32[]{:S(2)}) copy-start(f32[1,1,64,512]{3,2,1,0:T(8,128)} %get-tuple-element.592) | copy-start | bytes 393220
  948.6 482.9 %all-reduce.15.cloned.1.call-start = ((), (), s32[]{:S(2)}) async-start(), calls=%async_computation.22 | async-start | bytes 1048576 | tf_op jit(solution)/shard_map/psum | solution.py:397
  948.6 440.7 %copy-start.70 = (f32[512,512]{1,0:T(8,128)S(1)}, f32[512,512]{1,0:T(8,128)}, u32[]{:S(2)}) copy-start(f32[512,512]{1,0:T(8,128)} %copy-done.68) | copy-start | bytes 3145732
  948.6 440.7 %copy-start.121 = (f32[576,512]{1,0:T(8,128)S(1)}, f32[576,512]{1,0:T(8,128)}, u32[]{:S(2)}) copy-start(f32[576,512]{1,0:T(8,128)} %copy-done.120) | copy-start | bytes 3538948
  (389 other events, 3643.2 us)
Sparse Core Ops, SparseCore 0:
  10.8 62.1 all-gather.7
  75.7 61.7 all-gather.9
  140.3 59.4 all-gather.11
  202.5 57.3 all-gather.13
  262.4 54.0 all-gather.15
  720.9 73.2 reduce-scatter.24
  796.6 74.0 reduce-scatter.20
  872.9 74.1 reduce-scatter.12
  949.4 76.6 reduce-scatter.22
  1028.4 81.6 reduce-scatter.18
  1112.5 81.3 reduce-scatter.10
  1196.2 91.7 reduce-scatter.16
  1290.9 94.7 reduce-scatter.14
  1389.5 17.6 all-reduce.12
  1411.1 20.2 all-reduce.14
where the time goes:
time: 1460 us; the launch traced here: 1450 us
  waiting for transfers between devices  533 us (37%)
  matrix products  388 us (27%)
  blocking collectives  273 us (19%)
  other arithmetic  144 us (10%)
  local copies, waits for them, and re-layouts  79.6 us (5%)
  between operations  26.5 us (2%)
    dot_general x44, matrix products, matmul(): return jnp.dot(left_side, right_side, preferred_element_type=jnp.float32)  127 us
    unnamed x2, blocking collectives  111 us
    reduce_scatter x1, waiting for transfers between devices, body(): lax.psum_scatter(micro_grads[2], 'dp', scatter_dimension=0, tiled=True)  96.1 us
    reduce_scatter x1, waiting for transfers between devices, body(): lax.psum_scatter(micro_grads[4], 'dp', scatter_dimension=0, tiled=True)  92.5 us
    reduce_scatter x1, waiting for transfers between devices, body(): lax.psum_scatter(micro_grads[5], 'dp', scatter_dimension=1, tiled=True)  82.4 us
    reduce_scatter x1, waiting for transfers between devices, body(): lax.psum_scatter(micro_grads[0], 'dp', scatter_dimension=1, tiled=True)  82.2 us
    reduce_scatter x1, waiting for transfers between devices, body(): lax.psum_scatter(micro_grads[7], 'dp', scatter_dimension=0, tiled=True)  75.5 us
    reduce_scatter x1, waiting for transfers between devices, body(): lax.psum_scatter(micro_grads[1], 'dp', scatter_dimension=0, tiled=True)  68.2 us
  transfers between devices with their start and end apart: 15, of which 8 were waited for; matrix products, arithmetic and copies ran while one was open for 24% of the time, Pallas kernels for 0%

commit v1 on v0

v1 whole, which is shorter than its diff:
```python
import functools

import jax
import jax.numpy as jnp
from jax import lax
from jax.experimental import pallas as pl
from jax.experimental.pallas import tpu as pltpu
from jax.sharding import PartitionSpec as P

HEADS = 8
BLOCK = 128
SPANS = ((0, 256), (0, 384), (128, 512), (256, 640))
STARTS = (0, 256, 640, 1024)
LIVE = 1408
F32 = jnp.float32
BF16 = jnp.bfloat16
VMEM_LIMIT = 60 * 1024 * 1024


def dot(a, b):
    return jnp.dot(a, b, preferred_element_type=F32)


def dot_nt(a, b):
    return lax.dot_general(a, b, (((1,), (1,)), ((), ())), preferred_element_type=F32)


def dot_tn(a, b):
    return lax.dot_general(a, b, (((0,), (0,)), ((), ())), preferred_element_type=F32)


def norm_parts(rows):
    centred = rows - jnp.mean(rows, axis=-1, keepdims=True)
    rstd = lax.rsqrt(jnp.mean(centred * centred, axis=-1, keepdims=True) + 1e-05)
    return centred * rstd, rstd


def norm_back(grad, hat, rstd, gain):
    scaled = grad * gain
    return rstd * (
        scaled
        - jnp.mean(scaled, axis=-1, keepdims=True)
        - hat * jnp.mean(scaled * hat, axis=-1, keepdims=True)
    )


def diagonal_pair(ref, top):
    ref[0:64, 0:128] = top[0:64]
    ref[64:128, 128:256] = top[64:128]


def forward_kernel(
    tok_ref, mem_ref, doc_ref, keep_ref, attn_ref, w1_ref, w2_ref, b1_ref, gain_ref,
    out_ref, res_ref, h1_ref, n1_ref, qt_ref, k_ref, v_ref, e_ref, linv_ref, ot_ref, act_ref, slope_ref,
    bias_ref, pair_ref, vt_ref,
):
    seg = tok_ref.shape[1]
    slots = mem_ref.shape[1]
    x = tok_ref[0].astype(F32)
    keep = keep_ref[0][:, 0:1]
    gain_one = gain_ref[0:1, :]
    hat, _ = norm_parts(x)
    n1t = (hat * gain_one).astype(BF16)
    hat, _ = norm_parts(mem_ref[0] * keep)
    n1_ref[0, 0:slots, :] = (hat * gain_one).astype(BF16)
    n1_ref[0, slots:128, :] = jnp.zeros((128 - slots, x.shape[1]), BF16)
    n1_ref[0, 128:, :] = n1t
    docs = doc_ref[0].astype(F32)
    key_docs = jnp.broadcast_to(docs, (128, seg)).T
    slot_docs = jnp.broadcast_to(keep - 1.0, (slots, 128))
    key_docs = jnp.concatenate([slot_docs, jnp.full((128 - slots, 128), -1.0, F32), key_docs], 0)
    for block, (first, last) in enumerate(SPANS):
        place = lax.broadcasted_iota(jnp.int32, (last - first, BLOCK), 0) + (first - 128 - block * BLOCK)
        place = place <= lax.broadcasted_iota(jnp.int32, (last - first, BLOCK), 1)
        same = key_docs[first:last] == docs[:, block * BLOCK:(block + 1) * BLOCK]
        bias_ref[STARTS[block]:STARTS[block] + last - first, :] = jnp.where(same & place, 0.0, -1e30)
    qt_ref[0] = (dot_nt(attn_ref[0].T, n1t) * 0.125).astype(BF16)
    n1 = n1_ref[0]
    k_ref[0] = dot(n1, attn_ref[1]).astype(BF16)
    v = dot(n1, attn_ref[2])
    v_ref[0] = v.astype(BF16)
    vt_ref[...] = v.astype(BF16).T
    pair_ref[...] = jnp.zeros_like(pair_ref)

    def one_pair(pair, carry):
        lanes = pl.ds(pl.multiple_of(pair * 128, 128), 128)
        for block, (first, last) in enumerate(SPANS):
            start = STARTS[block]
            held = pair_ref.at[block]
            columns = pl.ds(block * BLOCK, BLOCK)
            diagonal_pair(held, qt_ref[0, lanes, columns])
            scores = dot(k_ref[0, first:last, lanes], held[...])
            bias = bias_ref[start:start + last - first, :]
            scores = scores + jnp.concatenate([bias, bias], 1)
            largest = jnp.max(scores, axis=0, keepdims=True)
            e = jnp.exp(scores - largest)
            linv = 1.0 / jnp.sum(e, axis=0, keepdims=True)
            e = e.astype(BF16)
            e_ref[0, pair, start:start + last - first, :] = e
            linv_ref[0, pair, block, :, :] = linv
            mixed = dot(vt_ref[lanes, first:last], e) * linv
            ot_ref[0, lanes, columns] = jnp.concatenate(
                [mixed[0:64, 0:128], mixed[64:128, 128:256]], 0
            ).astype(BF16)
        return carry

    lax.fori_loop(0, 4, one_pair, 0)
    h1 = x + dot(ot_ref[0].T, attn_ref[3])
    h1_ref[0] = h1
    hat, _ = norm_parts(h1)
    n2 = (hat * gain_ref[1:2, :]).astype(BF16)
    result = h1
    for part in range(4):
        before = dot(n2, w1_ref[part]) + b1_ref[part]
        cdf = 0.5 + 0.5 * lax.erf(before * 0.7071067811865476)
        active = (before * cdf).astype(BF16)
        act_ref[0, part] = active
        slope = cdf + before * jnp.exp(before * before * -0.5) * 0.3989422804014327
        slope_ref[0, part] = slope.astype(BF16)
        result = result + dot(active, w2_ref[part])
    out_ref[0] = result.astype(BF16)
    res_ref[0] = result[seg // 2:]


def full_spec(shape):
    return pl.BlockSpec(shape, lambda i: (0,) * len(shape), pipeline_mode=pl.Buffered(1))


def step_spec(shape):
    return pl.BlockSpec((1,) + shape, lambda i: (i,) + (0,) * len(shape))


def call_forward(tokens, memory, docs, keep, attn, w1, w2, b1, gains):
    n, seg, d = tokens.shape
    slots = memory.shape[1]
    outs = [
        ((seg, d), BF16), ((seg // 2, d), F32), ((seg, d), F32), ((seg + 128, d), BF16), ((d, seg), BF16),
        ((seg + 128, d), BF16), ((seg + 128, d), BF16), ((4, LIVE, 256), BF16), ((4, 4, 1, 256), F32),
        ((d, seg), BF16), ((4, seg, 512), BF16), ((4, seg, 512), BF16),
    ]
    return pl.pallas_call(
        forward_kernel,
        grid=(n,),
        out_shape=[jax.ShapeDtypeStruct((n,) + shape, kind) for shape, kind in outs],
        in_specs=[
            step_spec((seg, d)), step_spec((slots, d)), step_spec((1, seg)), step_spec((1, 128)),
            full_spec(attn.shape), full_spec(w1.shape), full_spec(w2.shape), full_spec(b1.shape), full_spec(gains.shape),
        ],
        out_specs=[step_spec(shape) for shape, _ in outs],
        scratch_shapes=[
            pltpu.VMEM((LIVE, 128), F32), pltpu.VMEM((4, 128, 256), BF16), pltpu.VMEM((d, seg + 128), BF16),
        ],
        compiler_params=pltpu.CompilerParams(vmem_limit_bytes=VMEM_LIMIT),
        name="forward_rows",
    )(tokens, memory, docs, keep, attn, w1, w2, b1, gains)


def writer_kernel(
    res_ref, mem_ref, memgrad_ref, doc_ref, keep_ref, wr_ref, gate_ref, gbias_ref, gain_ref,
    newmem_ref, dres_ref, dkept_ref, gwr_ref, ggate_ref, gsmall_ref,
    n3_ref, ns_ref, kept_ref, sq_ref, tk_ref, tv_ref, p_ref, wt_ref, dsq_ref, dtk_ref, dtv_ref, dlog_ref, dw_ref,
):
    n, half, d = res_ref.shape
    slots = mem_ref.shape[1]
    gain = gain_ref[2:3, :]

    def norm(i, carry):
        rows = pl.ds(pl.multiple_of(i * half, half), half)
        small = pl.ds(pl.multiple_of(i * slots, slots), slots)
        hat, _ = norm_parts(res_ref[i])
        n3_ref[rows, :] = (hat * gain).astype(BF16)
        kept = mem_ref[i] * keep_ref[i][:, 0:1]
        kept_ref[small, :] = kept
        hat, _ = norm_parts(kept)
        ns_ref[small, :] = (hat * gain).astype(BF16)
        tk_ref[rows, :] = dot(n3_ref[rows, :], wr_ref[1]).astype(BF16)
        tv_ref[rows, :] = dot(n3_ref[rows, :], wr_ref[2]).astype(BF16)
        return carry

    lax.fori_loop(0, n, norm, 0)
    sq_ref[...] = (dot(ns_ref[...], wr_ref[0]) * 0.125).astype(BF16)
    low_half = lax.broadcasted_iota(jnp.int32, (1, 128), 1) < 64

    def halves(rows):
        zero = jnp.zeros_like(rows)
        return jnp.concatenate([jnp.where(low_half, rows, zero), jnp.where(low_half, zero, rows)], 0)

    def read(i, carry):
        rows = pl.ds(pl.multiple_of(i * half, half), half)
        small = pl.ds(pl.multiple_of(i * slots, slots), slots)
        docs = doc_ref[i].astype(F32)
        bias = jnp.where(docs == jnp.max(docs), 0.0, -1e30)[:, docs.shape[1] - half:]
        for pair in range(4):
            lanes = slice(pair * 128, pair * 128 + 128)
            scores = dot_nt(halves(sq_ref[small, lanes]), tk_ref[rows, lanes]) + bias
            e = jnp.exp(scores - jnp.max(scores, axis=1, keepdims=True))
            p = e * (1.0 / jnp.sum(e, axis=1, keepdims=True))
            p_ref[i, pair] = p
            mixed = dot(p.astype(BF16), tv_ref[rows, lanes])
            wt_ref[small, lanes] = jnp.where(low_half, mixed[:slots], mixed[slots:]).astype(BF16)
        return carry

    lax.fori_loop(0, n, read, 0)
    write = dot(wt_ref[...], wr_ref[3])
    kept = kept_ref[...]
    write_low = write.astype(BF16)
    kept_low = kept.astype(BF16)
    logit = dot(kept_low, gate_ref[0]) + dot(write_low, gate_ref[1]) + gbias_ref[...]
    gate = jax.nn.sigmoid(logit)
    new = gate * kept + (1.0 - gate) * write
    memgrad = memgrad_ref[...].reshape(n * slots, d)
    newmem_ref[...] = new.reshape(n, slots, d)
    dlogit = memgrad * (kept - write) * gate * (1.0 - gate)
    dlog_ref[...] = dlogit.astype(BF16)
    dlow = dlog_ref[...]
    gsmall_ref[0:1, :] = jnp.sum(dlow.astype(F32), axis=0, keepdims=True)
    ggate_ref[0] = dot_tn(kept_low, dlow).astype(ggate_ref.dtype)
    ggate_ref[1] = dot_tn(write_low, dlow).astype(ggate_ref.dtype)
    dkept = memgrad * gate + dot_nt(dlow, gate_ref[0])
    dwrite = memgrad * (1.0 - gate) + dot_nt(dlow, gate_ref[1])
    dkept_ref[...] = dkept.reshape(n, slots, d)
    dw_low = dwrite.astype(BF16)
    gwr_ref[3] = dot_tn(wt_ref[...], dw_low).astype(gwr_ref.dtype)
    dw_ref[...] = dot_nt(dw_low, wr_ref[3]).astype(BF16)

    def read_back(i, carry):
        rows = pl.ds(pl.multiple_of(i * half, half), half)
        small = pl.ds(pl.multiple_of(i * slots, slots), slots)
        for pair in range(4):
            lanes = slice(pair * 128, pair * 128 + 128)
            p = p_ref[i, pair]
            grads = halves(dw_ref[small, lanes])
            dp = dot_nt(grads, tv_ref[rows, lanes])
            ds = (p * (dp - jnp.sum(dp * p, axis=1, keepdims=True))).astype(BF16)
            dq = dot(ds, tk_ref[rows, lanes]) * 0.125
            dsq_ref[small, lanes] = jnp.where(low_half, dq[:slots], dq[slots:]).astype(BF16)
            dtk_ref[rows, lanes] = dot_tn(ds, halves(sq_ref[small, lanes])).astype(BF16)
            dtv_ref[rows, lanes] = dot_tn(p.astype(BF16), grads).astype(BF16)
        return carry

    lax.fori_loop(0, n, read_back, 0)
    gwr_ref[0] = dot_tn(ns_ref[...], dsq_ref[...]).astype(gwr_ref.dtype)
    gwr_ref[1] = dot_tn(n3_ref[...], dtk_ref[...]).astype(gwr_ref.dtype)
    gwr_ref[2] = dot_tn(n3_ref[...], dtv_ref[...]).astype(gwr_ref.dtype)
    grad = dot_nt(dsq_ref[...], wr_ref[0])
    hat, rstd = norm_parts(kept_ref[...])
    dkept_ref[...] += norm_back(grad, hat, rstd, gain).reshape(n, slots, d)
    ggain = jnp.sum(grad * hat, axis=0, keepdims=True)

    def back(i, ggain):
        rows = pl.ds(pl.multiple_of(i * half, half), half)
        grad = dot_nt(dtk_ref[rows, :], wr_ref[1]) + dot_nt(dtv_ref[rows, :], wr_ref[2])
        hat, rstd = norm_parts(res_ref[i])
        dres_ref[i] = norm_back(grad, hat, rstd, gain)
        return ggain + jnp.sum(grad * hat, axis=0, keepdims=True)

    gsmall_ref[1:2, :] = lax.fori_loop(0, n, back, ggain)


def call_writer(res, memory, memory_grad, docs, keep, wr, gate, gbias, gains):
    n, half, d = res.shape
    slots = memory.shape[1]
    rows, small = n * half, n * slots
    vmem = pl.BlockSpec(memory_space=pltpu.VMEM)
    return pl.pallas_call(
        writer_kernel,
        out_shape=[
            jax.ShapeDtypeStruct((n, slots, d), F32), jax.ShapeDtypeStruct((n, half, d), F32),
            jax.ShapeDtypeStruct((n, slots, d), F32), jax.ShapeDtypeStruct((4, d, d), BF16),
            jax.ShapeDtypeStruct((2, d, d), BF16), jax.ShapeDtypeStruct((2, d), F32),
        ],
        in_specs=[vmem] * 9,
        out_specs=[vmem] * 6,
        scratch_shapes=[
            pltpu.VMEM((rows, d), BF16), pltpu.VMEM((small, d), BF16), pltpu.VMEM((small, d), F32),
            pltpu.VMEM((small, d), BF16), pltpu.VMEM((rows, d), BF16), pltpu.VMEM((rows, d), BF16),
            pltpu.VMEM((n, 4, 2 * slots, half), F32), pltpu.VMEM((small, d), BF16), pltpu.VMEM((small, d), BF16),
            pltpu.VMEM((rows, d), BF16), pltpu.VMEM((rows, d), BF16), pltpu.VMEM((small, d), BF16),
            pltpu.VMEM((small, d), BF16),
        ],
        compiler_params=pltpu.CompilerParams(vmem_limit_bytes=VMEM_LIMIT),
        name="writer",
    )(res, memory, memory_grad, docs, keep, wr, gate, gbias, gains)


def ffn_back_kernel(
    og_ref, dres_ref, h1_ref, act_ref, slope_ref, w1_ref, w2_ref, gain_ref,
    dh_ref, gw1_ref, gw2_ref, gb_ref, ggain_ref,
    acc1_ref, acc2_ref, accb_ref, accg_ref,
):
    step = pl.program_id(0)
    seg = og_ref.shape[1]

    @pl.when(step == 0)
    def _():
        acc1_ref[...] = jnp.zeros_like(acc1_ref)
        acc2_ref[...] = jnp.zeros_like(acc2_ref)
        accb_ref[...] = jnp.zeros_like(accb_ref)
        accg_ref[...] = jnp.zeros_like(accg_ref)

    top = og_ref[0, 0:seg // 2, :].astype(F32)
    bottom = og_ref[0, seg // 2:, :].astype(F32) + dres_ref[0]
    dresult = jnp.concatenate([top, bottom], 0)
    low = dresult.astype(BF16)
    h1 = h1_ref[0]
    hat, rstd = norm_parts(h1)
    gain = gain_ref[1:2, :]
    n2t = (hat * gain).astype(BF16).T
    lowt = low.T
    grad = jnp.zeros_like(dresult)
    for part in range(4):
        acc2_ref[part] += dot(lowt, act_ref[0, part])
        dbefore = (dot_nt(low, w2_ref[part]) * slope_ref[0, part].astype(F32)).astype(BF16)
        accb_ref[part] += jnp.sum(dbefore.astype(F32), axis=0, keepdims=True)
        acc1_ref[part] += dot(n2t, dbefore)
        grad = grad + dot_nt(dbefore, w1_ref[part])
    accg_ref[...] += jnp.sum(grad * hat, axis=0, keepdims=True)
    dh_ref[0] = dresult + norm_back(grad, hat, rstd, gain)

    @pl.when(step == pl.num_programs(0) - 1)
    def _():
        gw1_ref[...] = acc1_ref[...].astype(gw1_ref.dtype)
        for part in range(4):
            gw2_ref[part] = acc2_ref[part].T.astype(gw2_ref.dtype)
        gb_ref[...] = accb_ref[...]
        ggain_ref[...] = accg_ref[...]


def call_ffn_back(out_grad, dres, h1, act, slope, w1, w2, gains):
    n, seg, d = out_grad.shape
    return pl.pallas_call(
        ffn_back_kernel,
        grid=(n,),
        out_shape=[
            jax.ShapeDtypeStruct((n, seg, d), F32), jax.ShapeDtypeStruct(w1.shape, BF16),
            jax.ShapeDtypeStruct(w2.shape, BF16), jax.ShapeDtypeStruct((4, 1, 512), F32),
            jax.ShapeDtypeStruct((1, d), F32),
        ],
        in_specs=[
            step_spec((seg, d)), step_spec((seg // 2, d)), step_spec((seg, d)), step_spec((4, seg, 512)),
            step_spec((4, seg, 512)), full_spec(w1.shape), full_spec(w2.shape), full_spec(gains.shape),
        ],
        out_specs=[
            step_spec((seg, d)), full_spec(w1.shape), full_spec(w2.shape), full_spec((4, 1, 512)), full_spec((1, d)),
        ],
        scratch_shapes=[
            pltpu.VMEM(w1.shape, F32), pltpu.VMEM((4, d, 512), F32), pltpu.VMEM((4, 1, 512), F32), pltpu.VMEM((1, d), F32),
        ],
        compiler_params=pltpu.CompilerParams(vmem_limit_bytes=VMEM_LIMIT),
        name="ffn_back",
    )(out_grad, dres, h1, act, slope, w1, w2, gains)


def attn_back_kernel(
    dh_ref, tok_ref, mem_ref, keep_ref, n1_ref, qt_ref, k_ref, v_ref, e_ref, linv_ref, ot_ref, dkept_ref,
    attn_ref, gain_ref,
    gtok_ref, gmem_ref, gattn_ref, ggain_ref,
    dot_ref, kt_ref, dqt_ref, dk_ref, dv_ref, qp_ref, dp_ref, acc_ref, accg_ref,
):
    step = pl.program_id(0)
    seg = tok_ref.shape[1]
    slots = mem_ref.shape[1]

    @pl.when(step == 0)
    def _():
        acc_ref[...] = jnp.zeros_like(acc_ref)
        accg_ref[...] = jnp.zeros_like(accg_ref)

    dh = dh_ref[0]
    low = dh.astype(BF16)
    acc_ref[3] += dot(ot_ref[0], low)
    dot_ref[...] = dot_nt(attn_ref[3], low)
    kt_ref[...] = k_ref[0].T
    qp_ref[...] = jnp.zeros_like(qp_ref)
    dp_ref[...] = jnp.zeros_like(dp_ref)

    def one_pair(pair, carry):
        lanes = pl.ds(pl.multiple_of(pair * 128, 128), 128)
        dk_ref[:, lanes] = jnp.zeros((seg + 128, 128), F32)
        dv_ref[:, lanes] = jnp.zeros((seg + 128, 128), F32)
        for block, (first, last) in enumerate(SPANS):
            start = STARTS[block]
            columns = pl.ds(block * BLOCK, BLOCK)
            linv = linv_ref[0, pair, block, :, :]
            mixed_grad = dot_ref[lanes, columns]
            top = (mixed_grad[0:64] * linv[:, 0:128]).astype(BF16)
            bottom = (mixed_grad[64:128] * linv[:, 128:256]).astype(BF16)
            mixed = ot_ref[0, lanes, columns].astype(F32)
            delta = jnp.concatenate(
                [
                    jnp.sum(top.astype(F32) * mixed[0:64], axis=0, keepdims=True),
                    jnp.sum(bottom.astype(F32) * mixed[64:128], axis=0, keepdims=True),
                ],
                1,
            )
            held = dp_ref.at[block]
            held[0:64, 0:128] = top
            held[64:128, 128:256] = bottom
            query = qp_ref.at[block]
            diagonal_pair(query, qt_ref[0, lanes, columns])
            e = e_ref[0, pair, start:start + last - first, :]
            dp = dot(v_ref[0, first:last, lanes], held[...])
            ds = (e.astype(F32) * (dp - delta)).astype(BF16)
            dv_ref[first:last, lanes] += dot_nt(e, held[...])
            dk_ref[first:last, lanes] += dot_nt(ds, query[...])
            dq = dot(kt_ref[lanes, first:last], ds) * 0.125
            dqt_ref[lanes, columns] = jnp.concatenate([dq[0:64, 0:128], dq[64:128, 128:256]], 0).astype(BF16)
        return carry

    lax.fori_loop(0, 4, one_pair, 0)
    n1t = n1_ref[0].T
    dk = dk_ref[...].astype(BF16)
    dv = dv_ref[...].astype(BF16)
    acc_ref[0] += dot_nt(n1t[:, 128:], dqt_ref[...])
    acc_ref[1] += dot(n1t, dk)
    acc_ref[2] += dot(n1t, dv)
    gain = gain_ref[0:1, :]
    grad = dot_nt(dk, attn_ref[1]) + dot_nt(dv, attn_ref[2])
    slot_grad = grad[0:slots]
    kept = mem_ref[0] * keep_ref[0][:, 0:1]
    hat, rstd = norm_parts(kept)
    ggain = jnp.sum(slot_grad * hat, axis=0, keepdims=True)
    gmem_ref[0] = (dkept_ref[0] + norm_back(slot_grad, hat, rstd, gain)) * keep_ref[0][:, 0:1]
    grad = grad[128:] + dot_nt(dqt_ref[...].T, attn_ref[0])
    hat, rstd = norm_parts(tok_ref[0].astype(F32))
    accg_ref[...] += ggain + jnp.sum(grad * hat, axis=0, keepdims=True)
    gtok_ref[0] = dh + norm_back(grad, hat, rstd, gain)

    @pl.when(step == pl.num_programs(0) - 1)
    def _():
        gattn_ref[...] = acc_ref[...].astype(gattn_ref.dtype)
        ggain_ref[...] = accg_ref[...]


def call_attn_back(dh, tokens, memory, keep, n1, qt, k, v, e, linv, ot, dkept, attn, gains):
    n, seg, d = tokens.shape
    slots = memory.shape[1]
    return pl.pallas_call(
        attn_back_kernel,
        grid=(n,),
        out_shape=[
            jax.ShapeDtypeStruct((n, seg, d), F32), jax.ShapeDtypeStruct((n, slots, d), F32),
            jax.ShapeDtypeStruct((4, d, d), BF16), jax.ShapeDtypeStruct((1, d), F32),
        ],
        in_specs=[
            step_spec((seg, d)), step_spec((seg, d)), step_spec((slots, d)), step_spec((1, 128)),
            step_spec((seg + 128, d)), step_spec((d, seg)), step_spec((seg + 128, d)), step_spec((seg + 128, d)),
            step_spec((4, LIVE, 256)), step_spec((4, 4, 1, 256)), step_spec((d, seg)), step_spec((slots, d)),
            full_spec(attn.shape), full_spec(gains.shape),
        ],
        out_specs=[step_spec((seg, d)), step_spec((slots, d)), full_spec((4, d, d)), full_spec((1, d))],
        scratch_shapes=[
            pltpu.VMEM((d, seg), F32), pltpu.VMEM((d, seg + 128), BF16), pltpu.VMEM((d, seg), BF16),
            pltpu.VMEM((seg + 128, d), F32), pltpu.VMEM((seg + 128, d), F32), pltpu.VMEM((4, 128, 256), BF16),
            pltpu.VMEM((4, 128, 256), BF16), pltpu.VMEM((4, d, d), F32), pltpu.VMEM((1, d), F32),
        ],
        compiler_params=pltpu.CompilerParams(vmem_limit_bytes=VMEM_LIMIT),
        name="attn_back",
    )(dh, tokens, memory, keep, n1, qt, k, v, e, linv, ot, dkept, attn, gains)


def local_layer(tokens, memory, docs, resets, out_grad, memory_grad, attn, w1, w2, wr, gate, b1, gbias, gains):
    n = tokens.shape[0]
    keep = jnp.broadcast_to((1 - resets).astype(F32)[:, None, None], (n, 1, 128))
    docs = docs[:, None, :]
    out, res, h1, n1, qt, k, v, e, linv, ot, act, slope = call_forward(
        tokens, memory, docs, keep, attn, w1, w2, b1, gains
    )
    new_memory, dres, dkept, gwr, ggate, gsmall = call_writer(
        res, memory, memory_grad, docs, keep, wr, gate, gbias, gains
    )
    dh, gw1, gw2, gb, ggain_two = call_ffn_back(out_grad, dres, h1, act, slope, w1, w2, gains)
    grad_tokens, grad_memory, gattn, ggain_one = call_attn_back(
        dh, tokens, memory, keep, n1, qt, k, v, e, linv, ot, dkept, attn, gains
    )
    ggains = jnp.concatenate([ggain_one, ggain_two, gsmall[1:2]], 0)
    return out, new_memory, grad_tokens, grad_memory, gattn, gw1, gw2, gwr, ggate, gb.reshape(-1), gsmall[0], ggains


def pack_weights(attn_qkv, attn_out, ffn_in, ffn_out, writer_qkv, writer_out, gate_weight):
    rows, d = attn_out.shape
    blocks = ffn_in.shape[1] // d
    return jnp.concatenate(
        [
            attn_qkv, attn_out[None], ffn_in.reshape(rows, blocks, d).transpose(1, 0, 2), ffn_out.reshape(blocks, rows, d),
            writer_qkv, writer_out[None], gate_weight.reshape(2, rows, d),
        ],
        0,
    )


def unpack_weights(gathered):
    n, _, rows, d = gathered.shape

    def by_rows(first, last):
        return gathered[:, first:last].transpose(1, 0, 2, 3).reshape(last - first, n * rows, d)

    return (
        by_rows(0, 4), by_rows(4, 8), gathered[:, 8:12].reshape(4, d, d), by_rows(12, 16), gathered[:, 16:18].reshape(2, d, d),
    )


def pack_grads(n, gattn, gw1, gw2, gwr, ggate):
    d = gattn.shape[1]
    rows = d // n

    def by_rows(grad):
        return grad.reshape(-1, n, rows, d).transpose(1, 0, 2, 3)

    return jnp.concatenate(
        [by_rows(gattn), by_rows(gw1), gw2.reshape(n, 4, rows, d), by_rows(gwr), ggate.reshape(n, 2, rows, d)], 1
    )


def unpack_owned(owned):
    _, rows, d = owned.shape
    return (
        owned[0:3], owned[3], owned[4:8].transpose(1, 0, 2).reshape(rows, 4 * d), owned[8:12].reshape(4 * rows, d),
        owned[12:15], owned[15], owned[16:18].reshape(2 * rows, d),
    )


def body(
    tokens, memory, doc_ids, resets, out_grad, memory_grad,
    attn_qkv, attn_out, ffn_in, ffn_bias, ffn_out, writer_qkv, writer_out, gate_weight, gate_bias, gains,
):
    n = lax.axis_size("dp")
    micro, segs, seg, d = tokens.shape
    slots = memory.shape[2]
    rows = attn_out.shape[0]
    packed = pack_weights(attn_qkv, attn_out, ffn_in, ffn_out, writer_qkv, writer_out, gate_weight)
    small = jnp.concatenate([ffn_bias.reshape(4, rows), gate_bias[None], gains], 0).astype(F32)
    small = lax.all_gather(small, "dp", axis=0)
    bias_one = small[:, 0:4].reshape(4, 1, d)
    small = small.transpose(1, 0, 2).reshape(8, d)
    attn, w1, w2, wr, gate = unpack_weights(lax.all_gather(packed, "dp", axis=0))
    out, new_memory, grad_tokens, grad_memory, gattn, gw1, gw2, gwr, ggate, gb, ggb, ggains = local_layer(
        tokens.reshape(micro * segs, seg, d), memory.reshape(micro * segs, slots, d), doc_ids.reshape(micro * segs, seg),
        resets.reshape(micro * segs), out_grad.reshape(micro * segs, seg, d), memory_grad.reshape(micro * segs, slots, d),
        attn, w1, w2, wr, gate, bias_one, small[4:5], small[5:8],
    )
    owned = lax.psum_scatter(pack_grads(n, gattn, gw1, gw2, gwr, ggate).astype(F32), "dp", scatter_dimension=0, tiled=False)
    owned = lax.psum(owned.astype(BF16), "outer").astype(F32)
    small_grads = jnp.concatenate(
        [gb.reshape(n, 4 * rows), ggb.reshape(n, rows), ggains.reshape(3, n, rows).transpose(1, 0, 2).reshape(n, 3 * rows)], 1
    )
    small_owned = lax.psum(lax.psum_scatter(small_grads, "dp", scatter_dimension=0, tiled=False), "outer")
    gqkv, gout, gin, gffn, gwqkv, gwout, ggw = unpack_owned(owned)
    return (
        out.reshape(micro, segs, seg, d), new_memory.reshape(micro, segs, slots, d),
        grad_tokens.reshape(micro, segs, seg, d), grad_memory.reshape(micro, segs, slots, d),
        gqkv, gout, gin, small_owned[0:4 * rows], gffn, gwqkv, gwout, ggw, small_owned[4 * rows:5 * rows],
        small_owned[5 * rows:].reshape(3, rows),
    )


def solution(mesh):
    split = ("dp", "outer")
    whole = P(None, split, None, None)
    weights = (
        P(None, "dp", None), P("dp", None), P("dp", None), P("dp"), P("dp", None), P(None, "dp", None),
        P("dp", None), P("dp", None), P("dp"), P(None, "dp"),
    )
    return jax.shard_map(
        body,
        mesh=mesh,
        in_specs=(whole, whole, P(None, split, None), P(None, split), whole, whole) + weights,
        out_specs=(whole, whole, whole, whole) + weights,
        check_vma=False,
    )
```

time: 1460 us -> 702 us (0.48)
  matrix products: 388 us -> 0 us
  waiting for transfers between devices: 533 us -> 363 us
  blocking collectives: 273 us -> 121 us
  Pallas kernels: 0 us -> 146 us
  other arithmetic: 144 us -> 16.4 us
  local copies, waits for them, and re-layouts: 79.6 us -> 40.9 us
    dot_general x172 -> x0, matrix products: 343 us -> none  [the longest x44 127 us: matmul(): return jnp.dot(left_side, right_side, preferred_element_type=jnp.float32)]
    reduce_scatter x7 -> x1, waiting for transfers between devices: 497 us -> 283 us  [body(): lax.psum_scatter(pack_grads(n, gattn, gw1, gw2, gwr, ggate).astype(F32),...]
    pallas_call x0 -> x4, Pallas kernels: none -> 146 us  [the longest x1 53 us: call_forward(): pl.pallas_call(forward_kernel, grid=(n,), out_shape=[jax.ShapeDtypeStruct...]
    all_gather x4 -> x1, blocking collectives: 163 us -> 43.3 us  [body(): small = lax.all_gather(small, 'dp', axis=0)]
    all_gather x5 -> x1, waiting for transfers between devices: 0.09 us -> 79.9 us  [body(): lax.all_gather(packed, 'dp', axis=0)]
    convert_element_type x32 -> x5, other arithmetic: 78.8 us -> 16.3 us  [the longest x1 12.9 us: body(): pack_grads(n, gattn, gw1, gw2, gwr, ggate).astype(F32)]
    sub x8 -> x0, matrix products: 45.5 us -> none  [attention_forward(): expanded = jnp.exp(scores - largest)]
    unnamed x2 -> x1, blocking collectives: 111 us -> 75 us
  transfers between devices with their start and end apart: 15 -> 3, of which waited for: 8 -> 2; matrix products, arithmetic and copies ran while one was open for 24% -> 1% of each run, Pallas kernels for 0% -> 0%
where the time goes in v1:
time: 702 us; the launch traced here: 701 us
  waiting for transfers between devices  363 us (52%)
  Pallas kernels  146 us (21%)
  blocking collectives  121 us (17%)
  local copies, waits for them, and re-layouts  40.9 us (6%)
  other arithmetic  16.4 us (2%)
  between operations  14 us (2%)
    reduce_scatter x1, waiting for transfers between devices, body(): lax.psum_scatter(pack_grads(n, gattn, gw1, gw2, gwr, ggate).astype(F32),...  283 us
    all_gather x1, waiting for transfers between devices, body(): lax.all_gather(packed, 'dp', axis=0)  79.9 us
    unnamed x1, blocking collectives  75 us
    pallas_call x1, Pallas kernels, call_forward(): pl.pallas_call(forward_kernel, grid=(n,), out_shape=[jax.ShapeDtypeStruct...  53 us
    all_gather x1, blocking collectives, body(): small = lax.all_gather(small, 'dp', axis=0)  43.3 us
    pallas_call x1, Pallas kernels, call_attn_back(): pl.pallas_call(attn_back_kernel, grid=(n,), out_shape=[jax.ShapeDtypeStru...  40.1 us
    pallas_call x1, Pallas kernels, call_ffn_back(): pl.pallas_call(ffn_back_kernel, grid=(n,), out_shape=[jax.ShapeDtypeStruc...  29.7 us
    pallas_call x1, Pallas kernels, call_writer(): pl.pallas_call(writer_kernel, out_shape=[jax.ShapeDtypeStruct((n, slots,...  23 us
  transfers between devices with their start and end apart: 3, of which 2 were waited for; matrix products, arithmetic and copies ran while one was open for 1% of the time, Pallas kernels for 0%

profile of v1, /device:TPU:0, one launch (start us, length us, event | category | flops | bytes accessed | tf_op | source)
XLA Modules:
  0.0 701.2 jit_solution(8771104339919253855)
XLA Ops:
  7.2 0.8 copy.91
  8.0 0.8 copy.94
  8.9 0.9 copy.95
  9.8 1.0 copy.90
  10.8 1.0 reshape.183
  11.8 1.0 copy.92
  12.8 1.0 copy.93
  14.5 1.0 copy.96
  15.7 43.3 %all_gather.12 = f32[16,8,32]{2,1,0:T(8,128)S(1)} all-gather(f32[1,8,32]{2,1,0:T(8,128)S(1)} %maximum_convert_fusion), channel_id=1, replica_groups=mesh['dp'=16,'outer'=2] {'dp'}, dimensions={0}, use_global_device_ids=true | all-gather | bytes 17408 | tf_op jit(solution)/shard_map/all_gather | solution.py:533
  61.1 79.9 %all-gather.3.cloned.1.call-done = bf16[288,32,512]{2,1,0:T(8,128)(2,1)} async-done(((bf16[18,32,512]{2,1,0:T(8,128)(2,1)}), bf16[288,32,512]{2,1,0:T(8,128)(2,1)}) %all-gather.3.cloned.1.call-update) | async-done | bytes 9437200 | tf_op jit(solution)/shard_map/all_gather | solution.py:536
  141.1 2.3 slice.102
  143.4 5.0 slice_bitcast_fusion
  148.4 1.7 copy.100
  150.1 1.6 copy.98
  151.7 1.6 copy.97
  153.9 53.0 %forward_rows.1 = (bf16[4,512,512]{2,1,0:T(8,128)(2,1)}, f32[4,256,512]{2,1,0:T(8,128)}, f32[4,512,512]{2,1,0:T(8,128)}, bf16[4,640,512]{2,1,0:T(8,128)(2,1)}, b...) custom-call(bf16[4,512,512]{2,1,0:T(8,128)(2,1)} %bitcast.75, ...), custom_call_target="tpu_custom_call" | custom-call | tf_op jit(solution)/shard_map/forward_rows/pallas_call | solution.py:141
  206.9 23.0 %writer.1 = (f32[4,64,512]{2,1,0:T(8,128)}, f32[4,256,512]{2,1,0:T(8,128)}, f32[4,64,512]{2,1,0:T(8,128)}, bf16[4,512,512]{2,1,0:T(8,128)(2,1)}, bf16[2,512,512]{2,1,0:T(8,128)(2,1)}, /*index=5*/f32[2,512]{1,0:T(2,128)}) custom-call(f32[4,256,512]{2,1,0:T(8,128)} %get-tuple-element.42.res_ref, f32[4,64,512]{2,1,0:T(8,128)} %bitcast.79, ...), custom_call_target="tpu_custom_call" | custom-call | tf_op jit(solution)/shard_map/writer/pallas_call | solution.py:265
  229.9 29.7 %ffn_back.1 = (f32[4,512,512]{2,1,0:T(8,128)}, bf16[4,512,512]{2,1,0:T(8,128)(2,1)}, bf16[4,512,512]{2,1,0:T(8,128)(2,1)}, f32[4,1,512]{2,1,0:T(1,128)}, f32[1,512]{1,0:T(1,128)}) custom-call(bf16[4,512,512]{2,1,0:T(8,128)(2,1)} %bitcast.86, f32[4,256,512]{2,1,0:T(8,128)} %get-tuple-element.44.dres_ref, f32[4,512,512]{2,1,0:T(8,128)} %get-tuple-element.45.h1_ref, ...), custom_call_target="tpu_custom_call" | custom-call | tf_op jit(solution)/shard_map/ffn_back/pallas_call | solution.py:331
  259.6 40.1 %attn_back.1 = (f32[4,512,512]{2,1,0:T(8,128)}, f32[4,64,512]{2,1,0:T(8,128)}, bf16[4,512,512]{2,1,0:T(8,128)(2,1)}, f32[1,512]{1,0:T(1,128)}) custom-call(f32[4,512,512]{2,1,0:T(8,128)} %get-tuple-element.48.dh_ref, bf16[4,512,512]{2,1,0:T(8,128)(2,1)} %bitcast.76, f32[4,64,512]{2,1,0:T(8,128)} %bitcast.80, f32[4,1,128]{2,1,0:T(1,128)} %broadcast_in_dim.6.keep_ref, ...), custom_call_target="tpu_custom_call" | custom-call | tf_op jit(solution)/shard_map/attn_back/pallas_call | solution.py:438
  299.6 3.3 bitcast_dynamic-update-slice_fusion.2
  303.0 1.7 bitcast_dynamic-update-slice_fusion.1
  305.3 1.6 constant_dynamic-update-slice_fusion.1
  306.9 0.8 copy-done.1
  307.7 1.6 bitcast_dynamic-update-slice_fusion
  309.2 1.1 constant_dynamic-update-slice_fusion
  310.4 12.9 %convert_element_type.35 = f32[16,18,32,512]{3,2,1,0:T(8,128)} convert(bf16[16,18,32,512]{3,2,1,0:T(8,128)(2,1)} %constant_dynamic-update-slice_fusion) | non-fusion elementwise | flops 4718592 | bytes 28311552 | tf_op jit(solution)/shard_map/convert_element_type | solution.py:542
  323.4 283.4 %reduce-scatter.2.cloned.1.call-done = f32[1,18,32,512]{3,2,1,0:T(8,128)} async-done(((f32[16,18,32,512]{3,2,1,0:T(8,128)}), f32[1,18,32,512]{3,2,1,0:T(8,128)}) %reduce-scatter.2.cloned.1.call-update) | async-done | bytes 1179664 | tf_op jit(solution)/shard_map/reduce_scatter | solution.py:542
  606.8 2.2 convert_bitcast_fusion
  609.9 75.0 %all-reduce = f32[16,256]{1,0:T(8,128)S(1)} all-reduce(f32[16,256]{1,0:T(8,128)S(1)} %pad_maximum_fusion), channel_id=4, replica_groups=mesh['dp'=16,'outer'=2] {'dp'}, use_global_device_ids=true, to_apply=%region_2.0.clone | all-reduce | flops 4096 | bytes 32768
  685.5 2.5 psum.15
  689.8 1.3 convert_element_type.38
  693.9 0.8 fusion
  (64 shorter events, 10.6 us)
Async XLA Ops:
  7.2 133.9 %all-gather.3.cloned.1.call-start = ((), (), s32[]{:S(2)}) async-start(), calls=%async_computation.3 | async-start | bytes 10027008 | tf_op jit(solution)/shard_map/all_gather | solution.py:536
  10.7 4.8 copy-start.11
  10.8 4.9 copy-start.9
  10.8 4.9 copy-start.10
  12.8 48.3 %copy-start.12 = (s32[4,1]{0,1:T(1,128)S(1)}, s32[4,1]{0,1:T(1,128)}, u32[]{:S(2)}) copy-start(s32[4,1]{0,1:T(1,128)} %param.19) | copy-start | bytes 52
  15.5 591.2 %reduce-scatter.2.cloned.1.call-start = ((), (), s32[]{:S(2)}) async-start(), calls=%async_computation.1 | async-start | bytes 20054016 | tf_op jit(solution)/shard_map/reduce_scatter | solution.py:542
  299.6 3.3 copy-start.3
  303.0 2.3 copy-start.2
  305.3 2.3 copy-start.1
  307.7 1.6 copy-start.4
  323.3 285.7 %copy-start.13 = (u32[32]{0:T(128)S(1)}, u32[32]{0:T(128)}, u32[]{:S(2)}) copy-start(u32[32]{0:T(128)} %constant.10) | copy-start | bytes 388
  323.3 286.2 %copy-start.6 = (f32[2,512]{1,0:T(2,128)S(1)}, f32[2,512]{1,0:T(2,128)}, u32[]{:S(2)}) copy-start(f32[2,512]{1,0:T(2,128)} %get-tuple-element.65) | copy-start | bytes 12292
  323.3 286.3 %copy-start.7 = (f32[1,512]{1,0:T(1,128)S(1)}, f32[1,512]{1,0:T(1,128)}, u32[]{:S(2)}) copy-start(f32[1,512]{1,0:T(1,128)} %get-tuple-element.67) | copy-start | bytes 6148
  323.3 286.3 %copy-start.8 = (f32[1,512]{1,0:T(1,128)S(1)}, f32[1,512]{1,0:T(1,128)}, u32[]{:S(2)}) copy-start(f32[1,512]{1,0:T(1,128)} %get-tuple-element.66) | copy-start | bytes 6148
  323.3 286.5 %copy-start.5 = (f32[4,1,512]{2,1,0:T(1,128)S(1)}, f32[4,1,512]{2,1,0:T(1,128)}, u32[]{:S(2)}) copy-start(f32[4,1,512]{2,1,0:T(1,128)} %get-tuple-element.64) | copy-start | bytes 24580
  323.4 366.4 %all-reduce.3.cloned.1.call-start = ((), (), s32[]{:S(2)}) async-start(), calls=%async_computation.2 | async-start | bytes 1179648 | tf_op jit(solution)/shard_map/psum | solution.py:543
  689.8 2.7 copy-start
Sparse Core Ops, SparseCore 0:
  15.7 125.3 all-gather.2
  323.4 283.2 reduce-scatter.1
  609.1 17.9 all-reduce.2

commit v2 on v1

--- a/solution.py
+++ b/solution.py
@@ -477,46 +477,525 @@
     return out, new_memory, grad_tokens, grad_memory, gattn, gw1, gw2, gwr, ggate, gb.reshape(-1), gsmall[0], ggains
 
 
-def pack_weights(attn_qkv, attn_out, ffn_in, ffn_out, writer_qkv, writer_out, gate_weight):
+MESH = pl.DeviceIdType.MESH
+
+
+class Place:
+    def __init__(self):
+        self.dp = lax.axis_index("dp")
+        self.core = lax.axis_index("outer")
+        self.z, self.y, self.x = self.dp // 4, (self.dp // 2) % 2, self.dp % 2
+
+    def sibling(self):
+        return (self.dp, 1 - self.core)
+
+    def along_x(self):
+        return (self.dp + 1 - 2 * self.x, self.core)
+
+    def along_y(self):
+        return (self.dp + 2 - 4 * self.y, self.core)
+
+    def other_z(self, shift):
+        return lax.rem(self.z + shift, 4)
+
+    def along_z(self, shift):
+        return (self.dp + 4 * (self.other_z(shift) - self.z), self.core)
+
+    def greet(self):
+        barrier = pltpu.get_barrier_semaphore()
+        everyone = [self.sibling(), self.along_x(), self.along_y()] + [self.along_z(shift) for shift in (1, 2, 3)]
+        for device in everyone:
+            pl.semaphore_signal(barrier, inc=1, device_id=device, device_id_type=MESH)
+        pl.semaphore_wait(barrier, len(everyone))
+
+
+def remote(src, dst, send, recv, device):
+    return pltpu.make_async_remote_copy(
+        src_ref=src, dst_ref=dst, send_sem=send, recv_sem=recv, device_id=device, device_id_type=MESH
+    )
+
+
+class Gather:
+    STAGES = 7
+
+    def __init__(self, place, view, own, lane, send, recv, local):
+        self.place, self.view, self.own, self.lane = place, view, own, lane
+        self.send, self.recv, self.local = send, recv, local
+        self.unit = 2 * place.core + lane
+        self.sent = []
+        self.every = slice(None)
+
+    def go(self, stage, src, dst, device):
+        copy = remote(src, dst, self.send.at[stage], self.recv.at[stage], device)
+        copy.start()
+        self.sent.append(copy)
+
+    def arrived(self, stage, dst):
+        remote(dst, dst, self.send.at[stage], self.recv.at[stage], self.place.sibling()).wait_recv()
+
+    def stage_z(self):
+        at = self.place
+        mine = self.view(self.unit, at.z, at.y, at.x)
+        self.keep = pltpu.make_async_copy(self.own, mine, self.local)
+        self.keep.start()
+        for shift in (1, 2, 3):
+            self.go(shift - 1, self.own, mine, at.along_z(shift))
+
+    def wait_z(self):
+        at = self.place
+        self.keep.wait()
+        for shift in (1, 2, 3):
+            self.arrived(shift - 1, self.view(self.unit, at.other_z(4 - shift), at.y, at.x))
+
+    def stage_first(self):
+        at = self.place
+        part = self.view(self.unit, self.every, at.y, at.x)
+        self.go(3, part, part, at.along_y() if self.lane else at.along_x())
+
+    def wait_first(self):
+        at = self.place
+        if self.lane:
+            self.arrived(3, self.view(self.unit, self.every, 1 - at.y, at.x))
+        else:
+            self.arrived(3, self.view(self.unit, self.every, at.y, 1 - at.x))
+
+    def half(self, unit, far):
+        at = self.place
+        if self.lane:
+            return self.view(unit, self.every, self.every, 1 - at.x if far else at.x)
+        return self.view(unit, self.every, 1 - at.y if far else at.y, self.every)
+
+    def stage_second(self):
+        at = self.place
+        part = self.half(self.unit, False)
+        self.go(4, part, part, at.along_x() if self.lane else at.along_y())
+        self.go(5, part, part, at.sibling())
+
+    def wait_second(self):
+        self.arrived(4, self.half(self.unit, True))
+
+    def stage_share(self):
+        part = self.half(self.unit, True)
+        self.go(6, part, part, self.place.sibling())
+
+    def wait_share(self):
+        other = 2 * (1 - self.place.core) + self.lane
+        self.arrived(5, self.half(other, False))
+        self.arrived(6, self.half(other, True))
+
+    def finish(self):
+        for copy in self.sent:
+            copy.wait_send()
+
+
+class GatherSmall:
+    def __init__(self, place, view, own, send, recv, local):
+        self.place, self.view, self.own = place, view, own
+        self.send, self.recv, self.local = send, recv, local
+        self.sent = []
+
+    go = Gather.go
+    arrived = Gather.arrived
+    finish = Gather.finish
+
+    def stage_z(self):
+        at = self.place
+        mine = self.view(at.z, at.y, at.x)
+        self.keep = pltpu.make_async_copy(self.own, mine, self.local)
+        self.keep.start()
+        for shift in (1, 2, 3):
+            self.go(shift - 1, self.own, mine, at.along_z(shift))
+
+    def wait_z(self):
+        at = self.place
+        self.keep.wait()
+        for shift in (1, 2, 3):
+            self.arrived(shift - 1, self.view(at.other_z(4 - shift), at.y, at.x))
+
+    def stage_first(self):
+        at = self.place
+        part = self.view(slice(None), at.y, at.x)
+        self.go(3, part, part, at.along_x())
+
+    def wait_first(self):
+        at = self.place
+        self.arrived(3, self.view(slice(None), at.y, 1 - at.x))
+
+    def stage_second(self):
+        at = self.place
+        part = self.view(slice(None), at.y, slice(None))
+        self.go(4, part, part, at.along_y())
+
+    def wait_second(self):
+        at = self.place
+        self.arrived(4, self.view(slice(None), 1 - at.y, slice(None)))
+
+
+def unit_first(ref):
+    return lambda u, z, y, x: ref.at[u, z, y, x]
+
+
+def unit_last(ref):
+    return lambda u, z, y, x: ref.at[z, y, x, u]
+
+
+def gather_kernel(
+    src_ref, gsrc_ref, ssrc_ref, attn_ref, w1_ref, w2_ref, wr_ref, gate_ref, small_ref, send, recv, local, ssend, srecv, slocal
+):
+    place = Place()
+    place.greet()
+    views = [unit_first(attn_ref), unit_first(w1_ref), unit_last(w2_ref), unit_first(wr_ref), unit_last(gate_ref)]
+    rounds = []
+    for r, view in enumerate(views):
+        lanes = []
+        for lane in range(2):
+            unit = 2 * place.core + lane
+            own = src_ref.at[4 * r + unit] if r < 4 else gsrc_ref.at[unit]
+            lanes.append(Gather(place, view, own, lane, send.at[r, lane], recv.at[r, lane], local.at[r, lane]))
+        rounds.append(lanes)
+    small = GatherSmall(place, lambda z, y, x: small_ref.at[z, y, x], ssrc_ref, ssend, srecv, slocal)
+
+    def each(r, name):
+        for lane in rounds[r]:
+            getattr(lane, name)()
+
+    last = len(rounds) - 1
+    small.stage_z()
+    each(0, "stage_z")
+    small.wait_z()
+    small.stage_first()
+    each(0, "wait_z")
+    for r in range(last + 1):
+        each(r, "stage_first")
+        if r == 0:
+            small.wait_first()
+            small.stage_second()
+        if r > 0:
+            each(r - 1, "wait_second")
+            each(r - 1, "stage_share")
+        if r < last:
+            each(r + 1, "stage_z")
+        each(r, "wait_first")
+        each(r, "stage_second")
+        if r < last:
+            each(r + 1, "wait_z")
+    small.wait_second()
+    each(last, "wait_second")
+    each(last, "stage_share")
+    for r in range(last + 1):
+        each(r, "wait_share")
+        each(r, "finish")
+    small.finish()
+
+
+def call_gather(units, gate_units, small):
+    _, rows, d = units.shape
+    any_space = pl.BlockSpec(memory_space=pl.ANY)
+    first = (4, 4, 2, 2, rows, d)
+    shapes = [
+        (first, BF16), (first, BF16), ((4, 2, 2, 4, rows, d), BF16), (first, BF16), ((4, 2, 2, 4, rows // 2, d), BF16),
+        ((4, 2, 2, 8, 128), F32),
+    ]
+    return pl.pallas_call(
+        gather_kernel,
+        out_shape=[jax.ShapeDtypeStruct(shape, kind) for shape, kind in shapes],
+        in_specs=[any_space] * 3,
+        out_specs=[any_space] * 6,
+        scratch_shapes=[
+            pltpu.SemaphoreType.DMA((5, 2, 7)), pltpu.SemaphoreType.DMA((5, 2, 7)), pltpu.SemaphoreType.DMA((5, 2)),
+            pltpu.SemaphoreType.DMA((5,)), pltpu.SemaphoreType.DMA((5,)), pltpu.SemaphoreType.DMA,
+        ],
+        compiler_params=pltpu.CompilerParams(collective_id=0, has_side_effects=True),
+        name="gather_weights",
+    )(units, gate_units, small)
+
+
+class Reduce:
+    def __init__(self, place, grad, lane, acc, wide, mid, narrow, final, send, recv):
+        self.place, self.grad, self.lane = place, grad, lane
+        self.acc, self.wide, self.mid, self.narrow, self.final = acc, wide, mid, narrow, final
+        self.send, self.recv = send, recv
+        self.unit = 2 * place.core + lane
+        self.other = 2 * (1 - place.core) + lane
+        self.sent = []
+        self.every = slice(None)
+
+    go = Gather.go
+    arrived = Gather.arrived
+    finish = Gather.finish
+
+    def stage_share(self):
+        e = self.every
+        self.go(0, self.grad(self.other, e, e, e), self.wide, self.place.sibling())
+
+    def wait_share(self):
+        self.arrived(0, self.wide)
+        for z in range(4):
+            self.acc[z] = self.grad(self.unit, z, self.every, self.every)[...] + self.wide[z]
+
+    def half(self, far):
+        at = self.place
+        if self.lane:
+            return self.acc.at[:, :, 1 - at.x if far else at.x]
+        return self.acc.at[:, 1 - at.y if far else at.y]
+
+    def stage_first(self):
+        at = self.place
+        self.go(1, self.half(True), self.mid, at.along_x() if self.lane else at.along_y())
+
+    def wait_first(self):
+        self.arrived(1, self.mid)
+        half = self.half(False)
+        half[...] = half[...] + self.mid[...]
+
+    def stage_second(self):
+        at = self.place
+        if self.lane:
+            part, device = self.acc.at[:, 1 - at.y, at.x], at.along_y()
+        else:
+            part, device = self.acc.at[:, at.y, 1 - at.x], at.along_x()
+        self.go(2, part, self.narrow.at[0:4], device)
+
+    def wait_second(self):
+        at = self.place
+        self.arrived(2, self.narrow.at[0:4])
+        part = self.acc.at[:, at.y, at.x]
+        part[...] = part[...] + self.narrow[0:4]
+
+    def stage_z(self):
+        at = self.place
+        for shift in (1, 2, 3):
+            self.go(2 + shift, self.acc.at[at.other_z(shift), at.y, at.x], self.narrow.at[3 + shift], at.along_z(shift))
+
+    def wait_z(self):
+        at = self.place
+        total = self.acc[at.z, at.y, at.x].astype(F32)
+        for shift in (1, 2, 3):
+            self.arrived(2 + shift, self.narrow.at[3 + shift])
+            total = total + self.narrow[3 + shift].astype(F32)
+        self.final[self.unit] = total
+
+    def stage_final(self):
+        self.go(6, self.final.at[self.unit], self.final.at[self.unit], self.place.sibling())
+
+    def wait_final(self):
+        self.arrived(6, self.final.at[self.other])
+
+
+class ReduceSmall:
+    def __init__(self, place, grad, wide, mid, narrow, final, send, recv):
+        self.place, self.acc = place, grad
+        self.wide, self.mid, self.narrow, self.final = wide, mid, narrow, final
+        self.send, self.recv = send, recv
+        self.sent = []
+
+    go = Gather.go
+    arrived = Gather.arrived
+    finish = Gather.finish
+
+    def stage_share(self):
+        self.go(0, self.acc, self.wide, self.place.sibling())
+
+    def wait_share(self):
+        self.arrived(0, self.wide)
+        self.sent.pop().wait_send()
+        self.acc[...] = self.acc[...] + self.wide[...]
+
+    def stage_first(self):
+        at = self.place
+        self.go(1, self.acc.at[:, 1 - at.y], self.mid, at.along_y())
+
+    def wait_first(self):
+        at = self.place
+        self.arrived(1, self.mid)
+        half = self.acc.at[:, at.y]
+        half[...] = half[...] + self.mid[...]
+
+    def stage_second(self):
+        at = self.place
+        self.go(2, self.acc.at[:, at.y, 1 - at.x], self.narrow.at[0:4], at.along_x())
+
+    def wait_second(self):
+        at = self.place
+        self.arrived(2, self.narrow.at[0:4])
+        part = self.acc.at[:, at.y, at.x]
+        part[...] = part[...] + self.narrow[0:4]
+
+    def stage_z(self):
+        at = self.place
+        for shift in (1, 2, 3):
+            self.go(2 + shift, self.acc.at[at.other_z(shift), at.y, at.x], self.narrow.at[3 + shift], at.along_z(shift))
+
+    def wait_z(self):
+        at = self.place
+        total = self.acc[at.z, at.y, at.x]
+        for shift in (1, 2, 3):
+            self.arrived(2 + shift, self.narrow.at[3 + shift])
+            total = total + self.narrow[3 + shift]
+        self.final[...] = total
+
+
+def reduce_kernel(
+    gattn_ref, gw1_ref, gw2_ref, gwr_ref, ggate_ref, gsmall_ref, out_ref, gout_ref, sout_ref,
+    acc, wide, mid, narrow, gacc, gwide, gmid, gnarrow, sgrad, swide, smid, snarrow, send, recv, ssend, srecv,
+):
+    place = Place()
+    place.greet()
+    order = [4, 3, 2, 1, 0]
+    grads = [unit_first(gattn_ref), unit_first(gw1_ref), unit_last(gw2_ref), unit_first(gwr_ref), unit_last(ggate_ref)]
+    rounds = {}
+    for r in order:
+        rounds[r] = []
+        for lane in range(2):
+            scratch = (gacc, gwide, gmid, gnarrow) if r == 4 else [ref.at[r] for ref in (acc, wide, mid, narrow)]
+            final = gout_ref if r == 4 else out_ref.at[r]
+            rounds[r].append(
+                Reduce(place, grads[r], lane, *[ref.at[lane] for ref in scratch], final, send.at[r, lane], recv.at[r, lane])
+            )
+    sgrad[...] = gsmall_ref[...]
+    small = ReduceSmall(place, sgrad, swide, smid, snarrow, sout_ref, ssend, srecv)
+
+    def each(r, name):
+        for lane in rounds[r]:
+            getattr(lane, name)()
+
+    stages = ("share", "first", "second", "z", "final")
+    small.stage_share()
+    for tick in range(len(order) + len(stages)):
+        for s in reversed(range(len(stages) + 1)):
+            i = tick - s
+            if 0 <= i < len(order):
+                if s > 0:
+                    each(order[i], "wait_" + stages[s - 1])
+                if s < len(stages):
+                    each(order[i], "stage_" + stages[s])
+        if tick < 4:
+            getattr(small, "wait_" + stages[tick])()
+        if tick < 3:
+            getattr(small, "stage_" + stages[tick + 1])()
+    for r in order:
+        each(r, "finish")
+    small.finish()
+
+
+def call_reduce(gattn, gw1, gw2, gwr, ggate, gsmall):
+    rows, d = gattn.shape[-2:]
+    vmem = pl.BlockSpec(memory_space=pltpu.VMEM)
+
+    def scratch(lead, rows):
+        return [
+            pltpu.VMEM(lead + (4, 2, 2, rows, d), BF16), pltpu.VMEM(lead + (4, 2, 2, rows, d), BF16),
+            pltpu.VMEM(lead + (4, 2, rows, d), BF16), pltpu.VMEM(lead + (7, rows, d), BF16),
+        ]
+
+    return pl.pallas_call(
+        reduce_kernel,
+        out_shape=[
+            jax.ShapeDtypeStruct((4, 4, rows, d), F32), jax.ShapeDtypeStruct((4, rows // 2, d), F32),
+            jax.ShapeDtypeStruct((8, 128), F32),
+        ],
+        in_specs=[vmem] * 6,
+        out_specs=[vmem] * 3,
+        scratch_shapes=scratch((4, 2), rows) + scratch((2,), rows // 2) + [
+            pltpu.VMEM((4, 2, 2, 8, 128), F32), pltpu.VMEM((4, 2, 2, 8, 128), F32), pltpu.VMEM((4, 2, 8, 128), F32),
+            pltpu.VMEM((7, 8, 128), F32),
+            pltpu.SemaphoreType.DMA((5, 2, 7)), pltpu.SemaphoreType.DMA((5, 2, 7)),
+            pltpu.SemaphoreType.DMA((6,)), pltpu.SemaphoreType.DMA((6,)),
+        ],
+        compiler_params=pltpu.CompilerParams(collective_id=1, has_side_effects=True, vmem_limit_bytes=VMEM_LIMIT),
+        name="reduce_grads",
+    )(gattn, gw1, gw2, gwr, ggate, gsmall)
+
+
+def pack_weights(attn_qkv, attn_out, ffn_in, ffn_out, writer_qkv, writer_out):
     rows, d = attn_out.shape
     blocks = ffn_in.shape[1] // d
     return jnp.concatenate(
         [
             attn_qkv, attn_out[None], ffn_in.reshape(rows, blocks, d).transpose(1, 0, 2), ffn_out.reshape(blocks, rows, d),
-            writer_qkv, writer_out[None], gate_weight.reshape(2, rows, d),
+            writer_qkv, writer_out[None],
         ],
         0,
     )
 
 
-def unpack_weights(gathered):
-    n, _, rows, d = gathered.shape
+def own_weights(owned, gate):
+    rows, d = owned.shape[2:]
+    return (
+        owned[0, 0:3], owned[0, 3], owned[1].transpose(1, 0, 2).reshape(rows, 4 * d), owned[2].reshape(4 * rows, d),
+        owned[3, 0:3], owned[3, 3], gate.reshape(2 * rows, d),
+    )
+
+
+def ring_weights(units, gate_weight, ffn_bias, gate_bias, gains):
+    rows, d = units.shape[1:]
+    place = lax.axis_index("dp") % 4
+    lane = jnp.arange(128) // rows == place
+    narrow = jnp.concatenate([gate_bias[None], gains], 0)
+    narrow = jnp.where(lane, jnp.tile(narrow, (1, 128 // rows)), 0)
+    small = jnp.concatenate([ffn_bias[None], narrow, jnp.zeros((3, 128), BF16)], 0).astype(F32)
+    attn, w1, w2, wr, gate, small = call_gather(units, gate_weight.reshape(4, rows // 2, d), small)
+    small = small.reshape(4, 4, 8, 128)
+    b1 = small[:, :, 0, :].reshape(4, 1, d)
+    narrow = small.sum(1).transpose(1, 0, 2).reshape(8, d)
+    return (
+        attn.reshape(4, d, d), w1.reshape(4, d, d), w2.reshape(4, d, d), wr.reshape(4, d, d), gate.reshape(2, d, d),
+        b1, narrow[1:2], narrow[2:5],
+    )
+
+
+def ring_grads(rows, gattn, gw1, gw2, gwr, ggate, gb, ggb, ggains):
+    d = gattn.shape[-1]
+    narrow = jnp.concatenate([ggb[None], ggains], 0).reshape(4, 4, 128).transpose(1, 0, 2)
+    narrow = jnp.repeat(narrow, 4, axis=0)
+    small = jnp.concatenate([gb.reshape(16, 1, 128), narrow, jnp.zeros((16, 3, 128), F32)], 1)
+    first = (4, 4, 2, 2, rows, d)
+    owned, gate, small = call_reduce(
+        gattn.reshape(first), gw1.reshape(first), gw2.reshape(4, 2, 2, 4, rows, d), gwr.reshape(first),
+        ggate.reshape(4, 2, 2, 4, rows // 2, d), small.reshape(4, 2, 2, 8, 128),
+    )
+    place = lax.axis_index("dp") % 4
+    narrow = lax.dynamic_slice(small, (0, place * rows), (8, rows))
+    return own_weights(owned, gate), small[0], narrow[1], narrow[2:5]
+
+
+def plain_weights(units, gate_weight, ffn_bias, gate_bias, gains):
+    _, rows, d = units.shape
+    packed = lax.all_gather(jnp.concatenate([units, gate_weight.reshape(2, rows, d)], 0), "dp", axis=0)
+    n = packed.shape[0]
 
     def by_rows(first, last):
-        return gathered[:, first:last].transpose(1, 0, 2, 3).reshape(last - first, n * rows, d)
-
+        return packed[:, first:last].transpose(1, 0, 2, 3).reshape(last - first, n * rows, d)
+
+    small = jnp.concatenate([ffn_bias.reshape(4, rows), gate_bias[None], gains], 0).astype(F32)
+    small = lax.all_gather(small, "dp", axis=0)
+    b1 = small[:, 0:4].reshape(4, 1, d)
+    small = small.transpose(1, 0, 2).reshape(8, d)
     return (
-        by_rows(0, 4), by_rows(4, 8), gathered[:, 8:12].reshape(4, d, d), by_rows(12, 16), gathered[:, 16:18].reshape(2, d, d),
-    )
-
-
-def pack_grads(n, gattn, gw1, gw2, gwr, ggate):
-    d = gattn.shape[1]
-    rows = d // n
+        by_rows(0, 4), by_rows(4, 8), packed[:, 8:12].reshape(4, d, d), by_rows(12, 16), packed[:, 16:18].reshape(2, d, d),
+        b1, small[4:5], small[5:8],
+    )
+
+
+def plain_grads(rows, gattn, gw1, gw2, gwr, ggate, gb, ggb, ggains):
+    d = gattn.shape[-1]
+    n = d // rows
 
     def by_rows(grad):
         return grad.reshape(-1, n, rows, d).transpose(1, 0, 2, 3)
 
-    return jnp.concatenate(
+    packed = jnp.concatenate(
         [by_rows(gattn), by_rows(gw1), gw2.reshape(n, 4, rows, d), by_rows(gwr), ggate.reshape(n, 2, rows, d)], 1
     )
-
-
-def unpack_owned(owned):
-    _, rows, d = owned.shape
+    owned = lax.psum_scatter(packed.astype(F32), "dp", scatter_dimension=0, tiled=False)
+    owned = lax.psum(owned.astype(BF16), "outer").astype(F32)
+    small = jnp.concatenate(
+        [gb.reshape(n, 4 * rows), ggb.reshape(n, rows), ggains.reshape(3, n, rows).transpose(1, 0, 2).reshape(n, 3 * rows)], 1
+    )
+    small = lax.psum(lax.psum_scatter(small, "dp", scatter_dimension=0, tiled=False), "outer")
     return (
-        owned[0:3], owned[3], owned[4:8].transpose(1, 0, 2).reshape(rows, 4 * d), owned[8:12].reshape(4 * rows, d),
-        owned[12:15], owned[15], owned[16:18].reshape(2 * rows, d),
+        own_weights(owned[0:16].reshape(4, 4, rows, d), owned[16:18]),
+        small[0:4 * rows], small[4 * rows:5 * rows], small[5 * rows:].reshape(3, rows),
     )
 
 
@@ -524,33 +1003,26 @@
     tokens, memory, doc_ids, resets, out_grad, memory_grad,
     attn_qkv, attn_out, ffn_in, ffn_bias, ffn_out, writer_qkv, writer_out, gate_weight, gate_bias, gains,
 ):
-    n = lax.axis_size("dp")
     micro, segs, seg, d = tokens.shape
     slots = memory.shape[2]
     rows = attn_out.shape[0]
-    packed = pack_weights(attn_qkv, attn_out, ffn_in, ffn_out, writer_qkv, writer_out, gate_weight)
-    small = jnp.concatenate([ffn_bias.reshape(4, rows), gate_bias[None], gains], 0).astype(F32)
-    small = lax.all_gather(small, "dp", axis=0)
-    bias_one = small[:, 0:4].reshape(4, 1, d)
-    small = small.transpose(1, 0, 2).reshape(8, d)
-    attn, w1, w2, wr, gate = unpack_weights(lax.all_gather(packed, "dp", axis=0))
+    ring = lax.axis_size("dp") == 16 and lax.axis_size("outer") == 2 and rows == 32
+    units = pack_weights(attn_qkv, attn_out, ffn_in, ffn_out, writer_qkv, writer_out)
+    spread = ring_weights if ring else plain_weights
+    attn, w1, w2, wr, gate, b1, gbias, gain = spread(units, gate_weight, ffn_bias, gate_bias, gains)
     out, new_memory, grad_tokens, grad_memory, gattn, gw1, gw2, gwr, ggate, gb, ggb, ggains = local_layer(
         tokens.reshape(micro * segs, seg, d), memory.reshape(micro * segs, slots, d), doc_ids.reshape(micro * segs, seg),
         resets.reshape(micro * segs), out_grad.reshape(micro * segs, seg, d), memory_grad.reshape(micro * segs, slots, d),
-        attn, w1, w2, wr, gate, bias_one, small[4:5], small[5:8],
-    )
-    owned = lax.psum_scatter(pack_grads(n, gattn, gw1, gw2, gwr, ggate).astype(F32), "dp", scatter_dimension=0, tiled=False)
-    owned = lax.psum(owned.astype(BF16), "outer").astype(F32)
-    small_grads = jnp.concatenate(
-        [gb.reshape(n, 4 * rows), ggb.reshape(n, rows), ggains.reshape(3, n, rows).transpose(1, 0, 2).reshape(n, 3 * rows)], 1
-    )
-    small_owned = lax.psum(lax.psum_scatter(small_grads, "dp", scatter_dimension=0, tiled=False), "outer")
-    gqkv, gout, gin, gffn, gwqkv, gwout, ggw = unpack_owned(owned)
+        attn, w1, w2, wr, gate, b1, gbias, gain,
+    )
+    collect = ring_grads if ring else plain_grads
+    (gqkv, gout, gin, gffn, gwqkv, gwout, ggw), gb, ggb, ggains = collect(
+        rows, gattn, gw1, gw2, gwr, ggate, gb, ggb, ggains
+    )
     return (
         out.reshape(micro, segs, seg, d), new_memory.reshape(micro, segs, slots, d),
         grad_tokens.reshape(micro, segs, seg, d), grad_memory.reshape(micro, segs, slots, d),
-        gqkv, gout, gin, small_owned[0:4 * rows], gffn, gwqkv, gwout, ggw, small_owned[4 * rows:5 * rows],
-        small_owned[5 * rows:].reshape(3, rows),
+        gqkv, gout, gin, gb, gffn, gwqkv, gwout, ggw, ggb, ggains,
     )
 
 

time: 702 us -> 293 us (0.42)
  waiting for transfers between devices: 363 us -> 0 us
  Pallas kernels: 146 us -> 269 us
  blocking collectives: 121 us -> 0 us
  local copies, waits for them, and re-layouts: 40.9 us -> 17.7 us
  between operations: 14 us -> 0.8 us
  other arithmetic: 16.4 us -> 4.94 us
    reduce_scatter x1 -> x0, waiting for transfers between devices: 283 us -> none  [body(): lax.psum_scatter(pack_grads(n, gattn, gw1, gw2, gwr, ggate).astype(F32),...]
    pallas_call x0 -> x2, Pallas kernels: none -> 123 us  [the longest x1 62.4 us: call_reduce(): pl.pallas_call(reduce_kernel, out_shape=[jax.ShapeDtypeStruct((4, 4, rows...]
    all_gather x1 -> x0, waiting for transfers between devices: 79.9 us -> none  [body(): lax.all_gather(packed, 'dp', axis=0)]
    unnamed x1 -> x0, blocking collectives: 75 us -> none
    all_gather x1 -> x0, blocking collectives: 43.3 us -> none  [body(): small = lax.all_gather(small, 'dp', axis=0)]
    convert_element_type x4 -> x1, other arithmetic: 16.3 us -> 1.32 us  [ring_weights(): jnp.concatenate([ffn_bias[None], narrow, jnp.zeros((3, 128), BF16)], 0)]
    transpose x4 -> x0, local copies, waits for them, and re-layouts: 9.88 us -> none  [by_rows(): gathered[:, first:last].transpose(1, 0, 2, 3)]
    unnamed x37 -> x18, local copies, waits for them, and re-layouts: 12.9 us -> 5.86 us
  transfers between devices with their start and end apart: 3 -> 0, of which waited for: 2 -> 0; matrix products, arithmetic and copies ran while one was open for 1% -> 0% of each run, Pallas kernels for 0% -> 0%
where the time goes in v2:
time: 293 us; the launch traced here: 292 us
  Pallas kernels  269 us (92%)
  local copies, waits for them, and re-layouts  17.7 us (6%)
  other arithmetic  4.94 us (2%)
    pallas_call x1, Pallas kernels, call_reduce(): pl.pallas_call(reduce_kernel, out_shape=[jax.ShapeDtypeStruct((4, 4, rows...  62.4 us
    pallas_call x1, Pallas kernels, call_gather(): pl.pallas_call(gather_kernel, out_shape=[jax.ShapeDtypeStruct(shape, kind...  60.3 us
    pallas_call x1, Pallas kernels, call_forward(): pl.pallas_call(forward_kernel, grid=(n,), out_shape=[jax.ShapeDtypeStruct...  53 us
    pallas_call x1, Pallas kernels, call_attn_back(): pl.pallas_call(attn_back_kernel, grid=(n,), out_shape=[jax.ShapeDtypeStru...  40.1 us
    pallas_call x1, Pallas kernels, call_ffn_back(): pl.pallas_call(ffn_back_kernel, grid=(n,), out_shape=[jax.ShapeDtypeStruc...  29.9 us
    pallas_call x1, Pallas kernels, call_writer(): pl.pallas_call(writer_kernel, out_shape=[jax.ShapeDtypeStruct((n, slots,...  23 us
    unnamed x18, local copies, waits for them, and re-layouts  5.86 us

profile of v2, /device:TPU:0, one launch (start us, length us, event | category | flops | bytes accessed | tf_op | source)
XLA Modules:
  0.0 292.0 jit_solution(1661136499119652036)
XLA Ops:
  0.7 0.7 pad_maximum_fusion
  1.4 0.1 tile.10
  1.5 1.3 maximum_convert_fusion.ssrc_ref
  2.9 0.9 constant_dynamic-update-slice_fusion.2
  3.8 0.8 bitcast_dynamic-update-slice_fusion.1
  4.5 0.9 fusion
  5.4 0.9 constant_dynamic-update-slice_fusion.1
  6.4 0.9 constant_dynamic-update-slice_fusion
  7.3 0.8 bitcast_dynamic-update-slice_fusion.src_ref
  8.0 0.8 copy-done
  8.8 60.3 %gather_weights.1 = (bf16[4,4,2,2,32,512]{5,4,3,2,1,0:T(8,128)(2,1)}, bf16[4,4,2,2,32,512]{5,4,3,2,1,0:T(8,128)(2,1)}, bf16[4,2,2,4,32,512]{5,4,3,2,1,0:T(8,128)...) custom-call(bf16[16,32,512]{2,1,0:T(8,128)(2,1)} %copy-done, ...), custom_call_target="tpu_custom_call" | custom-call | tf_op jit(solution)/shard_map/gather_weights/pallas_call | solution.py:699
  69.2 0.8 reduce_sum.9
  70.0 0.6 slice_bitcast_fusion.5.gain_ref
  70.6 1.4 slice_bitcast_fusion.6.b1_ref
  72.1 0.7 convert_bitcast_fusion
  72.7 0.7 broadcast_in_dim.33.keep_ref
  73.4 53.0 %forward_rows.1 = (bf16[4,512,512]{2,1,0:T(8,128)(2,1)}, f32[4,256,512]{2,1,0:T(8,128)}, f32[4,512,512]{2,1,0:T(8,128)}, bf16[4,640,512]{2,1,0:T(8,128)(2,1)}, b...) custom-call(bf16[4,512,512]{2,1,0:T(8,128)(2,1)} %bitcast.80, ...), custom_call_target="tpu_custom_call" | custom-call | tf_op jit(solution)/shard_map/forward_rows/pallas_call | solution.py:141
  126.3 0.6 slice_bitcast_fusion.7.gbias_ref
  126.9 23.0 %writer.1 = (f32[4,64,512]{2,1,0:T(8,128)}, f32[4,256,512]{2,1,0:T(8,128)}, f32[4,64,512]{2,1,0:T(8,128)}, bf16[4,512,512]{2,1,0:T(8,128)(2,1)}, bf16[2,512,512]{2,1,0:T(8,128)(2,1)}, /*index=5*/f32[2,512]{1,0:T(2,128)}) custom-call(f32[4,256,512]{2,1,0:T(8,128)} %get-tuple-element.55.res_ref, f32[4,64,512]{2,1,0:T(8,128)} %bitcast.89, ...), custom_call_target="tpu_custom_call" | custom-call | tf_op jit(solution)/shard_map/writer/pallas_call | solution.py:265
  149.9 29.9 %ffn_back.1 = (f32[4,512,512]{2,1,0:T(8,128)}, bf16[4,512,512]{2,1,0:T(8,128)(2,1)}, bf16[4,512,512]{2,1,0:T(8,128)(2,1)}, f32[4,1,512]{2,1,0:T(1,128)}, f32[1,512]{1,0:T(1,128)}) custom-call(bf16[4,512,512]{2,1,0:T(8,128)(2,1)} %bitcast.96, f32[4,256,512]{2,1,0:T(8,128)} %get-tuple-element.59.dres_ref, f32[4,512,512]{2,1,0:T(8,128)} %get-tuple-element.60.h1_ref, ...), custom_call_target="tpu_custom_call" | custom-call | tf_op jit(solution)/shard_map/ffn_back/pallas_call | solution.py:331
  179.8 40.1 %attn_back.1 = (f32[4,512,512]{2,1,0:T(8,128)}, f32[4,64,512]{2,1,0:T(8,128)}, bf16[4,512,512]{2,1,0:T(8,128)(2,1)}, f32[1,512]{1,0:T(1,128)}) custom-call(f32[4,512,512]{2,1,0:T(8,128)} %get-tuple-element.63.dh_ref, bf16[4,512,512]{2,1,0:T(8,128)(2,1)} %bitcast.81, f32[4,64,512]{2,1,0:T(8,128)} %bitcast.90, f32[4,1,128]{2,1,0:T(1,128)} %broadcast_in_dim.33.keep_ref, ...), custom_call_target="tpu_custom_call" | custom-call | tf_op jit(solution)/shard_map/attn_back/pallas_call | solution.py:438
  219.9 0.7 maximum_bitcast_fusion
  220.7 0.7 maximum_maximum_fusion.gsmall_ref
  221.4 62.4 %reduce_grads.1 = (f32[4,4,32,512]{3,2,1,0:T(8,128)}, f32[4,16,512]{2,1,0:T(8,128)}, f32[8,128]{1,0:T(8,128)}) custom-call(bf16[4,4,2,2,32,512]{5,4,3,2,1,0:T(8,128)(2,1)} %bitcast.94, bf16[4,4,2,2,32,512]{5,4,3,2,1,0:T(8,128)(2,1)} %bitcast.92, bf16[4,2,2,4,32,512]{5,4,3,2,1,0:T(8,128)(2,1)} %bitcast.93, bf16[4,4,2,2,32,512]{5,4,3,2,1,0:T(8,128)(2,1)} %bitcast.91, ...), custom_call_target="tpu_custom_call" | custom-call | tf_op jit(solution)/shard_map/reduce_grads/pallas_call | solution.py:891
  283.8 1.8 fusion.2
  285.6 0.7 copy.54
  286.3 1.8 slice_bitcast_fusion.1
  288.2 0.6 slice.63
  288.8 0.5 slice_bitcast_fusion.8
  289.3 1.5 slice_bitcast_fusion.3
  290.8 0.5 slice_bitcast_fusion.9
  291.3 0.7 copy.62
  (21 shorter events, 0.3 us)
Async XLA Ops:
  8.0 0.8 copy-start
  179.8 40.1 %copy-start.3 = (f32[2,512]{1,0:T(2,128)S(1)}, f32[2,512]{1,0:T(2,128)}, u32[]{:S(2)}) copy-start(f32[2,512]{1,0:T(2,128)} %get-tuple-element.80) | copy-start | bytes 12292
  179.8 40.1 %copy-start.5 = (f32[1,512]{1,0:T(1,128)S(1)}, f32[1,512]{1,0:T(1,128)}, u32[]{:S(2)}) copy-start(f32[1,512]{1,0:T(1,128)} %get-tuple-element.82) | copy-start | bytes 6148
  179.8 40.9 %copy-start.2 = (f32[4,1,512]{2,1,0:T(1,128)S(1)}, f32[4,1,512]{2,1,0:T(1,128)}, u32[]{:S(2)}) copy-start(f32[4,1,512]{2,1,0:T(1,128)} %get-tuple-element.79) | copy-start | bytes 24580
  283.8 4.4 %copy-start.4 = (f32[8,128]{1,0:T(8,128)S(1)}, f32[8,128]{1,0:T(8,128)}, u32[]{:S(2)}) copy-start(f32[8,128]{1,0:T(8,128)} %get-tuple-element.84) | copy-start | bytes 12292
  283.8 7.6 %copy-start.1 = (f32[4,16,512]{2,1,0:T(8,128)S(1)}, f32[4,16,512]{2,1,0:T(8,128)}, u32[]{:S(2)}) copy-start(f32[4,16,512]{2,1,0:T(8,128)} %get-tuple-element.85) | copy-start | bytes 393220

commit v3 on v1

v3 whole, which is shorter than its diff:
```python
import functools

import jax
import jax.numpy as jnp
from jax import lax
from jax.experimental import pallas as pl
from jax.experimental.pallas import tpu as pltpu
from jax.sharding import PartitionSpec as P

HEADS = 8
BLOCK = 128
SPANS = ((0, 256), (0, 384), (128, 512), (256, 640))
STARTS = (0, 256, 640, 1024)
LIVE = 1408
F32 = jnp.float32
BF16 = jnp.bfloat16
VMEM_LIMIT = 60 * 1024 * 1024


def dot(a, b):
    return jnp.dot(a, b, preferred_element_type=F32)


def dot_nt(a, b):
    return lax.dot_general(a, b, (((1,), (1,)), ((), ())), preferred_element_type=F32)


def dot_tn(a, b):
    return lax.dot_general(a, b, (((0,), (0,)), ((), ())), preferred_element_type=F32)


def norm_parts(rows):
    centred = rows - jnp.mean(rows, axis=-1, keepdims=True)
    rstd = lax.rsqrt(jnp.mean(centred * centred, axis=-1, keepdims=True) + 1e-05)
    return centred * rstd, rstd


def norm_back(grad, hat, rstd, gain):
    scaled = grad * gain
    return rstd * (
        scaled
        - jnp.mean(scaled, axis=-1, keepdims=True)
        - hat * jnp.mean(scaled * hat, axis=-1, keepdims=True)
    )


def diagonal_pair(ref, top):
    ref[0:64, 0:128] = top[0:64]
    ref[64:128, 128:256] = top[64:128]


MESH = pl.DeviceIdType.MESH
EVERY = slice(None)


class Place:
    def __init__(self):
        self.dp = lax.axis_index("dp")
        self.core = lax.axis_index("outer")
        self.z, self.y, self.x = self.dp // 4, (self.dp // 2) % 2, self.dp % 2

    def sibling(self):
        return (self.dp, 1 - self.core)

    def along_x(self):
        return (self.dp + 1 - 2 * self.x, self.core)

    def along_y(self):
        return (self.dp + 2 - 4 * self.y, self.core)

    def other_z(self, shift):
        return lax.rem(self.z + shift, 4)

    def along_z(self, shift):
        return (self.dp + 4 * (self.other_z(shift) - self.z), self.core)

    def greet(self):
        barrier = pltpu.get_barrier_semaphore()
        everyone = [self.sibling(), self.along_x(), self.along_y()] + [self.along_z(shift) for shift in (1, 2, 3)]
        for device in everyone:
            pl.semaphore_signal(barrier, inc=1, device_id=device, device_id_type=MESH)
        pl.semaphore_wait(barrier, len(everyone))


class Travel:
    def __init__(self, place, send, recv):
        self.place, self.send, self.recv = place, send, recv

    def copy(self, stage, src, dst, device):
        return pltpu.make_async_remote_copy(
            src_ref=src, dst_ref=dst, send_sem=self.send.at[stage], recv_sem=self.recv.at[stage], device_id=device,
            device_id_type=MESH,
        )

    def go(self, stage, src, dst, device):
        self.copy(stage, src, dst, device).start()

    def arrived(self, stage, dst):
        self.copy(stage, dst, dst, self.place.sibling()).wait_recv()

    def left(self, stage, src):
        self.copy(stage, src, src, self.place.sibling()).wait_send()


class Gather(Travel):
    def __init__(self, place, view, own, lane, send, recv, local):
        super().__init__(place, send, recv)
        self.view, self.own, self.lane, self.local = view, own, lane, local
        self.unit = 2 * place.core + lane

    def mine(self):
        at = self.place
        return self.view(self.unit, at.z, at.y, at.x)

    def stage_z(self):
        at = self.place
        pltpu.make_async_copy(self.own(self.unit), self.mine(), self.local).start()
        for shift in (1, 2, 3):
            self.go(shift - 1, self.own(self.unit), self.mine(), at.along_z(shift))

    def wait_z(self):
        at = self.place
        pltpu.make_async_copy(self.own(self.unit), self.mine(), self.local).wait()
        for shift in (1, 2, 3):
            self.arrived(shift - 1, self.view(self.unit, at.other_z(4 - shift), at.y, at.x))

    def column(self, far):
        at = self.place
        if self.lane:
            return self.view(self.unit, EVERY, 1 - at.y if far else at.y, at.x)
        return self.view(self.unit, EVERY, at.y, 1 - at.x if far else at.x)

    def half(self, unit, far):
        at = self.place
        if self.lane:
            return self.view(unit, EVERY, EVERY, 1 - at.x if far else at.x)
        return self.view(unit, EVERY, 1 - at.y if far else at.y, EVERY)

    def stage_first(self):
        part = self.column(False)
        self.go(3, part, part, self.place.along_y() if self.lane else self.place.along_x())

    def wait_first(self):
        self.arrived(3, self.column(True))

    def stage_second(self):
        part = self.half(self.unit, False)
        self.go(4, part, part, self.place.along_x() if self.lane else self.place.along_y())
        self.go(5, part, part, self.place.sibling())

    def wait_second(self):
        self.arrived(4, self.half(self.unit, True))

    def stage_share(self):
        part = self.half(self.unit, True)
        self.go(6, part, part, self.place.sibling())

    def wait_share(self):
        other = 2 * (1 - self.place.core) + self.lane
        self.arrived(5, self.half(other, False))
        self.arrived(6, self.half(other, True))

    def finish(self):
        for stage in range(3):
            self.left(stage, self.own(self.unit))
        self.left(3, self.column(False))
        self.left(4, self.half(self.unit, False))
        self.left(5, self.half(self.unit, False))
        self.left(6, self.half(self.unit, True))


class GatherSmall(Travel):
    def __init__(self, place, ref, own, send, recv):
        super().__init__(place, send, recv)
        self.ref, self.own = ref, own

    def stage_z(self):
        at = self.place
        self.ref[at.z, at.y, at.x] = self.own[...]
        for shift in (1, 2, 3):
            self.go(shift - 1, self.own, self.ref.at[at.z, at.y, at.x], at.along_z(shift))

    def wait_z(self):
        at = self.place
        for shift in (1, 2, 3):
            self.arrived(shift - 1, self.ref.at[at.other_z(4 - shift), at.y, at.x])

    def stage_first(self):
        at = self.place
        part = self.ref.at[:, at.y, at.x]
        self.go(3, part, part, at.along_x())

    def wait_first(self):
        at = self.place
        self.arrived(3, self.ref.at[:, at.y, 1 - at.x])

    def stage_second(self):
        at = self.place
        part = self.ref.at[:, at.y]
        self.go(4, part, part, at.along_y())

    def wait_second(self):
        at = self.place
        self.arrived(4, self.ref.at[:, 1 - at.y])

    def finish(self):
        at = self.place
        for stage in range(3):
            self.left(stage, self.own)
        self.left(3, self.ref.at[:, at.y, at.x])
        self.left(4, self.ref.at[:, at.y])


def unit_first(ref):
    return lambda u, z, y, x: ref.at[u, z, y, x]


def unit_last(ref):
    return lambda u, z, y, x: ref.at[z, y, x, u]


class Reduce(Travel):
    def __init__(self, place, grad, lane, acc, wide, mid, narrow, final, send, recv, local):
        super().__init__(place, send, recv)
        self.grad, self.lane, self.local = grad, lane, local
        self.acc, self.wide, self.mid, self.narrow, self.final = acc, wide, mid, narrow, final
        self.unit = 2 * place.core + lane
        self.other = 2 * (1 - place.core) + lane

    def whole(self, unit):
        return self.grad(unit, EVERY, EVERY, EVERY)

    def stage_share(self):
        self.go(0, self.whole(self.other), self.wide, self.place.sibling())
        pltpu.make_async_copy(self.whole(self.unit), self.acc, self.local).start()

    def wait_share(self):
        pltpu.make_async_copy(self.whole(self.unit), self.acc, self.local).wait()
        self.arrived(0, self.wide)

        def add(z, carry):
            self.acc[z] = self.acc[z] + self.wide[z]
            return carry

        lax.fori_loop(0, 4, add, 0)

    def half(self, far):
        at = self.place
        if self.lane:
            return self.acc.at[:, :, 1 - at.x if far else at.x]
        return self.acc.at[:, 1 - at.y if far else at.y]

    def stage_first(self):
        at = self.place
        self.go(1, self.half(True), self.mid, at.along_x() if self.lane else at.along_y())

    def wait_first(self):
        at = self.place
        self.arrived(1, self.mid)

        def add(z, carry):
            for i in range(2):
                part = self.acc.at[z, i, at.x] if self.lane else self.acc.at[z, at.y, i]
                part[...] = part[...] + self.mid[z, i]
            return carry

        lax.fori_loop(0, 4, add, 0)

    def quarter(self):
        at = self.place
        if self.lane:
            return self.acc.at[:, 1 - at.y, at.x]
        return self.acc.at[:, at.y, 1 - at.x]

    def stage_second(self):
        self.go(2, self.quarter(), self.narrow.at[0:4], self.place.along_y() if self.lane else self.place.along_x())

    def wait_second(self):
        at = self.place
        self.arrived(2, self.narrow.at[0:4])
        part = self.acc.at[:, at.y, at.x]
        part[...] = part[...] + self.narrow[0:4]

    def block(self, shift):
        at = self.place
        return self.acc.at[at.other_z(shift), at.y, at.x]

    def stage_z(self):
        for shift in (1, 2, 3):
            self.go(2 + shift, self.block(shift), self.narrow.at[3 + shift], self.place.along_z(shift))

    def wait_z(self):
        total = self.block(0)[...].astype(F32)
        for shift in (1, 2, 3):
            self.arrived(2 + shift, self.narrow.at[3 + shift])
            total = total + self.narrow[3 + shift].astype(F32)
        self.final[self.unit] = total

    def stage_final(self):
        self.go(6, self.final.at[self.unit], self.final.at[self.unit], self.place.sibling())

    def wait_final(self):
        self.arrived(6, self.final.at[self.other])
        self.left(0, self.whole(self.other))
        self.left(1, self.half(True))
        self.left(2, self.quarter())
        for shift in (1, 2, 3):
            self.left(2 + shift, self.block(shift))
        self.left(6, self.final.at[self.unit])


class ReduceSmall(Travel):
    def __init__(self, place, own, acc, wide, mid, narrow, final, send, recv):
        super().__init__(place, send, recv)
        self.own, self.acc, self.wide, self.mid, self.narrow, self.final = own, acc, wide, mid, narrow, final

    def stage_share(self):
        self.go(0, self.own, self.wide, self.place.sibling())

    def wait_share(self):
        self.arrived(0, self.wide)
        self.acc[...] = self.own[...] + self.wide[...]

    def stage_first(self):
        at = self.place
        self.go(1, self.acc.at[:, 1 - at.y], self.mid, at.along_y())

    def wait_first(self):
        at = self.place
        self.arrived(1, self.mid)
        half = self.acc.at[:, at.y]
        half[...] = half[...] + self.mid[...]

    def stage_second(self):
        at = self.place
        self.go(2, self.acc.at[:, at.y, 1 - at.x], self.narrow.at[0:4], at.along_x())

    def wait_second(self):
        at = self.place
        self.arrived(2, self.narrow.at[0:4])
        part = self.acc.at[:, at.y, at.x]
        part[...] = part[...] + self.narrow[0:4]

    def block(self, shift):
        at = self.place
        return self.acc.at[at.other_z(shift), at.y, at.x]

    def stage_z(self):
        for shift in (1, 2, 3):
            self.go(2 + shift, self.block(shift), self.narrow.at[3 + shift], self.place.along_z(shift))

    def wait_z(self):
        at = self.place
        total = self.block(0)[...]
        for shift in (1, 2, 3):
            self.arrived(2 + shift, self.narrow.at[3 + shift])
            total = total + self.narrow[3 + shift]
        self.final[...] = total
        self.left(0, self.own)
        self.left(1, self.acc.at[:, 1 - at.y])
        self.left(2, self.acc.at[:, at.y, 1 - at.x])
        for shift in (1, 2, 3):
            self.left(2 + shift, self.block(shift))


def reduce_scratch(rounds, rows, d):
    return [
        pltpu.VMEM((rounds, 2, 4, 2, 2, rows, d), BF16), pltpu.VMEM((rounds, 2, 4, 2, 2, rows, d), BF16),
        pltpu.VMEM((rounds, 2, 4, 2, rows, d), BF16), pltpu.VMEM((rounds, 2, 7, rows, d), BF16),
        pltpu.SemaphoreType.DMA((rounds, 2, 7)), pltpu.SemaphoreType.DMA((rounds, 2, 7)),
        pltpu.SemaphoreType.DMA((rounds, 2)),
    ]


def reduce_round(place, grad, scratch, index, final):
    acc, wide, mid, narrow, send, recv, local = scratch
    return [
        Reduce(
            place, grad, lane, acc.at[index, lane], wide.at[index, lane], mid.at[index, lane], narrow.at[index, lane], final,
            send.at[index, lane], recv.at[index, lane], local.at[index, lane],
        )
        for lane in range(2)
    ]


def both(lanes, *names):
    for name in names:
        for lane in lanes:
            getattr(lane, name)()


def matrix(block):
    return block.reshape(-1, block.shape[-1])


def at_places(beats, step, last):
    def hook(slot):
        for when, where, beat in beats:
            if where == slot:

                @pl.when(step == min(when, last))
                def _(beat=beat):
                    beat()

    return hook


def forward_kernel(ring, count, *refs):
    refs = list(refs)

    def take(number):
        out = refs[:number]
        del refs[:number]
        return out

    tok_ref, mem_ref, doc_ref, keep_ref = take(4)
    if ring:
        shards = take(7)
        narrow_refs = take(3)
    else:
        attn_ref, w1_ref, w2_ref, vec_in_ref, b1_in_ref = take(5)
    n1_ref, qt_ref, k_ref, v_ref, e_ref, linv_ref, ot_ref, h1_ref, out_ref, res_ref, act_ref, slope_ref, vec_ref = take(13)
    if ring:
        attn_ref, w1_ref, w2_ref, wr_ref, gate_ref = take(5)
    bias_ref, pair_ref, vt_ref, hidden_ref, b1_ref, attn_v, w1_v, w2_v, wsem = take(9)
    seg = tok_ref.shape[1]
    slots = mem_ref.shape[1]
    step = pl.program_id(0)
    load_attn = lambda: pltpu.make_async_copy(attn_ref, attn_v, wsem.at[0])
    load_w1 = lambda: pltpu.make_async_copy(w1_ref, w1_v, wsem.at[1])
    load_w2 = lambda: pltpu.make_async_copy(w2_ref, w2_v, wsem.at[2])
    hook = None
    if ring:
        units, psem, sown_ref, sall_ref, send, recv, local, ssend, srecv = take(9)
        place = Place()
        views = [unit_first(attn_ref), unit_first(w1_ref), unit_last(w2_ref), unit_first(wr_ref), unit_last(gate_ref)]
        rounds = []
        for r, view in enumerate(views):
            own = (lambda u: shards[6].at[u]) if r == 4 else (lambda u, r=r: units.at[4 * r + u])
            rounds.append([Gather(place, view, own, l, send.at[r, l], recv.at[r, l], local.at[r, l]) for l in range(2)])
        small = GatherSmall(place, sall_ref, sown_ref, ssend, srecv)
        packs = [(shards[0], units.at[0:3]), (shards[1], units.at[3])]
        packs += [(shards[2].at[:, j * 512:(j + 1) * 512], units.at[4 + j]) for j in range(4)]
        packs += [(shards[3], units.at[8:12]), (shards[4], units.at[12:15]), (shards[5], units.at[15])]

        def pack(i):
            return pltpu.make_async_copy(packs[i][0], packs[i][1], psem.at[i])

        last = len(rounds) - 1

        def advance(r):
            if r > 0:
                both(rounds[r - 1], "wait_second", "stage_share")
            if r <= last:
                both(rounds[r], "wait_first", "stage_second")
            if r + 1 <= last:
                both(rounds[r + 1], "wait_z", "stage_first")
            if r + 2 <= last:
                both(rounds[r + 2], "stage_z")

        def third():
            advance(3)
            both(rounds[1], "wait_share")
            load_w1().start()

        def fourth():
            advance(4)
            both(rounds[2], "wait_share")
            load_w2().start()

        beats = [
            (0, 1, lambda: (both(rounds[1], "wait_first", "stage_second"), both(rounds[2], "wait_z", "stage_first"), both(rounds[3], "stage_z"))),
            (1, 0, lambda: advance(2)), (2, 0, third), (3, 0, fourth), (3, 1, lambda: advance(5)),
        ]
        hook = at_places(beats, step, count - 1)

    @pl.when(step < count)
    def _():
        if ring:

            @pl.when(step == 0)
            def _():
                for i in range(len(packs)):
                    pack(i).start()
                bias, gbias, gains = (ref[...].astype(F32) for ref in narrow_refs)
                narrow = jnp.concatenate([gbias, gains], 0)
                lane = lax.broadcasted_iota(jnp.int32, (4, 128), 1) // narrow.shape[1]
                narrow = jnp.where(lane == lax.rem(place.dp, 4), jnp.concatenate([narrow] * 4, 1), 0.0)
                sown_ref[...] = jnp.concatenate([bias, narrow, jnp.zeros((3, 128), F32)], 0)
                place.greet()
                small.stage_z()
                pack(0).wait()
                pack(1).wait()
                both(rounds[0], "stage_z")
                for i in range(2, len(packs)):
                    pack(i).wait()
        else:

            @pl.when(step == 0)
            def _():
                load_attn().start()
                load_w1().start()
                load_w2().start()
                vec_ref[...] = vec_in_ref[...]
                b1_ref[...] = b1_in_ref[...]
                load_attn().wait()

        keep = keep_ref[0][:, 0:1]
        docs = doc_ref[0].astype(F32)
        key_docs = jnp.broadcast_to(docs, (128, seg)).T
        slot_docs = jnp.broadcast_to(keep - 1.0, (slots, 128))
        key_docs = jnp.concatenate([slot_docs, jnp.full((128 - slots, 128), -1.0, F32), key_docs], 0)
        for block, (first, last_row) in enumerate(SPANS):
            length = last_row - first
            position = lax.broadcasted_iota(jnp.int32, (length, BLOCK), 0) + (first - 128 - block * BLOCK)
            position = position <= lax.broadcasted_iota(jnp.int32, (length, BLOCK), 1)
            same = key_docs[first:last_row] == docs[:, block * BLOCK:(block + 1) * BLOCK]
            bias_ref[STARTS[block]:STARTS[block] + length, :] = jnp.where(same & position, 0.0, -1e30)
        if ring:

            @pl.when(step == 0)
            def _():
                small.wait_z()
                small.stage_first()
                both(rounds[0], "wait_z", "stage_first")
                both(rounds[1], "stage_z")
                small.wait_first()
                small.stage_second()
                both(rounds[0], "wait_first", "stage_second")
                small.wait_second()
                for m in range(4):
                    total = sall_ref[m, 0, 0] + sall_ref[m, 0, 1] + sall_ref[m, 1, 0] + sall_ref[m, 1, 1]
                    vec_ref[:, m * 128:(m + 1) * 128] = jnp.concatenate([total[1:8], total[0:1]], 0)
                    for i in range(4):
                        b1_ref[m, :, i * 128:(i + 1) * 128] = sall_ref[m, i // 2, i % 2, 0:1, :]
                both(rounds[0], "wait_second", "stage_share")
                both(rounds[1], "wait_z", "stage_first")
                both(rounds[2], "stage_z")
                both(rounds[0], "wait_share")
                load_attn().start()
                load_attn().wait()

        x = tok_ref[0].astype(F32)
        gain_one = vec_ref[1:2, :]
        hat, _ = norm_parts(x)
        n1t = (hat * gain_one).astype(BF16)
        hat, _ = norm_parts(mem_ref[0] * keep)
        n1_ref[0, 0:slots, :] = (hat * gain_one).astype(BF16)
        n1_ref[0, slots:128, :] = jnp.zeros((128 - slots, x.shape[1]), BF16)
        n1_ref[0, 128:, :] = n1t
        qt_ref[0] = (dot_nt(matrix(attn_v[0]).T, n1t) * 0.125).astype(BF16)
        n1 = n1_ref[0]
        k_ref[0] = dot(n1, matrix(attn_v[1])).astype(BF16)
        v = dot(n1, matrix(attn_v[2])).astype(BF16)
        v_ref[0] = v
        vt_ref[...] = v.T
        pair_ref[...] = jnp.zeros_like(pair_ref)
        if hook:
            hook(0)

        def one_pair(pair, carry):
            lanes = pl.ds(pl.multiple_of(pair * 128, 128), 128)
            for block, (first, last_row) in enumerate(SPANS):
                start = STARTS[block]
                held = pair_ref.at[block]
                columns = pl.ds(block * BLOCK, BLOCK)
                diagonal_pair(held, qt_ref[0, lanes, columns])
                scores = dot(k_ref[0, first:last_row, lanes], held[...])
                bias = bias_ref[start:start + last_row - first, :]
                scores = scores + jnp.concatenate([bias, bias], 1)
                largest = jnp.max(scores, axis=0, keepdims=True)
                e = jnp.exp(scores - largest)
                linv = 1.0 / jnp.sum(e, axis=0, keepdims=True)
                e = e.astype(BF16)
                e_ref[0, pair, start:start + last_row - first, :] = e
                linv_ref[0, pair, block, :, :] = linv
                mixed = dot(vt_ref[lanes, first:last_row], e) * linv
                ot_ref[0, lanes, columns] = jnp.concatenate(
                    [mixed[0:64, 0:128], mixed[64:128, 128:256]], 0
                ).astype(BF16)
            return carry

        lax.fori_loop(0, 4, one_pair, 0)
        h1 = x + dot(ot_ref[0].T, matrix(attn_v[3]))
        h1_ref[0] = h1
        hidden_ref[step] = h1
        if hook:
            hook(1)

    @pl.when(step >= count)
    def _():
        @pl.when(step == count)
        def _():
            load_w1().wait()
            load_w2().wait()

        h1 = hidden_ref[step - count]
        hat, _ = norm_parts(h1)
        n2 = (hat * vec_ref[2:3, :]).astype(BF16)
        result = h1
        for part in range(4):
            before = dot(n2, matrix(w1_v[part])) + b1_ref[part]
            cdf = 0.5 + 0.5 * lax.erf(before * 0.7071067811865476)
            active = (before * cdf).astype(BF16)
            act_ref[0, part] = active
            slope = cdf + before * jnp.exp(before * before * -0.5) * 0.3989422804014327
            slope_ref[0, part] = slope.astype(BF16)
            result = result + dot(active, matrix(w2_v[part]))
        out_ref[0] = result.astype(BF16)
        res_ref[0] = result[seg // 2:]
        if ring:

            @pl.when(step == 2 * count - 1)
            def _():
                both(rounds[3], "wait_share")
                both(rounds[4], "wait_share")
                for lanes in rounds:
                    both(lanes, "finish")
                small.finish()


ANY = pl.BlockSpec(memory_space=pl.ANY)


def full_spec(shape):
    return pl.BlockSpec(shape, lambda i: (0,) * len(shape), pipeline_mode=pl.Buffered(1))


def phase_spec(shape, first, count):
    return pl.BlockSpec((1,) + shape, lambda i: (jnp.clip(i - first, 0, count - 1),) + (0,) * len(shape))


def call_forward(ring, tokens, memory, docs, keep, weights):
    n, seg, d = tokens.shape
    slots = memory.shape[1]
    early = [
        ((seg + 128, d), BF16), ((d, seg), BF16), ((seg + 128, d), BF16), ((seg + 128, d), BF16), ((4, LIVE, 256), BF16),
        ((4, 4, 1, 256), F32), ((d, seg), BF16), ((seg, d), F32),
    ]
    late = [((seg, d), BF16), ((seg // 2, d), F32), ((4, seg, 512), BF16), ((4, seg, 512), BF16)]
    units = (4, 4, 2, 2, 32, d)
    unit_shapes = [units, units, (4, 2, 2, 4, 32, d), units, (4, 2, 2, 4, 16, d)]
    out_shape = [jax.ShapeDtypeStruct((n,) + shape, kind) for shape, kind in early + late]
    out_shape += [jax.ShapeDtypeStruct((8, d), F32)]
    out_specs = [phase_spec(shape, 0, n) for shape, _ in early] + [phase_spec(shape, n, n) for shape, _ in late]
    out_specs += [full_spec((8, d))]
    in_specs = [phase_spec((seg, d), 0, n), phase_spec((slots, d), 0, n), phase_spec((1, seg), 0, n), phase_spec((1, 128), 0, n)]
    scratch = [
        pltpu.VMEM((LIVE, 128), F32), pltpu.VMEM((4, 128, 256), BF16), pltpu.VMEM((d, seg + 128), BF16),
        pltpu.VMEM((n, seg, d), F32), pltpu.VMEM((4, 1, d), F32), pltpu.VMEM(unit_shapes[0], BF16),
        pltpu.VMEM(unit_shapes[1], BF16), pltpu.VMEM(unit_shapes[2], BF16), pltpu.SemaphoreType.DMA((3,)),
    ]
    params = dict(vmem_limit_bytes=VMEM_LIMIT)
    if ring:
        in_specs += [ANY] * 7 + [full_spec(array.shape) for array in weights[7:]]
        out_shape += [jax.ShapeDtypeStruct(shape, BF16) for shape in unit_shapes]
        out_specs += [ANY] * 5
        scratch += [
            pltpu.VMEM((16, 32, d), BF16), pltpu.SemaphoreType.DMA((9,)), pltpu.VMEM((8, 128), F32),
            pltpu.VMEM((4, 2, 2, 8, 128), F32), pltpu.SemaphoreType.DMA((5, 2, 7)), pltpu.SemaphoreType.DMA((5, 2, 7)),
            pltpu.SemaphoreType.DMA((5, 2)), pltpu.SemaphoreType.DMA((5,)), pltpu.SemaphoreType.DMA((5,)),
        ]
        params.update(collective_id=0, has_side_effects=True)
    else:
        in_specs += [ANY] * 3 + [full_spec((8, d)), full_spec((4, 1, d))]
    return pl.pallas_call(
        functools.partial(forward_kernel, ring, n),
        grid=(2 * n,),
        out_shape=out_shape,
        in_specs=in_specs,
        out_specs=out_specs,
        scratch_shapes=scratch,
        compiler_params=pltpu.CompilerParams(**params),
        name="gather_forward" if ring else "forward_rows",
    )(tokens, memory, docs, keep, *weights)


def writer_all(
    res_ref, mem_ref, memgrad_ref, doc_ref, keep_ref, wr_ref, gate_ref, vec_ref,
    newmem_ref, dres_ref, dkept_ref, gwr_ref, ggate_ref, gvec_ref,
    n3_ref, ns_ref, kept_ref, sq_ref, tk_ref, tv_ref, p_ref, wt_ref, dsq_ref, dtk_ref, dtv_ref, dlog_ref, dw_ref,
):
    n, half, d = res_ref.shape
    slots = mem_ref.shape[1]
    gain = vec_ref[3:4, :]

    def norm(i, carry):
        rows = pl.ds(pl.multiple_of(i * half, half), half)
        small = pl.ds(pl.multiple_of(i * slots, slots), slots)
        hat, _ = norm_parts(res_ref[i])
        n3_ref[rows, :] = (hat * gain).astype(BF16)
        kept = mem_ref[i] * keep_ref[i][:, 0:1]
        kept_ref[small, :] = kept
        hat, _ = norm_parts(kept)
        ns_ref[small, :] = (hat * gain).astype(BF16)
        tk_ref[rows, :] = dot(n3_ref[rows, :], wr_ref[1]).astype(BF16)
        tv_ref[rows, :] = dot(n3_ref[rows, :], wr_ref[2]).astype(BF16)
        return carry

    lax.fori_loop(0, n, norm, 0)
    sq_ref[...] = (dot(ns_ref[...], wr_ref[0]) * 0.125).astype(BF16)
    low_half = lax.broadcasted_iota(jnp.int32, (1, 128), 1) < 64

    def halves(rows):
        zero = jnp.zeros_like(rows)
        return jnp.concatenate([jnp.where(low_half, rows, zero), jnp.where(low_half, zero, rows)], 0)

    def read(i, carry):
        rows = pl.ds(pl.multiple_of(i * half, half), half)
        small = pl.ds(pl.multiple_of(i * slots, slots), slots)
        docs = doc_ref[i].astype(F32)
        bias = jnp.where(docs == jnp.max(docs), 0.0, -1e30)[:, docs.shape[1] - half:]
        for pair in range(4):
            lanes = slice(pair * 128, pair * 128 + 128)
            scores = dot_nt(halves(sq_ref[small, lanes]), tk_ref[rows, lanes]) + bias
            e = jnp.exp(scores - jnp.max(scores, axis=1, keepdims=True))
            p = e * (1.0 / jnp.sum(e, axis=1, keepdims=True))
            p_ref[i, pair] = p
            mixed = dot(p.astype(BF16), tv_ref[rows, lanes])
            wt_ref[small, lanes] = jnp.where(low_half, mixed[:slots], mixed[slots:]).astype(BF16)
        return carry

    lax.fori_loop(0, n, read, 0)

    def put(ref, index, value):
        ref[index] = value.astype(BF16).reshape(ref.shape[1:])

    write = dot(wt_ref[...], wr_ref[3])
    kept = kept_ref[...]
    write_low = write.astype(BF16)
    kept_low = kept.astype(BF16)
    logit = dot(kept_low, gate_ref[0]) + dot(write_low, gate_ref[1]) + vec_ref[0:1, :]
    gate = jax.nn.sigmoid(logit)
    new = gate * kept + (1.0 - gate) * write
    memgrad = memgrad_ref[...].reshape(n * slots, d)
    newmem_ref[...] = new.reshape(n, slots, d)
    dlogit = memgrad * (kept - write) * gate * (1.0 - gate)
    dlog_ref[...] = dlogit.astype(BF16)
    dlow = dlog_ref[...]
    gvec_ref[0:1, :] = jnp.sum(dlow.astype(F32), axis=0, keepdims=True)
    ggate_ref[0:2] = dot_tn(kept_low, dlow).astype(BF16).reshape((2,) + ggate_ref.shape[1:])
    ggate_ref[2:4] = dot_tn(write_low, dlow).astype(BF16).reshape((2,) + ggate_ref.shape[1:])
    dkept = memgrad * gate + dot_nt(dlow, gate_ref[0])
    dwrite = memgrad * (1.0 - gate) + dot_nt(dlow, gate_ref[1])
    dkept_ref[...] = dkept.reshape(n, slots, d)
    dw_low = dwrite.astype(BF16)
    put(gwr_ref, 3, dot_tn(wt_ref[...], dw_low))
    dw_ref[...] = dot_nt(dw_low, wr_ref[3]).astype(BF16)

    def read_back(i, carry):
        rows = pl.ds(pl.multiple_of(i * half, half), half)
        small = pl.ds(pl.multiple_of(i * slots, slots), slots)
        for pair in range(4):
            lanes = slice(pair * 128, pair * 128 + 128)
            p = p_ref[i, pair]
            grads = halves(dw_ref[small, lanes])
            dp = dot_nt(grads, tv_ref[rows, lanes])
            ds = (p * (dp - jnp.sum(dp * p, axis=1, keepdims=True))).astype(BF16)
            dq = dot(ds, tk_ref[rows, lanes]) * 0.125
            dsq_ref[small, lanes] = jnp.where(low_half, dq[:slots], dq[slots:]).astype(BF16)
            dtk_ref[rows, lanes] = dot_tn(ds, halves(sq_ref[small, lanes])).astype(BF16)
            dtv_ref[rows, lanes] = dot_tn(p.astype(BF16), grads).astype(BF16)
        return carry

    lax.fori_loop(0, n, read_back, 0)
    put(gwr_ref, 0, dot_tn(ns_ref[...], dsq_ref[...]))
    put(gwr_ref, 1, dot_tn(n3_ref[...], dtk_ref[...]))
    put(gwr_ref, 2, dot_tn(n3_ref[...], dtv_ref[...]))
    grad = dot_nt(dsq_ref[...], wr_ref[0])
    hat, rstd = norm_parts(kept_ref[...])
    dkept_ref[...] += norm_back(grad, hat, rstd, gain).reshape(n, slots, d)
    ggain = jnp.sum(grad * hat, axis=0, keepdims=True)

    def back(i, ggain):
        rows = pl.ds(pl.multiple_of(i * half, half), half)
        grad = dot_nt(dtk_ref[rows, :], wr_ref[1]) + dot_nt(dtv_ref[rows, :], wr_ref[2])
        hat, rstd = norm_parts(res_ref[i])
        dres_ref[i] = norm_back(grad, hat, rstd, gain)
        return ggain + jnp.sum(grad * hat, axis=0, keepdims=True)

    gvec_ref[3:4, :] = lax.fori_loop(0, n, back, ggain)


def ffn_back_kernel(ring, count, *refs):
    refs = list(refs)

    def take(number):
        out = refs[:number]
        del refs[:number]
        return out

    writer_in = take(8)
    vec_ref = writer_in[7]
    og_ref, h1_ref, act_ref, slope_ref, w1_ref, w2_ref = take(6)
    newmem_ref, dkept_ref, gvec_ref, gb_ref, gw1_ref, gw2_ref, dh_ref, gwr_out, ggate_out = take(9)
    writer_scratch = take(13)
    dres_ref, acc1_ref, acc2_ref, w1_v, w2_v, wsem = take(6)
    step = pl.program_id(0)
    seg = og_ref.shape[1]
    load_w1 = lambda: pltpu.make_async_copy(w1_ref, w1_v, wsem.at[0])
    load_w2 = lambda: pltpu.make_async_copy(w2_ref, w2_v, wsem.at[1])
    hook = None
    if ring:
        gwr_ref, ggate_ref, fwr_ref, fgate_ref = take(4)
        wide_scratch, slim_scratch = take(7), take(7)
        place = Place()
        writer_round = reduce_round(place, unit_first(gwr_ref), wide_scratch, 0, fwr_ref)
        gate_round = reduce_round(place, unit_last(ggate_ref), slim_scratch, 0, fgate_ref)

        def hand_back():
            both(writer_round, "wait_final")
            both(gate_round, "wait_final")
            gwr_out[...] = fwr_ref[...]
            ggate_out[...] = fgate_ref[...]

        beats = [
            (0, 0, lambda: both(writer_round, "wait_share", "stage_first")),
            (0, 1, lambda: both(gate_round, "wait_share", "stage_first")),
            (1, 0, lambda: (both(writer_round, "wait_first", "stage_second"), both(gate_round, "wait_first", "stage_second"))),
            (1, 1, lambda: both(writer_round, "wait_second", "stage_z")),
            (2, 0, lambda: both(gate_round, "wait_second", "stage_z")),
            (2, 1, lambda: both(writer_round, "wait_z", "stage_final")),
            (3, 0, lambda: both(gate_round, "wait_z", "stage_final")),
            (3, 1, hand_back),
        ]
        hook = at_places(beats, step - 1, count - 1)
    else:
        gwr_ref, ggate_ref = gwr_out, ggate_out

    @pl.when(step == 0)
    def _():
        load_w1().start()
        load_w2().start()
        if ring:
            place.greet()
        acc1_ref[...] = jnp.zeros_like(acc1_ref)
        acc2_ref[...] = jnp.zeros_like(acc2_ref)
        gb_ref[...] = jnp.zeros_like(gb_ref)
        gvec_ref[...] = jnp.zeros_like(gvec_ref)
        writer_all(*writer_in, newmem_ref, dres_ref, dkept_ref, gwr_ref, ggate_ref, gvec_ref, *writer_scratch)
        if ring:
            both(writer_round, "stage_share")
            both(gate_round, "stage_share")
        load_w1().wait()
        load_w2().wait()

    @pl.when(step > 0)
    def _():
        if hook:
            hook(0)
        top = og_ref[0, 0:seg // 2, :].astype(F32)
        bottom = og_ref[0, seg // 2:, :].astype(F32) + dres_ref[step - 1]
        dresult = jnp.concatenate([top, bottom], 0)
        low = dresult.astype(BF16)
        h1 = h1_ref[0]
        hat, rstd = norm_parts(h1)
        gain = vec_ref[2:3, :]
        n2t = (hat * gain).astype(BF16).T
        lowt = low.T
        grad = jnp.zeros_like(dresult)
        for part in range(4):
            acc2_ref[part] += dot(lowt, act_ref[0, part])
            dbefore = (dot_nt(low, w2_v[part]) * slope_ref[0, part].astype(F32)).astype(BF16)
            gb_ref[part] += jnp.sum(dbefore.astype(F32), axis=0, keepdims=True)
            acc1_ref[part] += dot(n2t, dbefore)
            grad = grad + dot_nt(dbefore, w1_v[part])
            if part == 1 and hook:
                hook(1)
        gvec_ref[2:3, :] += jnp.sum(grad * hat, axis=0, keepdims=True)
        dh_ref[0] = dresult + norm_back(grad, hat, rstd, gain)

        @pl.when(step == count)
        def _():
            gw1_ref[...] = acc1_ref[...].astype(BF16)
            for part in range(4):
                gw2_ref[part] = acc2_ref[part].T.astype(BF16)


def call_ffn_back(ring, res, memory, memory_grad, docs, keep, wr, gate, vec, out_grad, h1, act, slope, w1, w2):
    n, half, d = res.shape
    seg = 2 * half
    slots = memory.shape[1]
    rows, small = n * half, n * slots
    writer_args = (res, memory, memory_grad, docs, keep, wr, gate, vec)
    units = (4, 4, 2, 2, 32, d)
    gate_units = (4, 2, 2, 4, 16, d)
    if ring:
        grads = [((4, 32, d), F32), ((4, 16, d), F32)]
    else:
        grads = [(units, BF16), (gate_units, BF16)]
    whole = [
        ((n, slots, d), F32), ((n, slots, d), F32), ((8, d), F32), ((4, 1, d), F32), ((4, d, d), BF16), ((4, d, d), BF16),
    ]
    scratch = [
        pltpu.VMEM((rows, d), BF16), pltpu.VMEM((small, d), BF16), pltpu.VMEM((small, d), F32), pltpu.VMEM((small, d), BF16),
        pltpu.VMEM((rows, d), BF16), pltpu.VMEM((rows, d), BF16), pltpu.VMEM((n, 4, 2 * slots, half), F32),
        pltpu.VMEM((small, d), BF16), pltpu.VMEM((small, d), BF16), pltpu.VMEM((rows, d), BF16),
        pltpu.VMEM((rows, d), BF16), pltpu.VMEM((small, d), BF16), pltpu.VMEM((small, d), BF16),
        pltpu.VMEM((n, half, d), F32), pltpu.VMEM((4, d, d), F32), pltpu.VMEM((4, d, d), F32),
        pltpu.VMEM((4, d, d), BF16), pltpu.VMEM((4, d, d), BF16), pltpu.SemaphoreType.DMA((2,)),
    ]
    params = dict(vmem_limit_bytes=VMEM_LIMIT)
    if ring:
        scratch += [pltpu.VMEM(units, BF16), pltpu.VMEM(gate_units, BF16)]
        scratch += [pltpu.VMEM((4, 32, d), F32), pltpu.VMEM((4, 16, d), F32)]
        scratch += reduce_scratch(1, 32, d) + reduce_scratch(1, 16, d)
        params.update(collective_id=1, has_side_effects=True)
    return pl.pallas_call(
        functools.partial(ffn_back_kernel, ring, n),
        grid=(n + 1,),
        out_shape=[jax.ShapeDtypeStruct(shape, kind) for shape, kind in whole]
        + [jax.ShapeDtypeStruct((n, seg, d), F32)] + [jax.ShapeDtypeStruct(shape, kind) for shape, kind in grads],
        in_specs=[full_spec(array.shape) for array in writer_args] + [
            phase_spec((seg, d), 1, n), phase_spec((seg, d), 1, n), phase_spec((4, seg, 512), 1, n),
            phase_spec((4, seg, 512), 1, n), ANY, ANY,
        ],
        out_specs=[full_spec(shape) for shape, _ in whole] + [phase_spec((seg, d), 1, n)]
        + [full_spec(shape) for shape, _ in grads],
        scratch_shapes=scratch,
        compiler_params=pltpu.CompilerParams(**params),
        name="ffn_back",
    )(*writer_args, out_grad, h1, act, slope, w1, w2)


def attn_back_kernel(ring, count, *refs):
    refs = list(refs)

    def take(number):
        out = refs[:number]
        del refs[:number]
        return out

    n1_ref, qt_ref, k_ref, v_ref, e_ref, linv_ref, ot_ref = take(7)
    tok_ref, mem_ref, keep_ref, dkept_ref, dh_ref = take(5)
    attn_ref, vec_ref, gvec_in_ref = take(3)
    if ring:
        gb_ref, gw1_ref, gw2_ref = take(3)
    gtok_ref, gmem_ref = take(2)
    if ring:
        fattn_ref, fw1_ref, fw2_ref, fsmall_ref = take(4)
    else:
        gattn_ref, gvec_ref = take(2)
    dot_ref, kt_ref, dqt_ref, dk_ref, dv_ref, dkl_ref, dvl_ref, qp_ref, dp_ref, acc_ref, accg_ref = take(11)
    step = pl.program_id(0)
    seg = tok_ref.shape[1]
    slots = mem_ref.shape[1]
    hook = late_hook = None
    if ring:
        gattn_ref, final_ref = take(2)
        scratch = take(7)
        sown, sacc, swide, smid, snarrow, ssend, srecv = take(7)
        place = Place()
        attn_round = reduce_round(place, unit_first(gattn_ref), scratch, 0, final_ref.at[0])
        w1_round = reduce_round(place, unit_first(gw1_ref), scratch, 1, final_ref.at[1])
        w2_round = reduce_round(place, unit_last(gw2_ref), scratch, 2, final_ref.at[2])
        small = ReduceSmall(place, sown, sacc, swide, smid, snarrow, fsmall_ref, ssend, srecv)
        beats = [
            (0, 0, lambda: both(w2_round, "wait_share", "stage_first")),
            (0, 1, lambda: (both(w2_round, "wait_first", "stage_second"), both(w1_round, "wait_share", "stage_first"))),
            (1, 1, lambda: (both(w2_round, "wait_second", "stage_z"), both(w1_round, "wait_first", "stage_second"))),
            (2, 1, lambda: (both(w2_round, "wait_z", "stage_final"), both(w1_round, "wait_second", "stage_z"))),
            (3, 0, lambda: both(w1_round, "wait_z", "stage_final")),
            (3, 1, lambda: (both(w2_round, "wait_final"), both(w1_round, "wait_final"))),
        ]
        hook = at_places(beats, step, count - 1)
        late_beats = [
            (0, 0, lambda: both(attn_round, "wait_share", "stage_first")),
            (2, 0, lambda: both(attn_round, "wait_first", "stage_second")),
            (3, 0, lambda: both(attn_round, "wait_second", "stage_z")),
        ]
        late_hook = at_places(late_beats, step - count, count - 1)

    @pl.when(step < count)
    def _():
        @pl.when(step == 0)
        def _():
            if ring:
                place.greet()
                both(w2_round, "stage_share")
                both(w1_round, "stage_share")
            acc_ref[...] = jnp.zeros_like(acc_ref)
            accg_ref[...] = jnp.zeros_like(accg_ref)

        low = dh_ref[0].astype(BF16)
        acc_ref[3] += dot(ot_ref[0], low)
        dot_ref[...] = dot_nt(attn_ref[3], low)
        kt_ref[...] = k_ref[0].T
        qp_ref[...] = jnp.zeros_like(qp_ref)
        dp_ref[...] = jnp.zeros_like(dp_ref)
        if hook:
            hook(0)

        def one_pair(pair, carry):
            lanes = pl.ds(pl.multiple_of(pair * 128, 128), 128)
            dk_ref[:, lanes] = jnp.zeros((seg + 128, 128), F32)
            dv_ref[:, lanes] = jnp.zeros((seg + 128, 128), F32)
            for block, (first, last) in enumerate(SPANS):
                start = STARTS[block]
                columns = pl.ds(block * BLOCK, BLOCK)
                linv = linv_ref[0, pair, block, :, :]
                mixed_grad = dot_ref[lanes, columns]
                top = (mixed_grad[0:64] * linv[:, 0:128]).astype(BF16)
                bottom = (mixed_grad[64:128] * linv[:, 128:256]).astype(BF16)
                mixed = ot_ref[0, lanes, columns].astype(F32)
                delta = jnp.concatenate(
                    [
                        jnp.sum(top.astype(F32) * mixed[0:64], axis=0, keepdims=True),
                        jnp.sum(bottom.astype(F32) * mixed[64:128], axis=0, keepdims=True),
                    ],
                    1,
                )
                held = dp_ref.at[block]
                held[0:64, 0:128] = top
                held[64:128, 128:256] = bottom
                query = qp_ref.at[block]
                diagonal_pair(query, qt_ref[0, lanes, columns])
                e = e_ref[0, pair, start:start + last - first, :]
                dp = dot(v_ref[0, first:last, lanes], held[...])
                ds = (e.astype(F32) * (dp - delta)).astype(BF16)
                dv_ref[first:last, lanes] += dot_nt(e, held[...])
                dk_ref[first:last, lanes] += dot_nt(ds, query[...])
                dq = dot(kt_ref[lanes, first:last], ds) * 0.125
                dqt_ref[step, lanes, columns] = jnp.concatenate([dq[0:64, 0:128], dq[64:128, 128:256]], 0).astype(BF16)
            return carry

        lax.fori_loop(0, 4, one_pair, 0)
        n1t = n1_ref[0].T
        dk = dk_ref[...].astype(BF16)
        dv = dv_ref[...].astype(BF16)
        dkl_ref[step] = dk
        dvl_ref[step] = dv
        acc_ref[0] += dot_nt(n1t[:, 128:], dqt_ref[step])
        acc_ref[1] += dot(n1t, dk)
        acc_ref[2] += dot(n1t, dv)
        if hook:
            hook(1)

        @pl.when(step == count - 1)
        def _():
            gattn_ref[...] = acc_ref[...].astype(BF16).reshape(gattn_ref.shape)
            if ring:
                both(attn_round, "stage_share")

    @pl.when(step >= count)
    def _():
        here = step - count
        gain = vec_ref[1:2, :]
        dk = dkl_ref[here]
        dv = dvl_ref[here]
        grad = dot_nt(dk, attn_ref[1]) + dot_nt(dv, attn_ref[2])
        slot_grad = grad[0:slots]
        kept = mem_ref[0] * keep_ref[0][:, 0:1]
        hat, rstd = norm_parts(kept)
        ggain = jnp.sum(slot_grad * hat, axis=0, keepdims=True)
        gmem_ref[0] = (dkept_ref[0] + norm_back(slot_grad, hat, rstd, gain)) * keep_ref[0][:, 0:1]
        grad = grad[128:] + dot_nt(dqt_ref[here].T, attn_ref[0])
        hat, rstd = norm_parts(tok_ref[0].astype(F32))
        accg_ref[...] += ggain + jnp.sum(grad * hat, axis=0, keepdims=True)
        gtok_ref[0] = dh_ref[0] + norm_back(grad, hat, rstd, gain)
        if late_hook:
            late_hook(0)

        @pl.when(step == 2 * count - 1)
        def _():
            if not ring:
                gvec_ref[...] = gvec_in_ref[...]
                gvec_ref[1:2, :] = accg_ref[...]
                return
            vector = gvec_in_ref[...]
            vector = jnp.concatenate([vector[0:1], accg_ref[...], vector[2:4], jnp.zeros((3, vector.shape[1]), F32)], 0)
            for m in range(4):
                for i in range(4):
                    sown[m, i // 2, i % 2] = jnp.concatenate(
                        [gb_ref[m, :, i * 128:(i + 1) * 128], vector[:, m * 128:(m + 1) * 128]], 0
                    )
            small.stage_share()
            small.wait_share()
            small.stage_first()
            both(attn_round, "wait_z", "stage_final")
            small.wait_first()
            small.stage_second()
            small.wait_second()
            small.stage_z()
            both(attn_round, "wait_final")
            fattn_ref[...] = final_ref[0]
            fw1_ref[...] = final_ref[1]
            fw2_ref[...] = final_ref[2]
            small.wait_z()


def call_attn_back(ring, dh, tokens, memory, keep, n1, qt, k, v, e, linv, ot, dkept, attn, vec, gvec, extra):
    n, seg, d = tokens.shape
    slots = memory.shape[1]
    shapes = [((n, seg, d), F32), ((n, slots, d), F32)]
    out_specs = [phase_spec((seg, d), n, n), phase_spec((slots, d), n, n)]
    in_specs = [
        phase_spec((seg + 128, d), 0, n), phase_spec((d, seg), 0, n), phase_spec((seg + 128, d), 0, n),
        phase_spec((seg + 128, d), 0, n), phase_spec((4, LIVE, 256), 0, n), phase_spec((4, 4, 1, 256), 0, n),
        phase_spec((d, seg), 0, n), phase_spec((seg, d), n, n), phase_spec((slots, d), n, n), phase_spec((1, 128), n, n),
        phase_spec((slots, d), n, n), pl.BlockSpec((1, seg, d), lambda i: (lax.rem(i, n), 0, 0)),
        full_spec(attn.shape), full_spec(vec.shape), full_spec(gvec.shape),
    ]
    units = (4, 4, 2, 2, 32, d)
    scratch = [
        pltpu.VMEM((d, seg), F32), pltpu.VMEM((d, seg + 128), BF16), pltpu.VMEM((n, d, seg), BF16),
        pltpu.VMEM((seg + 128, d), F32), pltpu.VMEM((seg + 128, d), F32), pltpu.VMEM((n, seg + 128, d), BF16),
        pltpu.VMEM((n, seg + 128, d), BF16), pltpu.VMEM((4, 128, 256), BF16), pltpu.VMEM((4, 128, 256), BF16),
        pltpu.VMEM((4, d, d), F32), pltpu.VMEM((1, d), F32),
    ]
    params = dict(vmem_limit_bytes=VMEM_LIMIT)
    if ring:
        in_specs += [full_spec(extra[0].shape), ANY, ANY]
        more = [((4, 32, d), F32)] * 3 + [((8, 128), F32)]
        scratch += [pltpu.VMEM(units, BF16), pltpu.VMEM((3, 4, 32, d), F32)] + reduce_scratch(3, 32, d)
        scratch += [pltpu.VMEM((4, 2, 2, 8, 128), F32)] * 3 + [
            pltpu.VMEM((4, 2, 8, 128), F32), pltpu.VMEM((7, 8, 128), F32),
            pltpu.SemaphoreType.DMA((6,)), pltpu.SemaphoreType.DMA((6,)),
        ]
        params.update(collective_id=2, has_side_effects=True)
    else:
        more = [(units, BF16), ((8, d), F32)]
    return pl.pallas_call(
        functools.partial(attn_back_kernel, ring, n),
        grid=(2 * n,),
        out_shape=[jax.ShapeDtypeStruct(shape, kind) for shape, kind in shapes + more],
        in_specs=in_specs,
        out_specs=out_specs + [full_spec(shape) for shape, _ in more],
        scratch_shapes=scratch,
        compiler_params=pltpu.CompilerParams(**params),
        name="attn_back",
    )(n1, qt, k, v, e, linv, ot, tokens, memory, keep, dkept, dh, attn, vec, gvec, *extra)


def hand_out_kernel(
    fattn_ref, fw1_ref, fw2_ref, fwr_ref, fgate_ref, small_ref,
    gqkv_ref, gout_ref, gin_ref, gffn_ref, gwqkv_ref, gwout_ref, ggate_ref, gb_ref, ggb_ref, ggain_ref,
):
    gqkv_ref[...] = fattn_ref[0:3]
    gout_ref[...] = fattn_ref[3]
    for j in range(4):
        gin_ref[:, j * 512:(j + 1) * 512] = fw1_ref[j]
    gffn_ref[...] = fw2_ref[...]
    gwqkv_ref[...] = fwr_ref[0:3]
    gwout_ref[...] = fwr_ref[3]
    ggate_ref[...] = fgate_ref[...]
    gb_ref[...] = small_ref[0:1, :]
    rows = ggb_ref.shape[1]
    place = lax.rem(lax.axis_index("dp"), 4)
    narrow = jnp.zeros((4, rows), F32)
    for i in range(4):
        narrow = narrow + small_ref[1:5, i * rows:(i + 1) * rows] * (place == i).astype(F32)
    ggb_ref[...] = narrow[0:1]
    ggain_ref[...] = narrow[1:4]


def call_hand_out(*args):
    rows, d = args[0].shape[1:]
    vmem = pl.BlockSpec(memory_space=pltpu.VMEM)
    shapes = [
        (3, rows, d), (rows, d), (rows, 4 * d), (4, rows, d), (3, rows, d), (rows, d), (4, rows // 2, d), (1, 128), (1, rows),
        (3, rows),
    ]
    return pl.pallas_call(
        hand_out_kernel,
        out_shape=[jax.ShapeDtypeStruct(shape, F32) for shape in shapes],
        in_specs=[vmem] * 6,
        out_specs=[vmem] * 10,
        name="hand_out",
    )(*args)


def plain_weights(attn_qkv, attn_out, ffn_in, ffn_out, writer_qkv, writer_out, gate_weight, ffn_bias, gate_bias, gains):
    rows, d = attn_out.shape
    packed = jnp.concatenate(
        [
            attn_qkv, attn_out[None], ffn_in.reshape(rows, 4, d).transpose(1, 0, 2), ffn_out.reshape(4, rows, d),
            writer_qkv, writer_out[None], gate_weight.reshape(2, rows, d),
        ],
        0,
    )
    packed = lax.all_gather(packed, "dp", axis=0)
    n = packed.shape[0]

    def by_rows(first, last):
        return packed[:, first:last].transpose(1, 0, 2, 3).reshape(last - first, n * rows, d)

    small = jnp.concatenate([ffn_bias.reshape(4, rows), gate_bias[None], gains], 0).astype(F32)
    small = lax.all_gather(small, "dp", axis=0)
    b1 = small[:, 0:4].reshape(4, 1, d)
    vec = small.transpose(1, 0, 2).reshape(8, d)
    vec = jnp.concatenate([vec[4:8], jnp.zeros((4, d), F32)], 0)
    w2 = packed[:, 8:12].reshape(4, d, d)
    return by_rows(0, 4), by_rows(4, 8), w2, by_rows(12, 16), packed[:, 16:18].reshape(2, d, d), vec, b1


def plain_grads(rows, gattn, gw1, gw2, gwr, ggate, gb, gvec):
    d = gattn.shape[-1]
    n = d // rows

    def by_rows(grad):
        return grad.reshape(-1, n, rows, d).transpose(1, 0, 2, 3)

    packed = jnp.concatenate(
        [by_rows(gattn), by_rows(gw1), gw2.reshape(n, 4, rows, d), by_rows(gwr), ggate.reshape(n, 2, rows, d)], 1
    )
    owned = lax.psum_scatter(packed.astype(F32), "dp", scatter_dimension=0, tiled=False)
    owned = lax.psum(owned.astype(BF16), "outer").astype(F32)
    vectors = gvec[0:4].reshape(4, n, rows).transpose(1, 0, 2).reshape(n, 4 * rows)
    small = jnp.concatenate([gb.reshape(n, 4 * rows), vectors], 1)
    small = lax.psum(lax.psum_scatter(small, "dp", scatter_dimension=0, tiled=False), "outer")
    return (
        owned[0:3], owned[3], owned[4:8].transpose(1, 0, 2).reshape(rows, 4 * d), owned[8:12].reshape(4 * rows, d),
        owned[12:15], owned[15], owned[16:18].reshape(2 * rows, d),
        small[0:4 * rows], small[4 * rows:5 * rows], small[5 * rows:].reshape(3, rows),
    )


def body(
    tokens, memory, doc_ids, resets, out_grad, memory_grad,
    attn_qkv, attn_out, ffn_in, ffn_bias, ffn_out, writer_qkv, writer_out, gate_weight, gate_bias, gains,
):
    micro, segs, seg, d = tokens.shape
    slots = memory.shape[2]
    rows = attn_out.shape[0]
    n = micro * segs
    ring = lax.axis_size("dp") == 16 and lax.axis_size("outer") == 2 and rows == 32
    tokens, out_grad = tokens.reshape(n, seg, d), out_grad.reshape(n, seg, d)
    memory, memory_grad = memory.reshape(n, slots, d), memory_grad.reshape(n, slots, d)
    docs = doc_ids.reshape(n, 1, seg)
    keep = jnp.broadcast_to((1 - resets).astype(F32).reshape(n, 1, 1), (n, 1, 128))
    if ring:
        weights = (
            attn_qkv, attn_out, ffn_in, ffn_out.reshape(4, rows, d), writer_qkv, writer_out,
            gate_weight.reshape(4, rows // 2, d), ffn_bias.reshape(1, 4 * rows), gate_bias.reshape(1, rows), gains,
        )
    else:
        attn, w1, w2, wr, gate, vec, b1 = plain_weights(
            attn_qkv, attn_out, ffn_in, ffn_out, writer_qkv, writer_out, gate_weight, ffn_bias, gate_bias, gains
        )
        units = (4, 4, 2, 2, 32, d)
        weights = (attn.reshape(units), w1.reshape(units), w2.reshape(4, 2, 2, 4, 32, d), vec, b1)
    n1, qt, k, v, e, linv, ot, h1, out, res, act, slope, vec, *whole = call_forward(ring, tokens, memory, docs, keep, weights)
    if ring:
        attn, w1, w2, wr = (array.reshape(4, d, d) for array in whole[:4])
        gate = whole[4].reshape(2, d, d)
    new_memory, dkept, gvec, gb, gw1, gw2, dh, gwr, ggate = call_ffn_back(
        ring, res, memory, memory_grad, docs, keep, wr, gate, vec, out_grad, h1, act, slope, w1, w2
    )
    extra = (gb, gw1.reshape(4, 4, 2, 2, 32, d), gw2.reshape(4, 2, 2, 4, 32, d)) if ring else ()
    grad_tokens, grad_memory, *rest = call_attn_back(
        ring, dh, tokens, memory, keep, n1, qt, k, v, e, linv, ot, dkept, attn, vec, gvec, extra
    )
    if ring:
        fattn, fw1, fw2, small = rest
        grads = call_hand_out(fattn, fw1, fw2, gwr, ggate, small)
    else:
        gattn, gvec = rest
        grads = plain_grads(rows, gattn.reshape(4, d, d), gw1, gw2, gwr, ggate, gb, gvec)
    gqkv, gout, gin, gffn, gwqkv, gwout, ggw, gb, ggb, ggains = grads
    return (
        out.reshape(micro, segs, seg, d), new_memory.reshape(micro, segs, slots, d),
        grad_tokens.reshape(micro, segs, seg, d), grad_memory.reshape(micro, segs, slots, d),
        gqkv, gout, gin, gb.reshape(4 * rows), gffn.reshape(4 * rows, d), gwqkv, gwout, ggw.reshape(2 * rows, d),
        ggb.reshape(rows), ggains,
    )


def solution(mesh):
    split = ("dp", "outer")
    whole = P(None, split, None, None)
    weights = (
        P(None, "dp", None), P("dp", None), P("dp", None), P("dp"), P("dp", None), P(None, "dp", None),
        P("dp", None), P("dp", None), P("dp"), P(None, "dp"),
    )
    return jax.shard_map(
        body,
        mesh=mesh,
        in_specs=(whole, whole, P(None, split, None), P(None, split), whole, whole) + weights,
        out_specs=(whole, whole, whole, whole) + weights,
        check_vma=False,
    )
```

time: 702 us -> 248 us (0.35)
  waiting for transfers between devices: 363 us -> 0 us
  blocking collectives: 121 us -> 0 us
  Pallas kernels: 146 us -> 240 us
  local copies, waits for them, and re-layouts: 40.9 us -> 6.59 us
  other arithmetic: 16.4 us -> 0.66 us
  between operations: 14 us -> 0.7 us
    reduce_scatter x1 -> x0, waiting for transfers between devices: 283 us -> none  [body(): lax.psum_scatter(pack_grads(n, gattn, gw1, gw2, gwr, ggate).astype(F32),...]
    pallas_call x4, Pallas kernels: 146 us -> 240 us  [the longest x1 93 us: call_forward(): pl.pallas_call(functools.partial(forward_kernel, ring, n), grid=(2 * n,),...]
    all_gather x1 -> x0, waiting for transfers between devices: 79.9 us -> none  [body(): lax.all_gather(packed, 'dp', axis=0)]
    unnamed x1 -> x0, blocking collectives: 75 us -> none
    all_gather x1 -> x0, blocking collectives: 43.3 us -> none  [body(): small = lax.all_gather(small, 'dp', axis=0)]
    convert_element_type x5 -> x0, other arithmetic: 16.3 us -> none  [the longest x1 12.9 us: body(): pack_grads(n, gattn, gw1, gw2, gwr, ggate).astype(F32)]
    transpose x4 -> x0, local copies, waits for them, and re-layouts: 9.88 us -> none  [by_rows(): gathered[:, first:last].transpose(1, 0, 2, 3)]
  transfers between devices with their start and end apart: 3 -> 0, of which waited for: 2 -> 0; matrix products, arithmetic and copies ran while one was open for 1% -> 0% of each run, Pallas kernels for 0% -> 0%
where the time goes in v3:
time: 248 us; the launch traced here: 247 us
  Pallas kernels  240 us (97%)
  local copies, waits for them, and re-layouts  6.59 us (3%)
    pallas_call x1, Pallas kernels, call_forward(): pl.pallas_call(functools.partial(forward_kernel, ring, n), grid=(2 * n,),...  93 us
    pallas_call x1, Pallas kernels, call_attn_back(): pl.pallas_call(functools.partial(attn_back_kernel, ring, n), grid=(2 * n,...  79.2 us
    pallas_call x1, Pallas kernels, call_ffn_back(): pl.pallas_call(functools.partial(ffn_back_kernel, ring, n), grid=(n + 1,)...  65 us
    unnamed x12, local copies, waits for them, and re-layouts  5.94 us

profile of v3, /device:TPU:0, one launch (start us, length us, event | category | flops | bytes accessed | tf_op | source)
XLA Modules:
  0.0 247.5 jit_solution(6782763783801573795)
XLA Ops:
  0.6 0.7 convert_bitcast_fusion
  1.3 0.7 broadcast_in_dim.8.refs_3_.refs_4_.refs_9_
  2.0 93.0 %gather_forward.1 = (bf16[4,640,512]{2,1,0:T(8,128)(2,1)}, bf16[4,512,512]{2,1,0:T(8,128)(2,1)}, bf16[4,640,512]{2,1,0:T(8,128)(2,1)}, bf16[4,640,512]{2,1,0:T(8...) custom-call(bf16[4,512,512]{2,1,0:T(8,128)(2,1)} %bitcast.33, ...), custom_call_target="tpu_custom_call" | custom-call | tf_op jit(solution)/shard_map/gather_forward/pallas_call | solution.py:666
  95.0 65.0 %ffn_back.1 = (f32[4,64,512]{2,1,0:T(8,128)}, f32[4,64,512]{2,1,0:T(8,128)}, f32[8,512]{1,0:T(8,128)}, f32[4,1,512]{2,1,0:T(1,128)}, bf16[4,512,512]{2,1,0:T(8,1...) custom-call(f32[4,256,512]{2,1,0:T(8,128)} %get-tuple-element.58.ref, ...), custom_call_target="tpu_custom_call" | custom-call | tf_op jit(solution)/shard_map/ffn_back/pallas_call | solution.py:908
  160.0 0.0 copy-start.1
  160.0 79.2 %attn_back.1 = (f32[4,512,512]{2,1,0:T(8,128)}, f32[4,64,512]{2,1,0:T(8,128)}, f32[4,32,512]{2,1,0:T(8,128)}, f32[4,32,512]{2,1,0:T(8,128)}, f32[4,32,512]{2,1,0:T(8,128)}, /*index=5*/f32[8,128]{1,0:T(8,128)}) custom-call(bf16[4,640,512]{2,1,0:T(8,128)(2,1)} %get-tuple-element.68.refs_0_, bf16[4,512,512]{2,1,0:T(8,128)(2,1)} %get-tuple-element.69.refs_1_, ...), custom_call_target="tpu_custom_call" | custom-call | tf_op jit(solution)/shard_map/attn_back/pallas_call | solution.py:1122
  239.2 0.0 copy-start.2
  239.2 2.3 hand_out.1
  241.5 0.0 copy-done.1
  241.5 0.0 copy-start
  241.5 1.3 copy.38
  242.8 0.0 copy-done.2
  242.8 0.8 copy.39
  243.6 1.0 copy-done
  244.6 0.0 copy-start.3
  244.6 2.0 copy.40
  246.7 0.0 copy-done.3
  246.7 0.8 copy.41
Async XLA Ops:
  160.0 81.5 %copy-start.1 = (bf16[4,512,512]{2,1,0:T(8,128)(2,1)S(1)}, bf16[4,512,512]{2,1,0:T(8,128)(2,1)}, u32[]{:S(2)}) copy-start(bf16[4,512,512]{2,1,0:T(8,128)(2,1)} %get-tuple-element.57) | copy-start | bytes 6291460
  239.2 3.7 %copy-start.2 = (f32[4,64,512]{2,1,0:T(8,128)S(1)}, f32[4,64,512]{2,1,0:T(8,128)}, u32[]{:S(2)}) copy-start(f32[4,64,512]{2,1,0:T(8,128)} %get-tuple-element.67) | copy-start | bytes 1572868
  241.5 3.1 %copy-start = (f32[4,512,512]{2,1,0:T(8,128)S(1)}, f32[4,512,512]{2,1,0:T(8,128)}, u32[]{:S(2)}) copy-start(f32[4,512,512]{2,1,0:T(8,128)} %get-tuple-element.82) | copy-start | bytes 12582916
  244.6 2.0 copy-start.3

commit v4 on v3

--- a/solution.py
+++ b/solution.py
@@ -169,6 +169,88 @@
         self.left(6, self.half(self.unit, True))
 
 
+class FirstGather(Travel):
+    SHIFTS = (0, 3, 1, 2)
+
+    def __init__(self, place, view, own, lane, send, recv, local):
+        super().__init__(place, send, recv)
+        self.view, self.own, self.lane, self.local = view, own, lane, local
+        self.unit = 2 * place.core + lane
+
+    def part(self, unit, z, far_first, far_second):
+        at = self.place
+        far_x, far_y = (far_second, far_first) if self.lane else (far_first, far_second)
+        return self.view(unit, z, 1 - at.y if far_y else at.y, 1 - at.x if far_x else at.x)
+
+    def block(self, shift, far_first, far_second):
+        return self.part(self.unit, self.place.other_z(4 - shift), far_first, far_second)
+
+    def first_partner(self):
+        return self.place.along_y() if self.lane else self.place.along_x()
+
+    def second_partner(self):
+        return self.place.along_x() if self.lane else self.place.along_y()
+
+    def keep(self):
+        return pltpu.make_async_copy(self.own(self.unit), self.block(0, False, False), self.local)
+
+    def begin(self):
+        mine = self.own(self.unit)
+        there = self.block(0, False, False)
+        for shift in (3, 1, 2):
+            self.go(shift - 1, mine, there, self.place.along_z(shift))
+        self.go(4, mine, there, self.first_partner())
+        self.go(8, mine, there, self.second_partner())
+        self.keep().start()
+
+    def column_block(self, shift):
+        here = self.block(shift, False, False)
+        self.arrived(shift - 1, here)
+        self.go(4 + shift, here, here, self.first_partner())
+        self.go(8 + shift, here, here, self.second_partner())
+
+    def column_done(self):
+        self.keep().wait()
+        self.share(0, False, False)
+
+    def share(self, index, far_first, far_second):
+        part = self.part(self.unit, EVERY, far_first, far_second)
+        self.go(16 + index, part, part, self.place.sibling())
+
+    def far_block(self, shift):
+        here = self.block(shift, True, False)
+        self.arrived(4 + shift, here)
+        self.go(12 + shift, here, here, self.second_partner())
+
+    def far_done(self):
+        self.share(1, True, False)
+        for shift in self.SHIFTS:
+            self.arrived(8 + shift, self.block(shift, False, True))
+        self.share(2, False, True)
+
+    def rest(self):
+        for shift in self.SHIFTS:
+            self.arrived(12 + shift, self.block(shift, True, True))
+        self.share(3, True, True)
+
+    def done(self):
+        other = 2 * (1 - self.place.core) + self.lane
+        for index, (far_first, far_second) in enumerate(((False, False), (True, False), (False, True), (True, True))):
+            self.arrived(16 + index, self.part(other, EVERY, far_first, far_second))
+
+    def finish(self):
+        for stage in range(3):
+            self.left(stage, self.own(self.unit))
+        for leg in (4, 8):
+            self.left(leg, self.own(self.unit))
+            for shift in (1, 2, 3):
+                self.left(leg + shift, self.block(shift, False, False))
+        for shift in range(4):
+            self.left(12 + shift, self.block(shift, True, False))
+        for index, (far_first, far_second) in enumerate(((False, False), (True, False), (False, True), (True, True))):
+            self.left(16 + index, self.part(self.unit, EVERY, far_first, far_second))
+
+
 class GatherSmall(Travel):
     def __init__(self, place, ref, own, send, recv):
         super().__init__(place, send, recv)
@@ -220,22 +302,18 @@
 
 
 class Reduce(Travel):
-    def __init__(self, place, grad, lane, acc, wide, mid, narrow, final, send, recv, local):
+    def __init__(self, place, own, other, lane, acc, wide, mid, narrow, final, final_other, send, recv, local):
         super().__init__(place, send, recv)
-        self.grad, self.lane, self.local = grad, lane, local
-        self.acc, self.wide, self.mid, self.narrow, self.final = acc, wide, mid, narrow, final
-        self.unit = 2 * place.core + lane
-        self.other = 2 * (1 - place.core) + lane
-
-    def whole(self, unit):
-        return self.grad(unit, EVERY, EVERY, EVERY)
+        self.own, self.other, self.lane, self.local = own, other, lane, local
+        self.acc, self.wide, self.mid, self.narrow = acc, wide, mid, narrow
+        self.final, self.final_other = final, final_other
 
     def stage_share(self):
-        self.go(0, self.whole(self.other), self.wide, self.place.sibling())
-        pltpu.make_async_copy(self.whole(self.unit), self.acc, self.local).start()
+        self.go(0, self.other, self.wide, self.place.sibling())
+        pltpu.make_async_copy(self.own, self.acc, self.local).start()
 
     def wait_share(self):
-        pltpu.make_async_copy(self.whole(self.unit), self.acc, self.local).wait()
+        pltpu.make_async_copy(self.own, self.acc, self.local).wait()
         self.arrived(0, self.wide)
 
         def add(z, carry):
@@ -294,19 +372,19 @@
         for shift in (1, 2, 3):
             self.arrived(2 + shift, self.narrow.at[3 + shift])
             total = total + self.narrow[3 + shift].astype(F32)
-        self.final[self.unit] = total
+        self.final[...] = total
 
     def stage_final(self):
-        self.go(6, self.final.at[self.unit], self.final.at[self.unit], self.place.sibling())
+        self.go(6, self.final, self.final, self.place.sibling())
 
     def wait_final(self):
-        self.arrived(6, self.final.at[self.other])
-        self.left(0, self.whole(self.other))
+        self.arrived(6, self.final_other)
+        self.left(0, self.other)
         self.left(1, self.half(True))
         self.left(2, self.quarter())
         for shift in (1, 2, 3):
             self.left(2 + shift, self.block(shift))
-        self.left(6, self.final.at[self.unit])
+        self.left(6, self.final)
 
 
 class ReduceSmall(Travel):
@@ -363,23 +441,33 @@
             self.left(2 + shift, self.block(shift))
 
 
-def reduce_scratch(rounds, rows, d):
+def reduce_scratch(count, rows, d):
     return [
-        pltpu.VMEM((rounds, 2, 4, 2, 2, rows, d), BF16), pltpu.VMEM((rounds, 2, 4, 2, 2, rows, d), BF16),
-        pltpu.VMEM((rounds, 2, 4, 2, rows, d), BF16), pltpu.VMEM((rounds, 2, 7, rows, d), BF16),
-        pltpu.SemaphoreType.DMA((rounds, 2, 7)), pltpu.SemaphoreType.DMA((rounds, 2, 7)),
-        pltpu.SemaphoreType.DMA((rounds, 2)),
+        pltpu.VMEM((count, 4, 2, 2, rows, d), BF16), pltpu.VMEM((count, 4, 2, 2, rows, d), BF16),
+        pltpu.VMEM((count, 4, 2, rows, d), BF16), pltpu.VMEM((count, 7, rows, d), BF16),
+        pltpu.SemaphoreType.DMA((count, 7)), pltpu.SemaphoreType.DMA((count, 7)), pltpu.SemaphoreType.DMA((count,)),
     ]
 
 
-def reduce_round(place, grad, scratch, index, final):
+def reduce_unit(place, grad, scratch, index, lane, final, unit, other, columns=None):
     acc, wide, mid, narrow, send, recv, local = scratch
+    own, theirs = grad(unit, EVERY, EVERY, EVERY), grad(other, EVERY, EVERY, EVERY)
+    final_own, final_other = final.at[unit], final.at[other]
+    if columns is not None:
+        own, theirs = own.at[:, :, :, :, columns], theirs.at[:, :, :, :, columns]
+        final_own, final_other = final_own.at[:, columns], final_other.at[:, columns]
+    return Reduce(
+        place, own, theirs, lane, acc.at[index], wide.at[index], mid.at[index], narrow.at[index], final_own, final_other,
+        send.at[index], recv.at[index], local.at[index],
+    )
+
+
+def reduce_round(place, grad, scratch, index, final, columns=None):
     return [
-        Reduce(
-            place, grad, lane, acc.at[index, lane], wide.at[index, lane], mid.at[index, lane], narrow.at[index, lane], final,
-            send.at[index, lane], recv.at[index, lane], local.at[index, lane],
+        reduce_unit(
+            place, grad, scratch, index + l, l, final, 2 * place.core + l, 2 * (1 - place.core) + l, columns
         )
-        for lane in range(2)
+        for l in range(2)
     ]
 
 
@@ -389,20 +477,59 @@
             getattr(lane, name)()
 
 
+REDUCE_STEPS = (
+    ("stage_share",), ("wait_share", "stage_first"), ("wait_first", "stage_second"), ("wait_second", "stage_z"),
+    ("wait_z", "stage_final"), ("wait_final",),
+)
+GATHER_STEPS = (
+    ("stage_z",), ("wait_z", "stage_first"), ("wait_first", "stage_second"), ("wait_second", "stage_share"), ("wait_share",),
+)
+
+
+def job(lanes, steps):
+    return [lambda names=names: both(lanes, *names) for names in steps]
+
+
+def plan(jobs, places):
+    found, late = {}, []
+    for number, (steps, start, spans, *latest) in enumerate(jobs):
+        time = start
+        allowed = places[:places.index(latest[0]) + 1] if latest else places
+        for i, step in enumerate(steps):
+            fitting = [place for place in allowed if place[1] >= time] or allowed[-1:] * len(latest)
+            if fitting:
+                name, time = fitting[0]
+                found.setdefault(name, []).append(step)
+            else:
+                late.append((time, number, step))
+            time = time + (spans[i] if i < len(spans) else 0.0)
+    return found, [step for _, _, step in sorted(late, key=lambda entry: entry[:2])]
+
+
+def hook_in(found, name, condition):
+    if name in found:
+
+        @pl.when(condition)
+        def _():
+            for step in found[name]:
+                step()
+
+
+GATHER_PACE = 9.5
+GATHER_SPANS = (6.0, 7.0, 10.0, 4.0)
+PASS_TIME, PASS_TIMES = 8.5, (1.5, 3.0, 4.5, 6.0, 7.5, 8.5)
+FFN_TIME = 5.0
+FFN_BACK_TIME = 6.0
+REDUCE_SPANS = (4.0, 8.0, 6.0, 8.0, 3.0)
+SLIM_SPANS = (3.0, 6.0, 5.0, 6.0, 3.0)
+HALVES = (slice(0, 256), slice(256, 512))
+HEADS_TIME, HEADS_TIMES = 8.0, (0.0, 1.7, 3.4, 5.1, 6.8)
+LAST_TIME = 2.0
+FFN_REDUCE_PACE = 4.5
+
+
 def matrix(block):
     return block.reshape(-1, block.shape[-1])
-
-
-def at_places(beats, step, last):
-    def hook(slot):
-        for when, where, beat in beats:
-            if where == slot:
-
-                @pl.when(step == min(when, last))
-                def _(beat=beat):
-                    beat()
-
-    return hook
 
 
 def forward_kernel(ring, count, *refs):
@@ -429,15 +556,20 @@
     load_attn = lambda: pltpu.make_async_copy(attn_ref, attn_v, wsem.at[0])
     load_w1 = lambda: pltpu.make_async_copy(w1_ref, w1_v, wsem.at[1])
     load_w2 = lambda: pltpu.make_async_copy(w2_ref, w2_v, wsem.at[2])
-    hook = None
     if ring:
-        units, psem, sown_ref, sall_ref, send, recv, local, ssend, srecv = take(9)
+        units, psem, sown_ref, sall_ref, send, recv, local, ssend, srecv, fsend, frecv = take(11)
         place = Place()
         views = [unit_first(attn_ref), unit_first(w1_ref), unit_last(w2_ref), unit_first(wr_ref), unit_last(gate_ref)]
         rounds = []
         for r, view in enumerate(views):
             own = (lambda u: shards[6].at[u]) if r == 4 else (lambda u, r=r: units.at[4 * r + u])
-            rounds.append([Gather(place, view, own, l, send.at[r, l], recv.at[r, l], local.at[r, l]) for l in range(2)])
+            if r == 0:
+                lanes = [
+                    FirstGather(place, unit_first(attn_v), own, l, fsend.at[l], frecv.at[l], local.at[r, l]) for l in range(2)
+                ]
+            else:
+                lanes = [Gather(place, view, own, l, send.at[r, l], recv.at[r, l], local.at[r, l]) for l in range(2)]
+            rounds.append(lanes)
         small = GatherSmall(place, sall_ref, sown_ref, ssend, srecv)
         packs = [(shards[0], units.at[0:3]), (shards[1], units.at[3])]
         packs += [(shards[2].at[:, j * 512:(j + 1) * 512], units.at[4 + j]) for j in range(4)]
@@ -446,33 +578,27 @@
         def pack(i):
             return pltpu.make_async_copy(packs[i][0], packs[i][1], psem.at[i])
 
-        last = len(rounds) - 1
-
-        def advance(r):
-            if r > 0:
-                both(rounds[r - 1], "wait_second", "stage_share")
-            if r <= last:
-                both(rounds[r], "wait_first", "stage_second")
-            if r + 1 <= last:
-                both(rounds[r + 1], "wait_z", "stage_first")
-            if r + 2 <= last:
-                both(rounds[r + 2], "stage_z")
-
-        def third():
-            advance(3)
-            both(rounds[1], "wait_share")
-            load_w1().start()
-
-        def fourth():
-            advance(4)
-            both(rounds[2], "wait_share")
-            load_w2().start()
-
-        beats = [
-            (0, 1, lambda: (both(rounds[1], "wait_first", "stage_second"), both(rounds[2], "wait_z", "stage_first"), both(rounds[3], "stage_z"))),
-            (1, 0, lambda: advance(2)), (2, 0, third), (3, 0, fourth), (3, 1, lambda: advance(5)),
-        ]
-        hook = at_places(beats, step, count - 1)
+        passes = [((s, i), PASS_TIME * s + PASS_TIMES[i]) for s in range(count) for i in range(len(PASS_TIMES))]
+        jobs = []
+        for r in range(1, 5):
+            steps = job(rounds[r], GATHER_STEPS)
+            if r in (1, 2):
+                share = steps[-1]
+                load = load_w1 if r == 1 else load_w2
+                steps[-1] = lambda share=share, load=load: (share(), load().start())
+            latest = (passes[-1],) if r in (1, 2) else ()
+            if r == 1:
+                jobs.append((steps[1:], 0.0, GATHER_SPANS[1:]) + latest)
+            else:
+                jobs.append((steps, GATHER_PACE * (r - 1) - GATHER_SPANS[0], GATHER_SPANS) + latest)
+        places = list(passes)
+        at_load = PASS_TIME * count
+        places += [((count + s, i), at_load + FFN_TIME * (s + i / 4)) for s in range(count) for i in range(4)]
+        found, rest = plan(jobs, places)
+
+    def hook(name, extra=True):
+        if ring:
+            hook_in(found, name, (step == name[0]) & extra)
 
     @pl.when(step < count)
     def _():
@@ -491,7 +617,7 @@
                 small.stage_z()
                 pack(0).wait()
                 pack(1).wait()
-                both(rounds[0], "stage_z")
+                both(rounds[0], "begin")
                 for i in range(2, len(packs)):
                     pack(i).wait()
         else:
@@ -522,23 +648,26 @@
             def _():
                 small.wait_z()
                 small.stage_first()
-                both(rounds[0], "wait_z", "stage_first")
-                both(rounds[1], "stage_z")
+                for shift in FirstGather.SHIFTS[1:]:
+                    for lane in rounds[0]:
+                        lane.column_block(shift)
+                both(rounds[0], "column_done")
                 small.wait_first()
                 small.stage_second()
-                both(rounds[0], "wait_first", "stage_second")
+                for shift in FirstGather.SHIFTS:
+                    for lane in rounds[0]:
+                        lane.far_block(shift)
+                both(rounds[1], "stage_z")
+                both(rounds[0], "far_done")
                 small.wait_second()
                 for m in range(4):
                     total = sall_ref[m, 0, 0] + sall_ref[m, 0, 1] + sall_ref[m, 1, 0] + sall_ref[m, 1, 1]
                     vec_ref[:, m * 128:(m + 1) * 128] = jnp.concatenate([total[1:8], total[0:1]], 0)
                     for i in range(4):
                         b1_ref[m, :, i * 128:(i + 1) * 128] = sall_ref[m, i // 2, i % 2, 0:1, :]
-                both(rounds[0], "wait_second", "stage_share")
-                both(rounds[1], "wait_z", "stage_first")
-                both(rounds[2], "stage_z")
-                both(rounds[0], "wait_share")
-                load_attn().start()
-                load_attn().wait()
+                both(rounds[0], "rest")
+                both(rounds[0], "done")
+                pltpu.make_async_copy(attn_v, attn_ref, wsem.at[0]).start()
 
         x = tok_ref[0].astype(F32)
         gain_one = vec_ref[1:2, :]
@@ -550,13 +679,15 @@
         n1_ref[0, 128:, :] = n1t
         qt_ref[0] = (dot_nt(matrix(attn_v[0]).T, n1t) * 0.125).astype(BF16)
         n1 = n1_ref[0]
-        k_ref[0] = dot(n1, matrix(attn_v[1])).astype(BF16)
+        keys = dot(n1, matrix(attn_v[1])).astype(BF16)
         v = dot(n1, matrix(attn_v[2])).astype(BF16)
-        v_ref[0] = v
+        for pair in range(4):
+            k_ref[0, pair] = keys[:, pair * 128:(pair + 1) * 128]
+            v_ref[0, pair] = v[:, pair * 128:(pair + 1) * 128]
         vt_ref[...] = v.T
         pair_ref[...] = jnp.zeros_like(pair_ref)
-        if hook:
-            hook(0)
+        for s in range(count):
+            hook((s, 0))
 
         def one_pair(pair, carry):
             lanes = pl.ds(pl.multiple_of(pair * 128, 128), 128)
@@ -565,7 +696,7 @@
                 held = pair_ref.at[block]
                 columns = pl.ds(block * BLOCK, BLOCK)
                 diagonal_pair(held, qt_ref[0, lanes, columns])
-                scores = dot(k_ref[0, first:last_row, lanes], held[...])
+                scores = dot(k_ref[0, pair, first:last_row, :], held[...])
                 bias = bias_ref[start:start + last_row - first, :]
                 scores = scores + jnp.concatenate([bias, bias], 1)
                 largest = jnp.max(scores, axis=0, keepdims=True)
@@ -578,14 +709,17 @@
                 ot_ref[0, lanes, columns] = jnp.concatenate(
                     [mixed[0:64, 0:128], mixed[64:128, 128:256]], 0
                 ).astype(BF16)
+            for s in range(count):
+                for i in range(4):
+                    hook((s, 1 + i), pair == i)
             return carry
 
         lax.fori_loop(0, 4, one_pair, 0)
         h1 = x + dot(ot_ref[0].T, matrix(attn_v[3]))
         h1_ref[0] = h1
         hidden_ref[step] = h1
-        if hook:
-            hook(1)
+        for s in range(count):
+            hook((s, 5))
 
     @pl.when(step >= count)
     def _():
@@ -597,23 +731,31 @@
         h1 = hidden_ref[step - count]
         hat, _ = norm_parts(h1)
         n2 = (hat * vec_ref[2:3, :]).astype(BF16)
-        result = h1
-        for part in range(4):
-            before = dot(n2, matrix(w1_v[part])) + b1_ref[part]
-            cdf = 0.5 + 0.5 * lax.erf(before * 0.7071067811865476)
-            active = (before * cdf).astype(BF16)
-            act_ref[0, part] = active
-            slope = cdf + before * jnp.exp(before * before * -0.5) * 0.3989422804014327
-            slope_ref[0, part] = slope.astype(BF16)
-            result = result + dot(active, matrix(w2_v[part]))
-        out_ref[0] = result.astype(BF16)
-        res_ref[0] = result[seg // 2:]
+        tall = seg // 2
+        for block in range(2):
+            rows = slice(block * tall, (block + 1) * tall)
+            result = h1[rows]
+            for part in range(8):
+                columns = slice((part % 2) * 256, (part % 2) * 256 + 256)
+                before = dot(n2[rows], matrix(w1_v[part // 2])[:, columns]) + b1_ref[part // 2][:, columns]
+                cdf = 0.5 + 0.5 * lax.erf(before * 0.7071067811865476)
+                active = (before * cdf).astype(BF16)
+                act_ref[0, part // 2, rows, columns] = active
+                slope = cdf + before * jnp.exp(before * before * -0.5) * 0.3989422804014327
+                slope_ref[0, part // 2, rows, columns] = slope.astype(BF16)
+                result = result + dot(active, matrix(w2_v[part // 2])[columns, :])
+                if part in (3, 7):
+                    for s in range(count, 2 * count):
+                        hook((s, 2 * block + (part == 7)))
+            out_ref[0, rows, :] = result.astype(BF16)
+        res_ref[0] = result
         if ring:
 
             @pl.when(step == 2 * count - 1)
             def _():
-                both(rounds[3], "wait_share")
-                both(rounds[4], "wait_share")
+                pltpu.make_async_copy(attn_v, attn_ref, wsem.at[0]).wait()
+                for step_left in rest:
+                    step_left()
                 for lanes in rounds:
                     both(lanes, "finish")
                 small.finish()
@@ -634,7 +776,7 @@
     n, seg, d = tokens.shape
     slots = memory.shape[1]
     early = [
-        ((seg + 128, d), BF16), ((d, seg), BF16), ((seg + 128, d), BF16), ((seg + 128, d), BF16), ((4, LIVE, 256), BF16),
+        ((seg + 128, d), BF16), ((d, seg), BF16), ((4, seg + 128, 128), BF16), ((4, seg + 128, 128), BF16), ((4, LIVE, 256), BF16),
         ((4, 4, 1, 256), F32), ((d, seg), BF16), ((seg, d), F32),
     ]
     late = [((seg, d), BF16), ((seg // 2, d), F32), ((4, seg, 512), BF16), ((4, seg, 512), BF16)]
@@ -659,6 +801,7 @@
             pltpu.VMEM((16, 32, d), BF16), pltpu.SemaphoreType.DMA((9,)), pltpu.VMEM((8, 128), F32),
             pltpu.VMEM((4, 2, 2, 8, 128), F32), pltpu.SemaphoreType.DMA((5, 2, 7)), pltpu.SemaphoreType.DMA((5, 2, 7)),
             pltpu.SemaphoreType.DMA((5, 2)), pltpu.SemaphoreType.DMA((5,)), pltpu.SemaphoreType.DMA((5,)),
+            pltpu.SemaphoreType.DMA((2, 20)), pltpu.SemaphoreType.DMA((2, 20)),
         ]
         params.update(collective_id=0, has_side_effects=True)
     else:
@@ -676,9 +819,9 @@
 
 
 def writer_all(
-    res_ref, mem_ref, memgrad_ref, doc_ref, keep_ref, wr_ref, gate_ref, vec_ref,
-    newmem_ref, dres_ref, dkept_ref, gwr_ref, ggate_ref, gvec_ref,
-    n3_ref, ns_ref, kept_ref, sq_ref, tk_ref, tv_ref, p_ref, wt_ref, dsq_ref, dtk_ref, dtv_ref, dlog_ref, dw_ref,
+    gate_done, read_done, res_ref, mem_ref, memgrad_ref, doc_ref, keep_ref, wr_ref, gate_ref, vec_ref,
+    newmem_ref, dres_ref, dkept_ref, gwr_ref, ggate_ref, ggb_ref,
+    n3_ref, ns_ref, kept_ref, sq_ref, tk_ref, tv_ref, p_ref, wt_ref, dsq_ref, dlog_ref, dw_ref,
 ):
     n, half, d = res_ref.shape
     slots = mem_ref.shape[1]
@@ -737,9 +880,10 @@
     dlogit = memgrad * (kept - write) * gate * (1.0 - gate)
     dlog_ref[...] = dlogit.astype(BF16)
     dlow = dlog_ref[...]
-    gvec_ref[0:1, :] = jnp.sum(dlow.astype(F32), axis=0, keepdims=True)
+    ggb_ref[...] = jnp.sum(dlow.astype(F32), axis=0, keepdims=True)
     ggate_ref[0:2] = dot_tn(kept_low, dlow).astype(BF16).reshape((2,) + ggate_ref.shape[1:])
     ggate_ref[2:4] = dot_tn(write_low, dlow).astype(BF16).reshape((2,) + ggate_ref.shape[1:])
+    gate_done()
     dkept = memgrad * gate + dot_nt(dlow, gate_ref[0])
     dwrite = memgrad * (1.0 - gate) + dot_nt(dlow, gate_ref[1])
     dkept_ref[...] = dkept.reshape(n, slots, d)
@@ -758,27 +902,27 @@
             ds = (p * (dp - jnp.sum(dp * p, axis=1, keepdims=True))).astype(BF16)
             dq = dot(ds, tk_ref[rows, lanes]) * 0.125
             dsq_ref[small, lanes] = jnp.where(low_half, dq[:slots], dq[slots:]).astype(BF16)
-            dtk_ref[rows, lanes] = dot_tn(ds, halves(sq_ref[small, lanes])).astype(BF16)
-            dtv_ref[rows, lanes] = dot_tn(p.astype(BF16), grads).astype(BF16)
+            tk_ref[rows, lanes] = dot_tn(ds, halves(sq_ref[small, lanes])).astype(BF16)
+            tv_ref[rows, lanes] = dot_tn(p.astype(BF16), grads).astype(BF16)
         return carry
 
     lax.fori_loop(0, n, read_back, 0)
+    read_done()
     put(gwr_ref, 0, dot_tn(ns_ref[...], dsq_ref[...]))
-    put(gwr_ref, 1, dot_tn(n3_ref[...], dtk_ref[...]))
-    put(gwr_ref, 2, dot_tn(n3_ref[...], dtv_ref[...]))
+    put(gwr_ref, 1, dot_tn(n3_ref[...], tk_ref[...]))
+    put(gwr_ref, 2, dot_tn(n3_ref[...], tv_ref[...]))
     grad = dot_nt(dsq_ref[...], wr_ref[0])
     hat, rstd = norm_parts(kept_ref[...])
     dkept_ref[...] += norm_back(grad, hat, rstd, gain).reshape(n, slots, d)
-    ggain = jnp.sum(grad * hat, axis=0, keepdims=True)
-
-    def back(i, ggain):
+
+    def back(i, carry):
         rows = pl.ds(pl.multiple_of(i * half, half), half)
-        grad = dot_nt(dtk_ref[rows, :], wr_ref[1]) + dot_nt(dtv_ref[rows, :], wr_ref[2])
+        grad = dot_nt(tk_ref[rows, :], wr_ref[1]) + dot_nt(tv_ref[rows, :], wr_ref[2])
         hat, rstd = norm_parts(res_ref[i])
         dres_ref[i] = norm_back(grad, hat, rstd, gain)
-        return ggain + jnp.sum(grad * hat, axis=0, keepdims=True)
-
-    gvec_ref[3:4, :] = lax.fori_loop(0, n, back, ggain)
+        return carry
+
+    lax.fori_loop(0, n, back, 0)
 
 
 def ffn_back_kernel(ring, count, *refs):
@@ -791,63 +935,56 @@
 
     writer_in = take(8)
     vec_ref = writer_in[7]
-    og_ref, h1_ref, act_ref, slope_ref, w1_ref, w2_ref = take(6)
-    newmem_ref, dkept_ref, gvec_ref, gb_ref, gw1_ref, gw2_ref, dh_ref, gwr_out, ggate_out = take(9)
-    writer_scratch = take(13)
-    dres_ref, acc1_ref, acc2_ref, w1_v, w2_v, wsem = take(6)
+    og_ref, h1_ref, act_ref, slope_ref, ot_ref, linv_ref, w1_ref, w2_ref, attn_ref = take(9)
+    newmem_ref, dkept_ref, ggb_ref, gb_ref, gw1_ref, gw2_ref, gwo_ref, dh_ref, dot_ref, gwr_out, ggate_out = take(11)
+    writer_scratch = take(11)
+    dres_ref, acc1_ref, acc2_ref, acco_ref, w1_v, w2_v, wo_v, wsem = take(8)
     step = pl.program_id(0)
     seg = og_ref.shape[1]
-    load_w1 = lambda: pltpu.make_async_copy(w1_ref, w1_v, wsem.at[0])
-    load_w2 = lambda: pltpu.make_async_copy(w2_ref, w2_v, wsem.at[1])
-    hook = None
+    loads = lambda: [
+        pltpu.make_async_copy(w1_ref, w1_v, wsem.at[0]), pltpu.make_async_copy(w2_ref, w2_v, wsem.at[1]),
+        pltpu.make_async_copy(attn_ref.at[3], wo_v, wsem.at[2]),
+    ]
     if ring:
         gwr_ref, ggate_ref, fwr_ref, fgate_ref = take(4)
         wide_scratch, slim_scratch = take(7), take(7)
         place = Place()
-        writer_round = reduce_round(place, unit_first(gwr_ref), wide_scratch, 0, fwr_ref)
+        writer_rounds = [
+            reduce_round(place, unit_first(gwr_ref), wide_scratch, 2 * i, fwr_ref, half) for i, half in enumerate(HALVES)
+        ]
         gate_round = reduce_round(place, unit_last(ggate_ref), slim_scratch, 0, fgate_ref)
-
-        def hand_back():
-            both(writer_round, "wait_final")
-            both(gate_round, "wait_final")
-            gwr_out[...] = fwr_ref[...]
-            ggate_out[...] = fgate_ref[...]
-
-        beats = [
-            (0, 0, lambda: both(writer_round, "wait_share", "stage_first")),
-            (0, 1, lambda: both(gate_round, "wait_share", "stage_first")),
-            (1, 0, lambda: (both(writer_round, "wait_first", "stage_second"), both(gate_round, "wait_first", "stage_second"))),
-            (1, 1, lambda: both(writer_round, "wait_second", "stage_z")),
-            (2, 0, lambda: both(gate_round, "wait_second", "stage_z")),
-            (2, 1, lambda: both(writer_round, "wait_z", "stage_final")),
-            (3, 0, lambda: both(gate_round, "wait_z", "stage_final")),
-            (3, 1, hand_back),
+        jobs = [
+            (job(gate_round, REDUCE_STEPS)[2:], 0.0, REDUCE_SPANS[2:]),
+            (job(writer_rounds[0], REDUCE_STEPS)[1:], 1.5, REDUCE_SPANS[1:]),
+            (job(writer_rounds[1], REDUCE_STEPS)[1:], 4.5, REDUCE_SPANS[1:]),
         ]
-        hook = at_places(beats, step - 1, count - 1)
+        places = [((1 + s, i), FFN_BACK_TIME * (s + i / 4)) for s in range(count) for i in range(4)]
+        found, rest = plan(jobs, places)
     else:
         gwr_ref, ggate_ref = gwr_out, ggate_out
 
     @pl.when(step == 0)
     def _():
-        load_w1().start()
-        load_w2().start()
+        for load in loads():
+            load.start()
         if ring:
             place.greet()
         acc1_ref[...] = jnp.zeros_like(acc1_ref)
         acc2_ref[...] = jnp.zeros_like(acc2_ref)
+        acco_ref[...] = jnp.zeros_like(acco_ref)
         gb_ref[...] = jnp.zeros_like(gb_ref)
-        gvec_ref[...] = jnp.zeros_like(gvec_ref)
-        writer_all(*writer_in, newmem_ref, dres_ref, dkept_ref, gwr_ref, ggate_ref, gvec_ref, *writer_scratch)
+        gate_done = (lambda: both(gate_round, "stage_share")) if ring else (lambda: None)
+        read_done = (lambda: both(gate_round, "wait_share", "stage_first")) if ring else (lambda: None)
+        writer_all(
+            gate_done, read_done, *writer_in, newmem_ref, dres_ref, dkept_ref, gwr_ref, ggate_ref, ggb_ref, *writer_scratch
+        )
         if ring:
-            both(writer_round, "stage_share")
-            both(gate_round, "stage_share")
-        load_w1().wait()
-        load_w2().wait()
+            both(writer_rounds[0] + writer_rounds[1], "stage_share")
+        for load in loads():
+            load.wait()
 
     @pl.when(step > 0)
     def _():
-        if hook:
-            hook(0)
         top = og_ref[0, 0:seg // 2, :].astype(F32)
         bottom = og_ref[0, seg // 2:, :].astype(F32) + dres_ref[step - 1]
         dresult = jnp.concatenate([top, bottom], 0)
@@ -859,24 +996,50 @@
         lowt = low.T
         grad = jnp.zeros_like(dresult)
         for part in range(4):
+            if ring:
+                for s in range(1, 1 + count):
+                    hook_in(found, (s, part), step == s)
             acc2_ref[part] += dot(lowt, act_ref[0, part])
             dbefore = (dot_nt(low, w2_v[part]) * slope_ref[0, part].astype(F32)).astype(BF16)
             gb_ref[part] += jnp.sum(dbefore.astype(F32), axis=0, keepdims=True)
             acc1_ref[part] += dot(n2t, dbefore)
             grad = grad + dot_nt(dbefore, w1_v[part])
-            if part == 1 and hook:
-                hook(1)
-        gvec_ref[2:3, :] += jnp.sum(grad * hat, axis=0, keepdims=True)
-        dh_ref[0] = dresult + norm_back(grad, hat, rstd, gain)
+        dh = dresult + norm_back(grad, hat, rstd, gain)
+        dh_ref[0] = dh
+        dlow = dh.astype(BF16)
+        mixed_grad = dot_nt(wo_v[...], dlow)
+        for pair in range(4):
+            for block in range(seg // BLOCK):
+                columns = slice(block * BLOCK, (block + 1) * BLOCK)
+                for i in range(2):
+                    features = slice(pair * 128 + i * 64, pair * 128 + i * 64 + 64)
+                    scale = linv_ref[0, pair, block, :, i * 128:(i + 1) * 128]
+                    dot_ref[0, features, columns] = (mixed_grad[features, columns] * scale).astype(BF16)
+        acco_ref[...] += dot(ot_ref[0], dlow)
 
         @pl.when(step == count)
         def _():
-            gw1_ref[...] = acc1_ref[...].astype(BF16)
+            stores = [
+                pltpu.make_async_copy(w1_v, gw1_ref, wsem.at[0]), pltpu.make_async_copy(w2_v, gw2_ref, wsem.at[1]),
+                pltpu.make_async_copy(wo_v, gwo_ref, wsem.at[2]),
+            ]
+            w1_v[...] = acc1_ref[...].astype(BF16)
+            stores[0].start()
             for part in range(4):
-                gw2_ref[part] = acc2_ref[part].T.astype(BF16)
-
-
-def call_ffn_back(ring, res, memory, memory_grad, docs, keep, wr, gate, vec, out_grad, h1, act, slope, w1, w2):
+                w2_v[part] = acc2_ref[part].T.astype(BF16)
+            stores[1].start()
+            wo_v[...] = acco_ref[...].astype(BF16)
+            stores[2].start()
+            if ring:
+                for step_left in rest:
+                    step_left()
+                gwr_out[...] = fwr_ref[...]
+                ggate_out[...] = fgate_ref[...]
+            for store in stores:
+                store.wait()
+
+
+def call_ffn_back(ring, res, memory, memory_grad, docs, keep, wr, gate, vec, out_grad, h1, act, slope, ot, linv, w1, w2, attn):
     n, half, d = res.shape
     seg = 2 * half
     slots = memory.shape[1]
@@ -888,38 +1051,37 @@
         grads = [((4, 32, d), F32), ((4, 16, d), F32)]
     else:
         grads = [(units, BF16), (gate_units, BF16)]
-    whole = [
-        ((n, slots, d), F32), ((n, slots, d), F32), ((8, d), F32), ((4, 1, d), F32), ((4, d, d), BF16), ((4, d, d), BF16),
-    ]
+    whole = [((n, slots, d), F32), ((n, slots, d), F32), ((1, d), F32), ((4, 1, d), F32)]
+    stored = [((4, d, d), BF16), ((4, d, d), BF16), ((d, d), BF16)]
     scratch = [
         pltpu.VMEM((rows, d), BF16), pltpu.VMEM((small, d), BF16), pltpu.VMEM((small, d), F32), pltpu.VMEM((small, d), BF16),
         pltpu.VMEM((rows, d), BF16), pltpu.VMEM((rows, d), BF16), pltpu.VMEM((n, 4, 2 * slots, half), F32),
-        pltpu.VMEM((small, d), BF16), pltpu.VMEM((small, d), BF16), pltpu.VMEM((rows, d), BF16),
-        pltpu.VMEM((rows, d), BF16), pltpu.VMEM((small, d), BF16), pltpu.VMEM((small, d), BF16),
-        pltpu.VMEM((n, half, d), F32), pltpu.VMEM((4, d, d), F32), pltpu.VMEM((4, d, d), F32),
-        pltpu.VMEM((4, d, d), BF16), pltpu.VMEM((4, d, d), BF16), pltpu.SemaphoreType.DMA((2,)),
+        pltpu.VMEM((small, d), BF16), pltpu.VMEM((small, d), BF16), pltpu.VMEM((small, d), BF16), pltpu.VMEM((small, d), BF16),
+        pltpu.VMEM((n, half, d), F32), pltpu.VMEM((4, d, d), F32), pltpu.VMEM((4, d, d), F32), pltpu.VMEM((d, d), F32),
+        pltpu.VMEM((4, d, d), BF16), pltpu.VMEM((4, d, d), BF16), pltpu.VMEM((d, d), BF16), pltpu.SemaphoreType.DMA((3,)),
     ]
     params = dict(vmem_limit_bytes=VMEM_LIMIT)
     if ring:
         scratch += [pltpu.VMEM(units, BF16), pltpu.VMEM(gate_units, BF16)]
         scratch += [pltpu.VMEM((4, 32, d), F32), pltpu.VMEM((4, 16, d), F32)]
-        scratch += reduce_scratch(1, 32, d) + reduce_scratch(1, 16, d)
+        scratch += reduce_scratch(4, 32, d // 2) + reduce_scratch(2, 16, d)
         params.update(collective_id=1, has_side_effects=True)
     return pl.pallas_call(
         functools.partial(ffn_back_kernel, ring, n),
         grid=(n + 1,),
-        out_shape=[jax.ShapeDtypeStruct(shape, kind) for shape, kind in whole]
-        + [jax.ShapeDtypeStruct((n, seg, d), F32)] + [jax.ShapeDtypeStruct(shape, kind) for shape, kind in grads],
+        out_shape=[jax.ShapeDtypeStruct(shape, kind) for shape, kind in whole + stored]
+        + [jax.ShapeDtypeStruct((n, seg, d), F32), jax.ShapeDtypeStruct((n, d, seg), BF16)]
+        + [jax.ShapeDtypeStruct(shape, kind) for shape, kind in grads],
         in_specs=[full_spec(array.shape) for array in writer_args] + [
             phase_spec((seg, d), 1, n), phase_spec((seg, d), 1, n), phase_spec((4, seg, 512), 1, n),
-            phase_spec((4, seg, 512), 1, n), ANY, ANY,
+            phase_spec((4, seg, 512), 1, n), phase_spec((d, seg), 1, n), phase_spec((4, 4, 1, 256), 1, n), ANY, ANY, ANY,
         ],
-        out_specs=[full_spec(shape) for shape, _ in whole] + [phase_spec((seg, d), 1, n)]
+        out_specs=[full_spec(shape) for shape, _ in whole] + [ANY] * 3 + [phase_spec((seg, d), 1, n), phase_spec((d, seg), 1, n)]
         + [full_spec(shape) for shape, _ in grads],
         scratch_shapes=scratch,
         compiler_params=pltpu.CompilerParams(**params),
         name="ffn_back",
-    )(*writer_args, out_grad, h1, act, slope, w1, w2)
+    )(*writer_args, out_grad, h1, act, slope, ot, linv, w1, w2, attn)
 
 
 def attn_back_kernel(ring, count, *refs):
@@ -930,213 +1092,209 @@
         del refs[:number]
         return out
 
-    n1_ref, qt_ref, k_ref, v_ref, e_ref, linv_ref, ot_ref = take(7)
+    qt_ref, k_ref, v_ref, e_ref, ot_ref, dot_ref = take(6)
     tok_ref, mem_ref, keep_ref, dkept_ref, dh_ref = take(5)
-    attn_ref, vec_ref, gvec_in_ref = take(3)
+    n1_ref, attn_ref, vec_ref = take(3)
     if ring:
-        gb_ref, gw1_ref, gw2_ref = take(3)
+        ggb_ref, gb_ref, gw1_ref, gw2_ref, gwo_ref = take(5)
     gtok_ref, gmem_ref = take(2)
     if ring:
-        fattn_ref, fw1_ref, fw2_ref, fsmall_ref = take(4)
+        fqkv_ref, fo_ref, fw1_ref, fw2_ref, fsmall_ref = take(5)
     else:
-        gattn_ref, gvec_ref = take(2)
-    dot_ref, kt_ref, dqt_ref, dk_ref, dv_ref, dkl_ref, dvl_ref, qp_ref, dp_ref, acc_ref, accg_ref = take(11)
+        (gqkv_ref,) = take(1)
+    dqt_ref, dkl_ref, dvl_ref, dk_ref, dv_ref, qp_ref, dp_ref = take(7)
     step = pl.program_id(0)
     seg = tok_ref.shape[1]
+    d = tok_ref.shape[2]
     slots = mem_ref.shape[1]
-    hook = late_hook = None
     if ring:
-        gattn_ref, final_ref = take(2)
-        scratch = take(7)
+        gqkv_ref, ffn_final, out_final, heads_final = take(4)
+        wide_scratch, out_scratch, heads_scratch = take(7), take(7), take(7)
         sown, sacc, swide, smid, snarrow, ssend, srecv = take(7)
         place = Place()
-        attn_round = reduce_round(place, unit_first(gattn_ref), scratch, 0, final_ref.at[0])
-        w1_round = reduce_round(place, unit_first(gw1_ref), scratch, 1, final_ref.at[1])
-        w2_round = reduce_round(place, unit_last(gw2_ref), scratch, 2, final_ref.at[2])
+        ffn_rounds = [
+            reduce_round(place, grad, wide_scratch, 4 * j + 2 * i, ffn_final.at[j], half)
+            for j, grad in ((1, unit_last(gw2_ref)), (0, unit_first(gw1_ref))) for i, half in enumerate(HALVES)
+        ]
+        out_unit = reduce_unit(place, unit_last(gwo_ref), out_scratch, 0, 0, out_final, place.core, 1 - place.core)
+        heads = [
+            reduce_unit(
+                place, unit_first(gqkv_ref.at[p]), heads_scratch, p, p % 2, heads_final.at[p], place.core, 1 - place.core
+            )
+            for p in range(4)
+        ]
         small = ReduceSmall(place, sown, sacc, swide, smid, snarrow, fsmall_ref, ssend, srecv)
-        beats = [
-            (0, 0, lambda: both(w2_round, "wait_share", "stage_first")),
-            (0, 1, lambda: (both(w2_round, "wait_first", "stage_second"), both(w1_round, "wait_share", "stage_first"))),
-            (1, 1, lambda: (both(w2_round, "wait_second", "stage_z"), both(w1_round, "wait_first", "stage_second"))),
-            (2, 1, lambda: (both(w2_round, "wait_z", "stage_final"), both(w1_round, "wait_second", "stage_z"))),
-            (3, 0, lambda: both(w1_round, "wait_z", "stage_final")),
-            (3, 1, lambda: (both(w2_round, "wait_final"), both(w1_round, "wait_final"))),
-        ]
-        hook = at_places(beats, step, count - 1)
-        late_beats = [
-            (0, 0, lambda: both(attn_round, "wait_share", "stage_first")),
-            (2, 0, lambda: both(attn_round, "wait_first", "stage_second")),
-            (3, 0, lambda: both(attn_round, "wait_second", "stage_z")),
-        ]
-        late_hook = at_places(late_beats, step - count, count - 1)
-
-    @pl.when(step < count)
+        jobs = [(job(ffn_rounds[i], REDUCE_STEPS), FFN_REDUCE_PACE * i, REDUCE_SPANS) for i in range(4)]
+        jobs.append((job([out_unit], REDUCE_STEPS), FFN_REDUCE_PACE * 4, SLIM_SPANS))
+        jobs.append((job([small], REDUCE_STEPS[:4] + (("wait_z",),)), FFN_REDUCE_PACE * 4 + 1.0, SLIM_SPANS))
+        for p in range(4):
+            jobs.append((job([heads[p]], REDUCE_STEPS)[1:], HEADS_TIME * (p + 1) + SLIM_SPANS[0], SLIM_SPANS[1:]))
+        places = [((p, i), HEADS_TIME * p + HEADS_TIMES[i]) for p in range(4) for i in range(5)]
+        places += [((4 + s, 0), 4 * HEADS_TIME + LAST_TIME * (s + 1)) for s in range(count)]
+        found, rest = plan(jobs, places)
+
+    def hook(name, extra=True):
+        if ring:
+            hook_in(found, name, (step == name[0]) & extra)
+
+    @pl.when(step < 4)
     def _():
         @pl.when(step == 0)
         def _():
             if ring:
                 place.greet()
-                both(w2_round, "stage_share")
-                both(w1_round, "stage_share")
-            acc_ref[...] = jnp.zeros_like(acc_ref)
-            accg_ref[...] = jnp.zeros_like(accg_ref)
-
-        low = dh_ref[0].astype(BF16)
-        acc_ref[3] += dot(ot_ref[0], low)
-        dot_ref[...] = dot_nt(attn_ref[3], low)
-        kt_ref[...] = k_ref[0].T
-        qp_ref[...] = jnp.zeros_like(qp_ref)
-        dp_ref[...] = jnp.zeros_like(dp_ref)
-        if hook:
-            hook(0)
-
-        def one_pair(pair, carry):
-            lanes = pl.ds(pl.multiple_of(pair * 128, 128), 128)
-            dk_ref[:, lanes] = jnp.zeros((seg + 128, 128), F32)
-            dv_ref[:, lanes] = jnp.zeros((seg + 128, 128), F32)
+                for m in range(4):
+                    for i in range(4):
+                        lanes = slice(i * 128, (i + 1) * 128)
+                        sown[m, i // 2, i % 2] = jnp.concatenate(
+                            [gb_ref[m, :, lanes], ggb_ref[:, m * 128:(m + 1) * 128], jnp.zeros((6, 128), F32)], 0
+                        )
+            qp_ref[...] = jnp.zeros_like(qp_ref)
+            dp_ref[...] = jnp.zeros_like(dp_ref)
+
+        features = pl.ds(pl.multiple_of(step * 128, 128), 128)
+
+        def one_segment(s, carry):
+            for p in range(4):
+                for i in range(4):
+                    hook((p, i), s == min(i, count - 1))
+            dk_ref[...] = jnp.zeros_like(dk_ref)
+            dv_ref[...] = jnp.zeros_like(dv_ref)
             for block, (first, last) in enumerate(SPANS):
                 start = STARTS[block]
-                columns = pl.ds(block * BLOCK, BLOCK)
-                linv = linv_ref[0, pair, block, :, :]
-                mixed_grad = dot_ref[lanes, columns]
-                top = (mixed_grad[0:64] * linv[:, 0:128]).astype(BF16)
-                bottom = (mixed_grad[64:128] * linv[:, 128:256]).astype(BF16)
-                mixed = ot_ref[0, lanes, columns].astype(F32)
+                columns = slice(block * BLOCK, (block + 1) * BLOCK)
+                mixed_grad = dot_ref[s, :, columns]
+                delta = mixed_grad.astype(F32) * ot_ref[s, :, columns].astype(F32)
                 delta = jnp.concatenate(
-                    [
-                        jnp.sum(top.astype(F32) * mixed[0:64], axis=0, keepdims=True),
-                        jnp.sum(bottom.astype(F32) * mixed[64:128], axis=0, keepdims=True),
-                    ],
-                    1,
+                    [jnp.sum(delta[0:64], axis=0, keepdims=True), jnp.sum(delta[64:128], axis=0, keepdims=True)], 1
                 )
                 held = dp_ref.at[block]
-                held[0:64, 0:128] = top
-                held[64:128, 128:256] = bottom
+                diagonal_pair(held, mixed_grad)
                 query = qp_ref.at[block]
-                diagonal_pair(query, qt_ref[0, lanes, columns])
-                e = e_ref[0, pair, start:start + last - first, :]
-                dp = dot(v_ref[0, first:last, lanes], held[...])
+                diagonal_pair(query, qt_ref[s, :, columns])
+                e = e_ref[s, 0, start:start + last - first, :]
+                dp = dot(v_ref[s, 0, first:last, :], held[...])
                 ds = (e.astype(F32) * (dp - delta)).astype(BF16)
-                dv_ref[first:last, lanes] += dot_nt(e, held[...])
-                dk_ref[first:last, lanes] += dot_nt(ds, query[...])
-                dq = dot(kt_ref[lanes, first:last], ds) * 0.125
-                dqt_ref[step, lanes, columns] = jnp.concatenate([dq[0:64, 0:128], dq[64:128, 128:256]], 0).astype(BF16)
+                dv_ref[first:last, :] += dot_nt(e, held[...])
+                dk_ref[first:last, :] += dot_nt(ds, query[...])
+                dq = dot_tn(k_ref[s, 0, first:last, :], ds) * 0.125
+                dqt_ref[s, features, columns] = jnp.concatenate([dq[0:64, 0:128], dq[64:128, 128:256]], 0).astype(BF16)
+            dkl_ref[s, step] = dk_ref[...].astype(BF16)
+            dvl_ref[s, step] = dv_ref[...].astype(BF16)
             return carry
 
-        lax.fori_loop(0, 4, one_pair, 0)
-        n1t = n1_ref[0].T
-        dk = dk_ref[...].astype(BF16)
-        dv = dv_ref[...].astype(BF16)
-        dkl_ref[step] = dk
-        dvl_ref[step] = dv
-        acc_ref[0] += dot_nt(n1t[:, 128:], dqt_ref[step])
-        acc_ref[1] += dot(n1t, dk)
-        acc_ref[2] += dot(n1t, dv)
-        if hook:
-            hook(1)
-
-        @pl.when(step == count - 1)
-        def _():
-            gattn_ref[...] = acc_ref[...].astype(BF16).reshape(gattn_ref.shape)
-            if ring:
-                both(attn_round, "stage_share")
-
-    @pl.when(step >= count)
+        lax.fori_loop(0, count, one_segment, 0)
+        for p in range(4):
+            hook((p, 4))
+        gq = dot(dqt_ref[0, features, :], n1_ref[0, 128:, :])
+        gkv = dot_tn(n1_ref[0], jnp.concatenate([dkl_ref[0, step], dvl_ref[0, step]], 1))
+        for s in range(1, count):
+            gq = gq + dot(dqt_ref[s, features, :], n1_ref[s, 128:, :])
+            gkv = gkv + dot_tn(n1_ref[s], jnp.concatenate([dkl_ref[s, step], dvl_ref[s, step]], 1))
+        both_cores = (2, 16, 16, 128)
+        parts = [part.astype(BF16).reshape(16, 2, 16, 128) for part in (gq.T, gkv[:, 0:128], gkv[:, 128:256])]
+        for i, part in enumerate(parts):
+            for core in range(2):
+                gqkv_ref[step, core, :, :, :, i * 16:(i + 1) * 16, :] = part[:, core].reshape(4, 2, 2, 16, 128)
+        if ring:
+            for p in range(4):
+
+                @pl.when(step == p)
+                def _(p=p):
+                    both([heads[p]], "stage_share")
+
+    @pl.when(step >= 4)
     def _():
-        here = step - count
+        here = step - 4
         gain = vec_ref[1:2, :]
-        dk = dkl_ref[here]
-        dv = dvl_ref[here]
+        dk = jnp.concatenate([dkl_ref[here, p] for p in range(4)], 1)
+        dv = jnp.concatenate([dvl_ref[here, p] for p in range(4)], 1)
         grad = dot_nt(dk, attn_ref[1]) + dot_nt(dv, attn_ref[2])
         slot_grad = grad[0:slots]
         kept = mem_ref[0] * keep_ref[0][:, 0:1]
         hat, rstd = norm_parts(kept)
-        ggain = jnp.sum(slot_grad * hat, axis=0, keepdims=True)
         gmem_ref[0] = (dkept_ref[0] + norm_back(slot_grad, hat, rstd, gain)) * keep_ref[0][:, 0:1]
         grad = grad[128:] + dot_nt(dqt_ref[here].T, attn_ref[0])
         hat, rstd = norm_parts(tok_ref[0].astype(F32))
-        accg_ref[...] += ggain + jnp.sum(grad * hat, axis=0, keepdims=True)
         gtok_ref[0] = dh_ref[0] + norm_back(grad, hat, rstd, gain)
-        if late_hook:
-            late_hook(0)
-
-        @pl.when(step == 2 * count - 1)
-        def _():
-            if not ring:
-                gvec_ref[...] = gvec_in_ref[...]
-                gvec_ref[1:2, :] = accg_ref[...]
-                return
-            vector = gvec_in_ref[...]
-            vector = jnp.concatenate([vector[0:1], accg_ref[...], vector[2:4], jnp.zeros((3, vector.shape[1]), F32)], 0)
-            for m in range(4):
-                for i in range(4):
-                    sown[m, i // 2, i % 2] = jnp.concatenate(
-                        [gb_ref[m, :, i * 128:(i + 1) * 128], vector[:, m * 128:(m + 1) * 128]], 0
-                    )
-            small.stage_share()
-            small.wait_share()
-            small.stage_first()
-            both(attn_round, "wait_z", "stage_final")
-            small.wait_first()
-            small.stage_second()
-            small.wait_second()
-            small.stage_z()
-            both(attn_round, "wait_final")
-            fattn_ref[...] = final_ref[0]
-            fw1_ref[...] = final_ref[1]
-            fw2_ref[...] = final_ref[2]
-            small.wait_z()
-
-
-def call_attn_back(ring, dh, tokens, memory, keep, n1, qt, k, v, e, linv, ot, dkept, attn, vec, gvec, extra):
+        for s in range(count):
+            hook((4 + s, 0))
+
+        if ring:
+
+            @pl.when(step == 3 + count)
+            def _():
+                for step_left in rest:
+                    step_left()
+                fqkv_ref[...] = heads_final[...]
+                fo_ref[...] = out_final[...]
+                fw1_ref[...] = ffn_final[0]
+                fw2_ref[...] = ffn_final[1]
+
+
+def call_attn_back(
+    ring, dh, tokens, memory, keep, n1, qt, k, v, e, ot, mixed_grad, dkept, attn, vec, extra
+):
     n, seg, d = tokens.shape
     slots = memory.shape[1]
     shapes = [((n, seg, d), F32), ((n, slots, d), F32)]
-    out_specs = [phase_spec((seg, d), n, n), phase_spec((slots, d), n, n)]
+    out_specs = [phase_spec((seg, d), 4, n), phase_spec((slots, d), 4, n)]
+
+    def pair_spec(shape, axis):
+        return pl.BlockSpec(shape, lambda i: tuple(jnp.minimum(i, 3) if j == axis else 0 for j in range(len(shape))))
+
     in_specs = [
-        phase_spec((seg + 128, d), 0, n), phase_spec((d, seg), 0, n), phase_spec((seg + 128, d), 0, n),
-        phase_spec((seg + 128, d), 0, n), phase_spec((4, LIVE, 256), 0, n), phase_spec((4, 4, 1, 256), 0, n),
-        phase_spec((d, seg), 0, n), phase_spec((seg, d), n, n), phase_spec((slots, d), n, n), phase_spec((1, 128), n, n),
-        phase_spec((slots, d), n, n), pl.BlockSpec((1, seg, d), lambda i: (lax.rem(i, n), 0, 0)),
-        full_spec(attn.shape), full_spec(vec.shape), full_spec(gvec.shape),
+        pair_spec((n, 128, seg), 1), pair_spec((n, 1, seg + 128, 128), 1), pair_spec((n, 1, seg + 128, 128), 1),
+        pair_spec((n, 1, LIVE, 256), 1), pair_spec((n, 128, seg), 1), pair_spec((n, 128, seg), 1),
+        phase_spec((seg, d), 4, n), phase_spec((slots, d), 4, n), phase_spec((1, 128), 4, n), phase_spec((slots, d), 4, n),
+        phase_spec((seg, d), 4, n),
+        full_spec(n1.shape), full_spec((3, d, d)), full_spec(vec.shape),
     ]
-    units = (4, 4, 2, 2, 32, d)
+    heads = (4, 2, 4, 2, 2, 48, 128)
     scratch = [
-        pltpu.VMEM((d, seg), F32), pltpu.VMEM((d, seg + 128), BF16), pltpu.VMEM((n, d, seg), BF16),
-        pltpu.VMEM((seg + 128, d), F32), pltpu.VMEM((seg + 128, d), F32), pltpu.VMEM((n, seg + 128, d), BF16),
-        pltpu.VMEM((n, seg + 128, d), BF16), pltpu.VMEM((4, 128, 256), BF16), pltpu.VMEM((4, 128, 256), BF16),
-        pltpu.VMEM((4, d, d), F32), pltpu.VMEM((1, d), F32),
+        pltpu.VMEM((n, d, seg), BF16), pltpu.VMEM((n, 4, seg + 128, 128), BF16), pltpu.VMEM((n, 4, seg + 128, 128), BF16),
+        pltpu.VMEM((seg + 128, 128), F32), pltpu.VMEM((seg + 128, 128), F32), pltpu.VMEM((4, 128, 256), BF16),
+        pltpu.VMEM((4, 128, 256), BF16),
     ]
     params = dict(vmem_limit_bytes=VMEM_LIMIT)
     if ring:
-        in_specs += [full_spec(extra[0].shape), ANY, ANY]
-        more = [((4, 32, d), F32)] * 3 + [((8, 128), F32)]
-        scratch += [pltpu.VMEM(units, BF16), pltpu.VMEM((3, 4, 32, d), F32)] + reduce_scratch(3, 32, d)
+        in_specs += [full_spec(extra[0].shape), full_spec(extra[1].shape), ANY, ANY, ANY]
+        more = [((4, 2, 48, 128), F32), ((2, 16, d), F32), ((4, 32, d), F32), ((4, 32, d), F32), ((8, 128), F32)]
+        scratch += [
+            pltpu.VMEM(heads, BF16), pltpu.VMEM((2, 4, 32, d), F32), pltpu.VMEM((2, 16, d), F32),
+            pltpu.VMEM((4, 2, 48, 128), F32),
+        ]
+        scratch += reduce_scratch(8, 32, d // 2) + reduce_scratch(1, 16, d) + reduce_scratch(4, 48, 128)
         scratch += [pltpu.VMEM((4, 2, 2, 8, 128), F32)] * 3 + [
             pltpu.VMEM((4, 2, 8, 128), F32), pltpu.VMEM((7, 8, 128), F32),
             pltpu.SemaphoreType.DMA((6,)), pltpu.SemaphoreType.DMA((6,)),
         ]
         params.update(collective_id=2, has_side_effects=True)
     else:
-        more = [(units, BF16), ((8, d), F32)]
+        more = [(heads, BF16)]
     return pl.pallas_call(
         functools.partial(attn_back_kernel, ring, n),
-        grid=(2 * n,),
+        grid=(4 + n,),
         out_shape=[jax.ShapeDtypeStruct(shape, kind) for shape, kind in shapes + more],
         in_specs=in_specs,
         out_specs=out_specs + [full_spec(shape) for shape, _ in more],
         scratch_shapes=scratch,
         compiler_params=pltpu.CompilerParams(**params),
         name="attn_back",
-    )(n1, qt, k, v, e, linv, ot, tokens, memory, keep, dkept, dh, attn, vec, gvec, *extra)
+    )(qt, k, v, e, ot, mixed_grad, tokens, memory, keep, dkept, dh, n1, attn, vec, *extra)
 
 
 def hand_out_kernel(
-    fattn_ref, fw1_ref, fw2_ref, fwr_ref, fgate_ref, small_ref,
+    fqkv_ref, fo_ref, fw1_ref, fw2_ref, fwr_ref, fgate_ref, small_ref, qkv_ref, in_ref, wqkv_ref, gain_ref,
     gqkv_ref, gout_ref, gin_ref, gffn_ref, gwqkv_ref, gwout_ref, ggate_ref, gb_ref, ggb_ref, ggain_ref,
 ):
-    gqkv_ref[...] = fattn_ref[0:3]
-    gout_ref[...] = fattn_ref[3]
+    for pair in range(4):
+        for core in range(2):
+            rows = slice(core * 16, core * 16 + 16)
+            for i in range(3):
+                gqkv_ref[i, rows, pair * 128:(pair + 1) * 128] = fqkv_ref[pair, core, i * 16:(i + 1) * 16, :]
+    for core in range(2):
+        gout_ref[core * 16:core * 16 + 16, :] = fo_ref[core]
     for j in range(4):
         gin_ref[:, j * 512:(j + 1) * 512] = fw1_ref[j]
     gffn_ref[...] = fw2_ref[...]
@@ -1146,15 +1304,22 @@
     gb_ref[...] = small_ref[0:1, :]
     rows = ggb_ref.shape[1]
     place = lax.rem(lax.axis_index("dp"), 4)
-    narrow = jnp.zeros((4, rows), F32)
+    narrow = jnp.zeros((1, rows), F32)
     for i in range(4):
-        narrow = narrow + small_ref[1:5, i * rows:(i + 1) * rows] * (place == i).astype(F32)
-    ggb_ref[...] = narrow[0:1]
-    ggain_ref[...] = narrow[1:4]
+        narrow = narrow + small_ref[1:2, i * rows:(i + 1) * rows] * (place == i).astype(F32)
+    ggb_ref[...] = narrow
+    sums = [
+        jnp.sum(jnp.sum(qkv_ref[...].astype(F32) * gqkv_ref[...], axis=0), axis=-1, keepdims=True),
+        jnp.sum(in_ref[...].astype(F32) * gin_ref[...], axis=-1, keepdims=True),
+        jnp.sum(jnp.sum(wqkv_ref[...].astype(F32) * gwqkv_ref[...], axis=0), axis=-1, keepdims=True),
+    ]
+    for i in range(3):
+        across = jnp.broadcast_to(sums[i], (rows, 128)).T[0:1, :]
+        ggain_ref[i:i + 1, :] = across / gain_ref[i:i + 1, :].astype(F32)
 
 
 def call_hand_out(*args):
-    rows, d = args[0].shape[1:]
+    rows, d = args[2].shape[1:]
     vmem = pl.BlockSpec(memory_space=pltpu.VMEM)
     shapes = [
         (3, rows, d), (rows, d), (rows, 4 * d), (4, rows, d), (3, rows, d), (rows, d), (4, rows // 2, d), (1, 128), (1, rows),
@@ -1163,7 +1328,7 @@
     return pl.pallas_call(
         hand_out_kernel,
         out_shape=[jax.ShapeDtypeStruct(shape, F32) for shape in shapes],
-        in_specs=[vmem] * 6,
+        in_specs=[vmem] * 11,
         out_specs=[vmem] * 10,
         name="hand_out",
     )(*args)
@@ -1193,7 +1358,7 @@
     return by_rows(0, 4), by_rows(4, 8), w2, by_rows(12, 16), packed[:, 16:18].reshape(2, d, d), vec, b1
 
 
-def plain_grads(rows, gattn, gw1, gw2, gwr, ggate, gb, gvec):
+def plain_grads(rows, attn_qkv, ffn_in, writer_qkv, gains, gattn, gw1, gw2, gwr, ggate, gb, ggb):
     d = gattn.shape[-1]
     n = d // rows
 
@@ -1205,13 +1370,18 @@
     )
     owned = lax.psum_scatter(packed.astype(F32), "dp", scatter_dimension=0, tiled=False)
     owned = lax.psum(owned.astype(BF16), "outer").astype(F32)
-    vectors = gvec[0:4].reshape(4, n, rows).transpose(1, 0, 2).reshape(n, 4 * rows)
-    small = jnp.concatenate([gb.reshape(n, 4 * rows), vectors], 1)
+    small = jnp.concatenate([gb.reshape(n, 4 * rows), ggb.reshape(n, rows)], 1)
     small = lax.psum(lax.psum_scatter(small, "dp", scatter_dimension=0, tiled=False), "outer")
+    gin = owned[4:8].transpose(1, 0, 2).reshape(rows, 4 * d)
+    ggains = jnp.stack(
+        [
+            jnp.sum(attn_qkv.astype(F32) * owned[0:3], (0, 2)), jnp.sum(ffn_in.astype(F32) * gin, 1),
+            jnp.sum(writer_qkv.astype(F32) * owned[12:15], (0, 2)),
+        ]
+    )
     return (
-        owned[0:3], owned[3], owned[4:8].transpose(1, 0, 2).reshape(rows, 4 * d), owned[8:12].reshape(4 * rows, d),
-        owned[12:15], owned[15], owned[16:18].reshape(2 * rows, d),
-        small[0:4 * rows], small[4 * rows:5 * rows], small[5 * rows:].reshape(3, rows),
+        owned[0:3], owned[3], gin, owned[8:12].reshape(4 * rows, d), owned[12:15], owned[15], owned[16:18].reshape(2 * rows, d),
+        small[0:4 * rows], small[4 * rows:], ggains / gains.astype(F32),
     )
 
 
@@ -1243,19 +1413,22 @@
     if ring:
         attn, w1, w2, wr = (array.reshape(4, d, d) for array in whole[:4])
         gate = whole[4].reshape(2, d, d)
-    new_memory, dkept, gvec, gb, gw1, gw2, dh, gwr, ggate = call_ffn_back(
-        ring, res, memory, memory_grad, docs, keep, wr, gate, vec, out_grad, h1, act, slope, w1, w2
+    new_memory, dkept, ggb, gb, gw1, gw2, gwo, dh, mixed_grad, gwr, ggate = call_ffn_back(
+        ring, res, memory, memory_grad, docs, keep, wr, gate, vec, out_grad, h1, act, slope, ot, linv, w1, w2, attn
     )
-    extra = (gb, gw1.reshape(4, 4, 2, 2, 32, d), gw2.reshape(4, 2, 2, 4, 32, d)) if ring else ()
+    extra = ()
+    if ring:
+        extra = (ggb, gb, gw1.reshape(4, 4, 2, 2, 32, d), gw2.reshape(4, 2, 2, 4, 32, d), gwo.reshape(4, 2, 2, 2, 16, d))
     grad_tokens, grad_memory, *rest = call_attn_back(
-        ring, dh, tokens, memory, keep, n1, qt, k, v, e, linv, ot, dkept, attn, vec, gvec, extra
+        ring, dh, tokens, memory, keep, n1, qt, k, v, e, ot, mixed_grad, dkept, attn, vec, extra
     )
     if ring:
-        fattn, fw1, fw2, small = rest
-        grads = call_hand_out(fattn, fw1, fw2, gwr, ggate, small)
+        grads = call_hand_out(*rest[:4], gwr, ggate, rest[4], attn_qkv, ffn_in, writer_qkv, gains)
     else:
-        gattn, gvec = rest
-        grads = plain_grads(rows, gattn.reshape(4, d, d), gw1, gw2, gwr, ggate, gb, gvec)
+        (heads,) = rest
+        gattn = heads.reshape(4, 2, 16, 3, 16, 128).transpose(3, 2, 1, 4, 0, 5).reshape(3, d, d)
+        gattn = jnp.concatenate([gattn, gwo[None]], 0)
+        grads = plain_grads(rows, attn_qkv, ffn_in, writer_qkv, gains, gattn, gw1, gw2, gwr, ggate, gb, ggb)
     gqkv, gout, gin, gffn, gwqkv, gwout, ggw, gb, ggb, ggains = grads
     return (
         out.reshape(micro, segs, seg, d), new_memory.reshape(micro, segs, slots, d),

time: 248 us -> 209 us (0.84)
  Pallas kernels: 240 us -> 201 us
    pallas_call x1, Pallas kernels: 79.2 us -> 57.4 us  [call_attn_back(): pl.pallas_call(functools.partial(attn_back_kernel, ring, n), grid=(4 + n,...]
    pallas_call x1, Pallas kernels: 93 us -> 80.6 us  [call_forward(): pl.pallas_call(functools.partial(forward_kernel, ring, n), grid=(2 * n,),...]
    pallas_call x1, Pallas kernels: 65 us -> 60.5 us  [call_ffn_back(): pl.pallas_call(functools.partial(ffn_back_kernel, ring, n), grid=(n + 1,)...]
where the time goes in v4:
time: 209 us
  Pallas kernels  201 us (96%)
  local copies, waits for them, and re-layouts  6.59 us (3%)
    pallas_call x1, Pallas kernels, call_forward(): pl.pallas_call(functools.partial(forward_kernel, ring, n), grid=(2 * n,),...  80.6 us
    pallas_call x1, Pallas kernels, call_ffn_back(): pl.pallas_call(functools.partial(ffn_back_kernel, ring, n), grid=(n + 1,)...  60.5 us
    pallas_call x1, Pallas kernels, call_attn_back(): pl.pallas_call(functools.partial(attn_back_kernel, ring, n), grid=(4 + n,...  57.4 us
    unnamed x12, local copies, waits for them, and re-layouts  5.94 us

profile of v4, /device:TPU:0, one launch (start us, length us, event | category | flops | bytes accessed | tf_op | source)
XLA Modules:
  0.0 208.9 jit_solution(16974381555784681957)
XLA Ops:
  0.6 0.7 convert_bitcast_fusion
  1.3 0.7 broadcast_in_dim.8.refs_3_.refs_4_.refs_8_
  2.0 80.6 %gather_forward.1 = (bf16[4,640,512]{2,1,0:T(8,128)(2,1)}, bf16[4,512,512]{2,1,0:T(8,128)(2,1)}, bf16[4,4,640,128]{3,2,1,0:T(8,128)(2,1)}, bf16[4,4,640,128]{3,2...) custom-call(bf16[4,512,512]{2,1,0:T(8,128)(2,1)} %bitcast.36, ...), custom_call_target="tpu_custom_call" | custom-call | tf_op jit(solution)/shard_map/gather_forward/pallas_call | solution.py:809
  82.5 60.5 %ffn_back.1 = (f32[4,64,512]{2,1,0:T(8,128)}, f32[4,64,512]{2,1,0:T(8,128)}, f32[1,512]{1,0:T(1,128)}, f32[4,1,512]{2,1,0:T(1,128)}, bf16[4,512,512]{2,1,0:T(8,1...) custom-call(f32[4,256,512]{2,1,0:T(8,128)} %get-tuple-element.61.ref, ...), custom_call_target="tpu_custom_call" | custom-call | tf_op jit(solution)/shard_map/ffn_back/pallas_call | solution.py:1069
  143.0 0.0 copy-start.1
  143.0 57.4 %attn_back.1 = (f32[4,512,512]{2,1,0:T(8,128)}, f32[4,64,512]{2,1,0:T(8,128)}, f32[4,2,48,128]{3,2,1,0:T(8,128)}, f32[2,16,512]{2,1,0:T(8,128)}, f32[4,32,512]{2...) custom-call(bf16[4,512,512]{2,1,0:T(8,128)(2,1)} %get-tuple-element.74.refs_0_, ...), custom_call_target="tpu_custom_call" | custom-call | tf_op jit(solution)/shard_map/attn_back/pallas_call | solution.py:1275
  200.4 0.0 copy-start.2
  200.4 2.5 %hand_out.1 = (f32[3,32,512]{2,1,0:T(8,128)}, f32[32,512]{1,0:T(8,128)}, f32[32,2048]{1,0:T(8,128)}, f32[4,32,512]{2,1,0:T(8,128)}, f32[3,32,512]{2,1,0:T(8,128)...) custom-call(f32[4,2,48,128]{3,2,1,0:T(8,128)} %get-tuple-element.89.f, ...), custom_call_target="tpu_custom_call" | custom-call | tf_op jit(solution)/shard_map/hand_out/pallas_call | solution.py:1328
  202.9 0.0 copy-done.1
  202.9 0.0 copy-start
  202.9 1.3 copy.38
  204.2 0.0 copy-done.2
  204.2 0.8 copy.39
  205.0 1.0 copy-done
  206.1 0.0 copy-start.3
  206.1 2.0 copy.40
  208.1 0.0 copy-done.3
  208.1 0.8 copy.41
Async XLA Ops:
  143.0 59.9 %copy-start.1 = (bf16[4,512,512]{2,1,0:T(8,128)(2,1)S(1)}, bf16[4,512,512]{2,1,0:T(8,128)(2,1)}, u32[]{:S(2)}) copy-start(bf16[4,512,512]{2,1,0:T(8,128)(2,1)} %get-tuple-element.60) | copy-start | bytes 6291460
  200.4 3.8 %copy-start.2 = (f32[4,64,512]{2,1,0:T(8,128)S(1)}, f32[4,64,512]{2,1,0:T(8,128)}, u32[]{:S(2)}) copy-start(f32[4,64,512]{2,1,0:T(8,128)} %get-tuple-element.73) | copy-start | bytes 1572868
  202.9 3.1 %copy-start = (f32[4,512,512]{2,1,0:T(8,128)S(1)}, f32[4,512,512]{2,1,0:T(8,128)}, u32[]{:S(2)}) copy-start(f32[4,512,512]{2,1,0:T(8,128)} %get-tuple-element.87) | copy-start | bytes 12582916
  206.1 2.0 copy-start.3

commit v5 on v4

--- a/solution.py
+++ b/solution.py
@@ -526,6 +526,8 @@
 HEADS_TIME, HEADS_TIMES = 8.0, (0.0, 1.7, 3.4, 5.1, 6.8)
 LAST_TIME = 2.0
 FFN_REDUCE_PACE = 4.5
+WRITER_SPANS = (8.0, 6.0, 8.0, 3.0)
+WRITER_PACE = 3.0
 
 
 def matrix(block):
@@ -549,7 +551,7 @@
     n1_ref, qt_ref, k_ref, v_ref, e_ref, linv_ref, ot_ref, h1_ref, out_ref, res_ref, act_ref, slope_ref, vec_ref = take(13)
     if ring:
         attn_ref, w1_ref, w2_ref, wr_ref, gate_ref = take(5)
-    bias_ref, pair_ref, vt_ref, hidden_ref, b1_ref, attn_v, w1_v, w2_v, wsem = take(9)
+    bias_ref, vt_ref, hidden_ref, b1_ref, attn_v, w1_v, w2_v, wsem = take(8)
     seg = tok_ref.shape[1]
     slots = mem_ref.shape[1]
     step = pl.program_id(0)
@@ -685,30 +687,43 @@
             k_ref[0, pair] = keys[:, pair * 128:(pair + 1) * 128]
             v_ref[0, pair] = v[:, pair * 128:(pair + 1) * 128]
         vt_ref[...] = v.T
-        pair_ref[...] = jnp.zeros_like(pair_ref)
         for s in range(count):
             hook((s, 0))
 
         def one_pair(pair, carry):
             lanes = pl.ds(pl.multiple_of(pair * 128, 128), 128)
             for block, (first, last_row) in enumerate(SPANS):
-                start = STARTS[block]
-                held = pair_ref.at[block]
+                start = STARTS[block] - first
                 columns = pl.ds(block * BLOCK, BLOCK)
-                diagonal_pair(held, qt_ref[0, lanes, columns])
-                scores = dot(k_ref[0, pair, first:last_row, :], held[...])
-                bias = bias_ref[start:start + last_row - first, :]
-                scores = scores + jnp.concatenate([bias, bias], 1)
-                largest = jnp.max(scores, axis=0, keepdims=True)
-                e = jnp.exp(scores - largest)
-                linv = 1.0 / jnp.sum(e, axis=0, keepdims=True)
-                e = e.astype(BF16)
-                e_ref[0, pair, start:start + last_row - first, :] = e
+                query = qt_ref[0, lanes, columns]
+                zero = jnp.zeros((64, BLOCK), BF16)
+                query = jnp.concatenate(
+                    [jnp.concatenate([query[0:64], zero], 1), jnp.concatenate([zero, query[64:128]], 1)], 0
+                )
+                scores, largest = [], None
+                for row in range(first, last_row, 128):
+                    bias = bias_ref[start + row:start + row + 128, :]
+                    part = dot(k_ref[0, pair, row:row + 128, :], query) + jnp.concatenate([bias, bias], 1)
+                    scores.append(part)
+                    part = jnp.max(part.reshape(16, 8, 256), axis=0)
+                    largest = part if largest is None else jnp.maximum(largest, part)
+                largest = jnp.max(largest, axis=0, keepdims=True)
+                es, total = [], None
+                for i, row in enumerate(range(first, last_row, 128)):
+                    e = jnp.exp(scores[i] - largest)
+                    part = jnp.sum(e.reshape(16, 8, 256), axis=0)
+                    total = part if total is None else total + part
+                    es.append(e.astype(BF16))
+                    e_ref[0, pair, start + row:start + row + 128, :] = es[-1]
+                linv = 1.0 / jnp.sum(total, axis=0, keepdims=True)
                 linv_ref[0, pair, block, :, :] = linv
-                mixed = dot(vt_ref[lanes, first:last_row], e) * linv
-                ot_ref[0, lanes, columns] = jnp.concatenate(
-                    [mixed[0:64, 0:128], mixed[64:128, 128:256]], 0
-                ).astype(BF16)
+                e = jnp.concatenate(es, 0)
+                values = vt_ref[lanes, first:last_row]
+                mixed = [
+                    dot(values[i * 64:(i + 1) * 64], e[:, i * 128:(i + 1) * 128]) * linv[:, i * 128:(i + 1) * 128]
+                    for i in range(2)
+                ]
+                ot_ref[0, lanes, columns] = jnp.concatenate(mixed, 0).astype(BF16)
             for s in range(count):
                 for i in range(4):
                     hook((s, 1 + i), pair == i)
@@ -788,8 +803,7 @@
     out_specs += [full_spec((8, d))]
     in_specs = [phase_spec((seg, d), 0, n), phase_spec((slots, d), 0, n), phase_spec((1, seg), 0, n), phase_spec((1, 128), 0, n)]
     scratch = [
-        pltpu.VMEM((LIVE, 128), F32), pltpu.VMEM((4, 128, 256), BF16), pltpu.VMEM((d, seg + 128), BF16),
-        pltpu.VMEM((n, seg, d), F32), pltpu.VMEM((4, 1, d), F32), pltpu.VMEM(unit_shapes[0], BF16),
+        pltpu.VMEM((LIVE, 128), F32), pltpu.VMEM((d, seg + 128), BF16), pltpu.VMEM((n, seg, d), F32), pltpu.VMEM((4, 1, d), F32), pltpu.VMEM(unit_shapes[0], BF16),
         pltpu.VMEM(unit_shapes[1], BF16), pltpu.VMEM(unit_shapes[2], BF16), pltpu.SemaphoreType.DMA((3,)),
     ]
     params = dict(vmem_limit_bytes=VMEM_LIMIT)
@@ -827,20 +841,20 @@
     slots = mem_ref.shape[1]
     gain = vec_ref[3:4, :]
 
-    def norm(i, carry):
-        rows = pl.ds(pl.multiple_of(i * half, half), half)
-        small = pl.ds(pl.multiple_of(i * slots, slots), slots)
+    biases = []
+    for i in range(n):
+        rows, small = slice(i * half, (i + 1) * half), slice(i * slots, (i + 1) * slots)
         hat, _ = norm_parts(res_ref[i])
         n3_ref[rows, :] = (hat * gain).astype(BF16)
         kept = mem_ref[i] * keep_ref[i][:, 0:1]
         kept_ref[small, :] = kept
         hat, _ = norm_parts(kept)
         ns_ref[small, :] = (hat * gain).astype(BF16)
-        tk_ref[rows, :] = dot(n3_ref[rows, :], wr_ref[1]).astype(BF16)
-        tv_ref[rows, :] = dot(n3_ref[rows, :], wr_ref[2]).astype(BF16)
-        return carry
-
-    lax.fori_loop(0, n, norm, 0)
+        docs = doc_ref[i].astype(F32)
+        bias = jnp.where(docs == jnp.max(docs), 0.0, -1e30)[:, docs.shape[1] - half:]
+        biases.append(jnp.broadcast_to(bias, (128, half)).T)
+    tk_ref[...] = dot(n3_ref[...], wr_ref[1]).astype(BF16)
+    tv_ref[...] = dot(n3_ref[...], wr_ref[2]).astype(BF16)
     sq_ref[...] = (dot(ns_ref[...], wr_ref[0]) * 0.125).astype(BF16)
     low_half = lax.broadcasted_iota(jnp.int32, (1, 128), 1) < 64
 
@@ -848,22 +862,16 @@
         zero = jnp.zeros_like(rows)
         return jnp.concatenate([jnp.where(low_half, rows, zero), jnp.where(low_half, zero, rows)], 0)
 
-    def read(i, carry):
-        rows = pl.ds(pl.multiple_of(i * half, half), half)
-        small = pl.ds(pl.multiple_of(i * slots, slots), slots)
-        docs = doc_ref[i].astype(F32)
-        bias = jnp.where(docs == jnp.max(docs), 0.0, -1e30)[:, docs.shape[1] - half:]
+    for i in range(n):
+        rows, small = slice(i * half, (i + 1) * half), slice(i * slots, (i + 1) * slots)
         for pair in range(4):
             lanes = slice(pair * 128, pair * 128 + 128)
-            scores = dot_nt(halves(sq_ref[small, lanes]), tk_ref[rows, lanes]) + bias
-            e = jnp.exp(scores - jnp.max(scores, axis=1, keepdims=True))
-            p = e * (1.0 / jnp.sum(e, axis=1, keepdims=True))
+            scores = dot_nt(tk_ref[rows, lanes], halves(sq_ref[small, lanes])) + biases[i]
+            e = jnp.exp(scores - jnp.max(scores, axis=0, keepdims=True))
+            p = e * (1.0 / jnp.sum(e, axis=0, keepdims=True))
             p_ref[i, pair] = p
-            mixed = dot(p.astype(BF16), tv_ref[rows, lanes])
+            mixed = dot_tn(p.astype(BF16), tv_ref[rows, lanes])
             wt_ref[small, lanes] = jnp.where(low_half, mixed[:slots], mixed[slots:]).astype(BF16)
-        return carry
-
-    lax.fori_loop(0, n, read, 0)
 
     def put(ref, index, value):
         ref[index] = value.astype(BF16).reshape(ref.shape[1:])
@@ -891,22 +899,19 @@
     put(gwr_ref, 3, dot_tn(wt_ref[...], dw_low))
     dw_ref[...] = dot_nt(dw_low, wr_ref[3]).astype(BF16)
 
-    def read_back(i, carry):
-        rows = pl.ds(pl.multiple_of(i * half, half), half)
-        small = pl.ds(pl.multiple_of(i * slots, slots), slots)
+    for i in range(n):
+        rows, small = slice(i * half, (i + 1) * half), slice(i * slots, (i + 1) * slots)
         for pair in range(4):
             lanes = slice(pair * 128, pair * 128 + 128)
             p = p_ref[i, pair]
             grads = halves(dw_ref[small, lanes])
-            dp = dot_nt(grads, tv_ref[rows, lanes])
-            ds = (p * (dp - jnp.sum(dp * p, axis=1, keepdims=True))).astype(BF16)
-            dq = dot(ds, tk_ref[rows, lanes]) * 0.125
+            keys, values = tk_ref[rows, lanes], tv_ref[rows, lanes]
+            dp = dot_nt(values, grads)
+            ds = (p * (dp - jnp.sum(dp * p, axis=0, keepdims=True))).astype(BF16)
+            dq = dot_tn(ds, keys) * 0.125
             dsq_ref[small, lanes] = jnp.where(low_half, dq[:slots], dq[slots:]).astype(BF16)
-            tk_ref[rows, lanes] = dot_tn(ds, halves(sq_ref[small, lanes])).astype(BF16)
-            tv_ref[rows, lanes] = dot_tn(p.astype(BF16), grads).astype(BF16)
-        return carry
-
-    lax.fori_loop(0, n, read_back, 0)
+            tk_ref[rows, lanes] = dot(ds, halves(sq_ref[small, lanes])).astype(BF16)
+            tv_ref[rows, lanes] = dot(p.astype(BF16), grads).astype(BF16)
     read_done()
     put(gwr_ref, 0, dot_tn(ns_ref[...], dsq_ref[...]))
     put(gwr_ref, 1, dot_tn(n3_ref[...], tk_ref[...]))
@@ -915,14 +920,11 @@
     hat, rstd = norm_parts(kept_ref[...])
     dkept_ref[...] += norm_back(grad, hat, rstd, gain).reshape(n, slots, d)
 
-    def back(i, carry):
-        rows = pl.ds(pl.multiple_of(i * half, half), half)
+    for i in range(n):
+        rows = slice(i * half, (i + 1) * half)
         grad = dot_nt(tk_ref[rows, :], wr_ref[1]) + dot_nt(tv_ref[rows, :], wr_ref[2])
         hat, rstd = norm_parts(res_ref[i])
         dres_ref[i] = norm_back(grad, hat, rstd, gain)
-        return carry
-
-    lax.fori_loop(0, n, back, 0)
 
 
 def ffn_back_kernel(ring, count, *refs):
@@ -954,9 +956,9 @@
         ]
         gate_round = reduce_round(place, unit_last(ggate_ref), slim_scratch, 0, fgate_ref)
         jobs = [
-            (job(gate_round, REDUCE_STEPS)[2:], 0.0, REDUCE_SPANS[2:]),
-            (job(writer_rounds[0], REDUCE_STEPS)[1:], 1.5, REDUCE_SPANS[1:]),
-            (job(writer_rounds[1], REDUCE_STEPS)[1:], 4.5, REDUCE_SPANS[1:]),
+            (job(gate_round, REDUCE_STEPS)[2:], 0.0, WRITER_SPANS[1:]),
+            (job(writer_rounds[0], REDUCE_STEPS)[1:], 1.5, WRITER_SPANS),
+            (job(writer_rounds[1], REDUCE_STEPS)[1:], 1.5 + WRITER_PACE, WRITER_SPANS),
         ]
         places = [((1 + s, i), FFN_BACK_TIME * (s + i / 4)) for s in range(count) for i in range(4)]
         found, rest = plan(jobs, places)
@@ -1055,7 +1057,7 @@
     stored = [((4, d, d), BF16), ((4, d, d), BF16), ((d, d), BF16)]
     scratch = [
         pltpu.VMEM((rows, d), BF16), pltpu.VMEM((small, d), BF16), pltpu.VMEM((small, d), F32), pltpu.VMEM((small, d), BF16),
-        pltpu.VMEM((rows, d), BF16), pltpu.VMEM((rows, d), BF16), pltpu.VMEM((n, 4, 2 * slots, half), F32),
+        pltpu.VMEM((rows, d), BF16), pltpu.VMEM((rows, d), BF16), pltpu.VMEM((n, 4, half, 2 * slots), F32),
         pltpu.VMEM((small, d), BF16), pltpu.VMEM((small, d), BF16), pltpu.VMEM((small, d), BF16), pltpu.VMEM((small, d), BF16),
         pltpu.VMEM((n, half, d), F32), pltpu.VMEM((4, d, d), F32), pltpu.VMEM((4, d, d), F32), pltpu.VMEM((d, d), F32),
         pltpu.VMEM((4, d, d), BF16), pltpu.VMEM((4, d, d), BF16), pltpu.VMEM((d, d), BF16), pltpu.SemaphoreType.DMA((3,)),

time: 209 us -> 200 us (0.957)
  Pallas kernels: 201 us -> 191 us
    pallas_call x1, Pallas kernels: 60.5 us -> 54.3 us  [call_ffn_back(): pl.pallas_call(functools.partial(ffn_back_kernel, ring, n), grid=(n + 1,)...]
    pallas_call x1, Pallas kernels: 80.6 us -> 77.8 us  [call_forward(): pl.pallas_call(functools.partial(forward_kernel, ring, n), grid=(2 * n,),...]
where the time goes in v5:
time: 200 us; the launch traced here: 199 us
  Pallas kernels  191 us (96%)
  local copies, waits for them, and re-layouts  6.59 us (3%)
    pallas_call x1, Pallas kernels, call_forward(): pl.pallas_call(functools.partial(forward_kernel, ring, n), grid=(2 * n,),...  77.8 us
    pallas_call x1, Pallas kernels, call_attn_back(): pl.pallas_call(functools.partial(attn_back_kernel, ring, n), grid=(4 + n,...  56.9 us
    pallas_call x1, Pallas kernels, call_ffn_back(): pl.pallas_call(functools.partial(ffn_back_kernel, ring, n), grid=(n + 1,)...  54.3 us
    unnamed x12, local copies, waits for them, and re-layouts  5.94 us

profile of v5, /device:TPU:0, one launch (start us, length us, event | category | flops | bytes accessed | tf_op | source)
XLA Modules:
  0.0 199.4 jit_solution(17723854929086582438)
XLA Ops:
  0.6 0.7 convert_bitcast_fusion
  1.3 0.7 broadcast_in_dim.8.refs_3_.refs_4_.refs_8_
  2.0 77.8 %gather_forward.1 = (bf16[4,640,512]{2,1,0:T(8,128)(2,1)}, bf16[4,512,512]{2,1,0:T(8,128)(2,1)}, bf16[4,4,640,128]{3,2,1,0:T(8,128)(2,1)}, bf16[4,4,640,128]{3,2...) custom-call(bf16[4,512,512]{2,1,0:T(8,128)(2,1)} %bitcast.36, ...), custom_call_target="tpu_custom_call" | custom-call | tf_op jit(solution)/shard_map/gather_forward/pallas_call | solution.py:823
  79.8 54.3 %ffn_back.1 = (f32[4,64,512]{2,1,0:T(8,128)}, f32[4,64,512]{2,1,0:T(8,128)}, f32[1,512]{1,0:T(1,128)}, f32[4,1,512]{2,1,0:T(1,128)}, bf16[4,512,512]{2,1,0:T(8,1...) custom-call(f32[4,256,512]{2,1,0:T(8,128)} %get-tuple-element.61.ref, ...), custom_call_target="tpu_custom_call" | custom-call | tf_op jit(solution)/shard_map/ffn_back/pallas_call | solution.py:1071
  134.1 0.0 copy-start.1
  134.1 56.9 %attn_back.1 = (f32[4,512,512]{2,1,0:T(8,128)}, f32[4,64,512]{2,1,0:T(8,128)}, f32[4,2,48,128]{3,2,1,0:T(8,128)}, f32[2,16,512]{2,1,0:T(8,128)}, f32[4,32,512]{2...) custom-call(bf16[4,512,512]{2,1,0:T(8,128)(2,1)} %get-tuple-element.74.refs_0_, ...), custom_call_target="tpu_custom_call" | custom-call | tf_op jit(solution)/shard_map/attn_back/pallas_call | solution.py:1277
  191.0 0.0 copy-start.2
  191.0 2.5 %hand_out.1 = (f32[3,32,512]{2,1,0:T(8,128)}, f32[32,512]{1,0:T(8,128)}, f32[32,2048]{1,0:T(8,128)}, f32[4,32,512]{2,1,0:T(8,128)}, f32[3,32,512]{2,1,0:T(8,128)...) custom-call(f32[4,2,48,128]{3,2,1,0:T(8,128)} %get-tuple-element.89.f, ...), custom_call_target="tpu_custom_call" | custom-call | tf_op jit(solution)/shard_map/hand_out/pallas_call | solution.py:1330
  193.5 0.0 copy-done.1
  193.5 0.0 copy-start
  193.5 1.3 copy.38
  194.8 0.0 copy-done.2
  194.8 0.8 copy.39
  195.6 1.0 copy-done
  196.6 0.0 copy-start.3
  196.6 2.0 %copy.40 = f32[4,1,512,512]{3,2,1,0:T(8,128)} copy(f32[4,1,512,512]{3,2,1,0:T(8,128)S(1)} %bitcast.41) | data formatting | bytes 8388608
  198.6 0.0 copy-done.3
  198.6 0.8 copy.41
Async XLA Ops:
  134.1 59.4 %copy-start.1 = (bf16[4,512,512]{2,1,0:T(8,128)(2,1)S(1)}, bf16[4,512,512]{2,1,0:T(8,128)(2,1)}, u32[]{:S(2)}) copy-start(bf16[4,512,512]{2,1,0:T(8,128)(2,1)} %get-tuple-element.60) | copy-start | bytes 6291460
  191.0 3.8 %copy-start.2 = (f32[4,64,512]{2,1,0:T(8,128)S(1)}, f32[4,64,512]{2,1,0:T(8,128)}, u32[]{:S(2)}) copy-start(f32[4,64,512]{2,1,0:T(8,128)} %get-tuple-element.73) | copy-start | bytes 1572868
  193.5 3.1 %copy-start = (f32[4,512,512]{2,1,0:T(8,128)S(1)}, f32[4,512,512]{2,1,0:T(8,128)}, u32[]{:S(2)}) copy-start(f32[4,512,512]{2,1,0:T(8,128)} %get-tuple-element.87) | copy-start | bytes 12582916
  196.6 2.0 %copy-start.3 = (f32[4,64,512]{2,1,0:T(8,128)S(1)}, f32[4,64,512]{2,1,0:T(8,128)}, u32[]{:S(2)}) copy-start(f32[4,64,512]{2,1,0:T(8,128)} %get-tuple-element.88) | copy-start | bytes 1572868

commit v6 on v5

--- a/solution.py
+++ b/solution.py
@@ -1096,7 +1096,7 @@
 
     qt_ref, k_ref, v_ref, e_ref, ot_ref, dot_ref = take(6)
     tok_ref, mem_ref, keep_ref, dkept_ref, dh_ref = take(5)
-    n1_ref, attn_ref, vec_ref = take(3)
+    n1_from, attn_from, vec_ref = take(3)
     if ring:
         ggb_ref, gb_ref, gw1_ref, gw2_ref, gwo_ref = take(5)
     gtok_ref, gmem_ref = take(2)
@@ -1104,7 +1104,9 @@
         fqkv_ref, fo_ref, fw1_ref, fw2_ref, fsmall_ref = take(5)
     else:
         (gqkv_ref,) = take(1)
-    dqt_ref, dkl_ref, dvl_ref, dk_ref, dv_ref, qp_ref, dp_ref = take(7)
+    dqt_ref, dkl_ref, dvl_ref, dk_ref, dv_ref, qp_ref, dp_ref, n1_ref, attn_ref, wsem = take(10)
+    load_n1 = lambda: pltpu.make_async_copy(n1_from, n1_ref, wsem.at[0])
+    load_attn = lambda: pltpu.make_async_copy(attn_from.at[0:3], attn_ref, wsem.at[1])
     step = pl.program_id(0)
     seg = tok_ref.shape[1]
     d = tok_ref.shape[2]
@@ -1143,6 +1145,8 @@
     def _():
         @pl.when(step == 0)
         def _():
+            load_n1().start()
+            load_attn().start()
             if ring:
                 place.greet()
                 for m in range(4):
@@ -1188,6 +1192,12 @@
         lax.fori_loop(0, count, one_segment, 0)
         for p in range(4):
             hook((p, 4))
+
+        @pl.when(step == 0)
+        def _():
+            load_n1().wait()
+            load_attn().wait()
+
         gq = dot(dqt_ref[0, features, :], n1_ref[0, 128:, :])
         gkv = dot_tn(n1_ref[0], jnp.concatenate([dkl_ref[0, step], dvl_ref[0, step]], 1))
         for s in range(1, count):
@@ -1250,13 +1260,13 @@
         pair_spec((n, 1, LIVE, 256), 1), pair_spec((n, 128, seg), 1), pair_spec((n, 128, seg), 1),
         phase_spec((seg, d), 4, n), phase_spec((slots, d), 4, n), phase_spec((1, 128), 4, n), phase_spec((slots, d), 4, n),
         phase_spec((seg, d), 4, n),
-        full_spec(n1.shape), full_spec((3, d, d)), full_spec(vec.shape),
+        ANY, ANY, full_spec(vec.shape),
     ]
     heads = (4, 2, 4, 2, 2, 48, 128)
     scratch = [
         pltpu.VMEM((n, d, seg), BF16), pltpu.VMEM((n, 4, seg + 128, 128), BF16), pltpu.VMEM((n, 4, seg + 128, 128), BF16),
         pltpu.VMEM((seg + 128, 128), F32), pltpu.VMEM((seg + 128, 128), F32), pltpu.VMEM((4, 128, 256), BF16),
-        pltpu.VMEM((4, 128, 256), BF16),
+        pltpu.VMEM((4, 128, 256), BF16), pltpu.VMEM(n1.shape, BF16), pltpu.VMEM((3, d, d), BF16), pltpu.SemaphoreType.DMA((2,)),
     ]
     params = dict(vmem_limit_bytes=VMEM_LIMIT)
     if ring:

time: 200 us -> 198 us (0.990)
  no operation moved by 1% of the time
where the time goes in v6:
time: 198 us
  Pallas kernels  190 us (96%)
  local copies, waits for them, and re-layouts  6.59 us (3%)
    pallas_call x1, Pallas kernels, call_forward(): pl.pallas_call(functools.partial(forward_kernel, ring, n), grid=(2 * n,),...  77.8 us
    pallas_call x1, Pallas kernels, call_attn_back(): pl.pallas_call(functools.partial(attn_back_kernel, ring, n), grid=(4 + n,...  55.6 us
    pallas_call x1, Pallas kernels, call_ffn_back(): pl.pallas_call(functools.partial(ffn_back_kernel, ring, n), grid=(n + 1,)...  54.3 us
    unnamed x12, local copies, waits for them, and re-layouts  5.94 us

profile of v6, /device:TPU:0, one launch (start us, length us, event | category | flops | bytes accessed | tf_op | source)
XLA Modules:
  0.0 198.1 jit_solution(15515260137898746036)
XLA Ops:
  0.6 0.7 convert_bitcast_fusion
  1.3 0.7 broadcast_in_dim.8.refs_3_.refs_4_.refs_8_
  2.0 77.8 %gather_forward.1 = (bf16[4,640,512]{2,1,0:T(8,128)(2,1)}, bf16[4,512,512]{2,1,0:T(8,128)(2,1)}, bf16[4,4,640,128]{3,2,1,0:T(8,128)(2,1)}, bf16[4,4,640,128]{3,2...) custom-call(bf16[4,512,512]{2,1,0:T(8,128)(2,1)} %bitcast.36, ...), custom_call_target="tpu_custom_call" | custom-call | tf_op jit(solution)/shard_map/gather_forward/pallas_call | solution.py:823
  79.8 54.3 %ffn_back.1 = (f32[4,64,512]{2,1,0:T(8,128)}, f32[4,64,512]{2,1,0:T(8,128)}, f32[1,512]{1,0:T(1,128)}, f32[4,1,512]{2,1,0:T(1,128)}, bf16[4,512,512]{2,1,0:T(8,1...) custom-call(f32[4,256,512]{2,1,0:T(8,128)} %get-tuple-element.61.ref, ...), custom_call_target="tpu_custom_call" | custom-call | tf_op jit(solution)/shard_map/ffn_back/pallas_call | solution.py:1071
  134.1 0.0 copy-start.1
  134.1 55.6 %attn_back.1 = (f32[4,512,512]{2,1,0:T(8,128)}, f32[4,64,512]{2,1,0:T(8,128)}, f32[4,2,48,128]{3,2,1,0:T(8,128)}, f32[2,16,512]{2,1,0:T(8,128)}, f32[4,32,512]{2...) custom-call(bf16[4,512,512]{2,1,0:T(8,128)(2,1)} %get-tuple-element.74.refs_0_, ...), custom_call_target="tpu_custom_call" | custom-call | tf_op jit(solution)/shard_map/attn_back/pallas_call | solution.py:1287
  189.7 0.0 copy-start.2
  189.7 2.5 %hand_out.1 = (f32[3,32,512]{2,1,0:T(8,128)}, f32[32,512]{1,0:T(8,128)}, f32[32,2048]{1,0:T(8,128)}, f32[4,32,512]{2,1,0:T(8,128)}, f32[3,32,512]{2,1,0:T(8,128)...) custom-call(f32[4,2,48,128]{3,2,1,0:T(8,128)} %get-tuple-element.89.f, ...), custom_call_target="tpu_custom_call" | custom-call | tf_op jit(solution)/shard_map/hand_out/pallas_call | solution.py:1340
  192.2 0.0 copy-done.1
  192.2 0.0 copy-start
  192.2 1.3 copy.38
  193.5 0.0 copy-done.2
  193.5 0.8 copy.39
  194.3 1.0 copy-done
  195.3 0.0 copy-start.3
  195.3 2.0 %copy.40 = f32[4,1,512,512]{3,2,1,0:T(8,128)} copy(f32[4,1,512,512]{3,2,1,0:T(8,128)S(1)} %bitcast.41) | data formatting | bytes 8388608
  197.3 0.0 copy-done.3
  197.3 0.8 copy.41
Async XLA Ops:
  134.1 58.1 %copy-start.1 = (bf16[4,512,512]{2,1,0:T(8,128)(2,1)S(1)}, bf16[4,512,512]{2,1,0:T(8,128)(2,1)}, u32[]{:S(2)}) copy-start(bf16[4,512,512]{2,1,0:T(8,128)(2,1)} %get-tuple-element.60) | copy-start | bytes 6291460
  189.7 3.8 %copy-start.2 = (f32[4,64,512]{2,1,0:T(8,128)S(1)}, f32[4,64,512]{2,1,0:T(8,128)}, u32[]{:S(2)}) copy-start(f32[4,64,512]{2,1,0:T(8,128)} %get-tuple-element.73) | copy-start | bytes 1572868
  192.2 3.1 %copy-start = (f32[4,512,512]{2,1,0:T(8,128)S(1)}, f32[4,512,512]{2,1,0:T(8,128)}, u32[]{:S(2)}) copy-start(f32[4,512,512]{2,1,0:T(8,128)} %get-tuple-element.87) | copy-start | bytes 12582916
  195.3 2.0 %copy-start.3 = (f32[4,64,512]{2,1,0:T(8,128)S(1)}, f32[4,64,512]{2,1,0:T(8,128)}, u32[]{:S(2)}) copy-start(f32[4,64,512]{2,1,0:T(8,128)} %get-tuple-element.88) | copy-start | bytes 1572868
